TPU v7x, 256 devices: a whole 4x4x8 slice. The times are simulated.
256 devices in a mesh: seq: 32 (over z, x), outer: 8 (over y, core).
Axes of the slice: x: 4, y: 4, z: 8, core: 2. Of those that a mesh axis runs over, the one named last changes fastest.
Arguments:
- queries: bfloat16 [65536, 1024], P(('outer', 'seq')), may hold values from -48 to 48
- keys: bfloat16 [65536, 1024], P(('outer', 'seq')), may hold values from -6 to 6
- values: bfloat16 [65536, 1024], P(('outer', 'seq')), may hold values from -6 to 6
- out_grad: bfloat16 [65536, 1024], P(('outer', 'seq')), may hold values from -6 to 6
- near_offsets: int32 [16], replicated, may hold values from 0 to 63
- far_offsets: int32 [16], replicated, may hold values from 0 to 255
Outputs:
- attn_out: bfloat16 [65536, 1024], P(('outer', 'seq'))
- query_grad: bfloat16 [65536, 1024], P(('outer', 'seq'))
- key_grad: bfloat16 [65536, 1024], P(('outer', 'seq'))
- value_grad: bfloat16 [65536, 1024], P(('outer', 'seq'))
All inputs are finite; a program needn't handle non-finite values.
Results may differ from a plain program's by a relative error of at most 0.0065.
Values may be sent and summed in bfloat16 or wider, within the bound.
No kernel may reach another device: no remote copies, remote signals or barrier semaphores. Data moves between devices by JAX's collectives and lax.ppermute only.
A program may use at most 64 MiB of HBM per device.

v0:
```python
import jax
import jax.numpy as jnp
from jax import lax
from jax.sharding import PartitionSpec as P

NEAR_RATE = 64
FAR_RATE = 256
HEAD_BLOCK = 4


def split_heads(matrix, head_count):
    return matrix.reshape(matrix.shape[0], head_count, matrix.shape[1] // head_count)


def select_rows(source, dilation, offsets):
    shaped = source.reshape((source.shape[0] // dilation, dilation) + source.shape[1:])
    choose_index = jnp.broadcast_to(
        offsets[None, None, :, None], (shaped.shape[0], 1, shaped.shape[2], shaped.shape[3])
    )
    return jnp.take_along_axis(shaped, choose_index, axis=1)[:, 0]


def spread_rows(source, dilation, offsets, filler):
    chosen = (
        jnp.arange(dilation, dtype=jnp.int32)[None, :, None, None] == offsets[None, None, :, None]
    )
    spread = jnp.where(chosen, source[:, None], filler)
    return spread.reshape((source.shape[0] * dilation,) + source.shape[1:])


def select_stat(source, dilation, offsets):
    return select_rows(source[:, :, None], dilation, offsets)[:, :, 0]


def attend_level(query_piece, key_piece, value_piece, query_pos, key_pos, logit_scale_factor):
    score_matrix = (
        jnp.einsum("ywf,zwf->wyz", query_piece, key_piece, preferred_element_type=jnp.float32)
        * logit_scale_factor
    )
    allowed = key_pos[None, None, :] <= query_pos[None, :, None]
    level_top = jnp.max(jnp.where(allowed, score_matrix, -jnp.inf), axis=2)
    attention_weight = jnp.where(allowed, jnp.exp(score_matrix - level_top[:, :, None]), 0.0)
    level_total = jnp.sum(attention_weight, axis=2)
    level_running_sum = jnp.einsum(
        "cue,eco->uco",
        attention_weight.astype(jnp.bfloat16),
        value_piece,
        preferred_element_type=jnp.float32,
    )
    return (level_top.T, level_total.T, level_running_sum)


def pair_terms(
    query_piece,
    key_piece,
    value_piece,
    gradient_piece,
    lse_part,
    delta_part,
    query_pos,
    key_pos,
    logit_scale_factor,
):
    score_matrix = (
        jnp.einsum("ywf,zwf->wyz", query_piece, key_piece, preferred_element_type=jnp.float32)
        * logit_scale_factor
    )
    allowed = key_pos[None, None, :] <= query_pos[None, :, None]
    attention_weight = jnp.where(allowed, jnp.exp(score_matrix - lse_part.T[:, :, None]), 0.0)
    weight_gradient = jnp.einsum(
        "ywf,zwf->wyz", gradient_piece, value_piece, preferred_element_type=jnp.float32
    )
    dscores = attention_weight * (weight_gradient - delta_part.T[:, :, None])
    return (attention_weight.astype(jnp.bfloat16), dscores.astype(jnp.bfloat16))


def query_side(addend_list, key_piece, logit_scale_factor):
    return (
        jnp.einsum("cue,eco->uco", addend_list[1], key_piece, preferred_element_type=jnp.float32)
        * logit_scale_factor
    )


def key_side(addend_list, query_piece, gradient_piece, logit_scale_factor):
    key_addend = (
        jnp.einsum("lap,alv->plv", addend_list[1], query_piece, preferred_element_type=jnp.float32)
        * logit_scale_factor
    )
    value_addend = jnp.einsum(
        "lap,alv->plv", addend_list[0], gradient_piece, preferred_element_type=jnp.float32
    )
    return (key_addend, value_addend)


def all_grads(
    query_piece,
    key_piece,
    value_piece,
    gradient_piece,
    lse_part,
    delta_part,
    query_pos,
    key_pos,
    logit_scale_factor,
):
    addend_list = pair_terms(
        query_piece,
        key_piece,
        value_piece,
        gradient_piece,
        lse_part,
        delta_part,
        query_pos,
        key_pos,
        logit_scale_factor,
    )
    key_addend, value_addend = key_side(
        addend_list, query_piece, gradient_piece, logit_scale_factor
    )
    return (query_side(addend_list, key_piece, logit_scale_factor), key_addend, value_addend)


def by_head_groups(level_fn, arrays, head_count):

    def one_group(group):
        pieces = tuple(
            (
                lax.dynamic_slice_in_dim(tensor, group * HEAD_BLOCK, HEAD_BLOCK, 1)
                for tensor in arrays
            )
        )
        return level_fn(pieces)

    results = lax.map(one_group, jnp.arange(head_count // HEAD_BLOCK, dtype=jnp.int32))
    return tuple(
        (
            jnp.moveaxis(tensor, 0, 1).reshape((tensor.shape[1], head_count) + tensor.shape[3:])
            for tensor in results
        )
    )


def spread_level(pieces, dilation, offsets):
    level_top = spread_rows(pieces[0][:, :, None], dilation, offsets, -jnp.inf)[:, :, 0]
    level_total = spread_rows(pieces[1][:, :, None], dilation, offsets, 0.0)[:, :, 0]
    level_running_sum = spread_rows(pieces[2], dilation, offsets, 0.0)
    return (level_top, level_total, level_running_sum)


def merge_levels(levels):
    overall = jnp.maximum(jnp.maximum(levels[0][0], levels[1][0]), levels[2][0])
    denom = jnp.exp(levels[0][0] - overall) * levels[0][1]
    denom = denom + jnp.exp(levels[1][0] - overall) * levels[1][1]
    denom = denom + jnp.exp(levels[2][0] - overall) * levels[2][1]
    lse = overall + jnp.log(denom)
    out_full = jnp.exp(levels[0][0] - lse)[:, :, None] * levels[0][2]
    out_full = out_full + jnp.exp(levels[1][0] - lse)[:, :, None] * levels[1][2]
    out_full = out_full + jnp.exp(levels[2][0] - lse)[:, :, None] * levels[2][2]
    return (lse, out_full)


def on_device(queries, keys, values, out_grad, near_offsets, far_offsets):
    head_count = near_offsets.shape[0]
    query_h = split_heads(queries, head_count)
    key_h = split_heads(keys, head_count)
    value_h = split_heads(values, head_count)
    grad_h = split_heads(out_grad, head_count)
    row_count = query_h.shape[0]
    logit_scale_factor = query_h.shape[2] ** (-0.5)
    seq_count = lax.axis_size("seq")
    outer_count = lax.axis_size("outer")
    seq_at = lax.axis_index("seq")
    outer_at = lax.axis_index("outer")
    near_rows = row_count // NEAR_RATE
    far_rows = row_count // FAR_RATE
    positions = jnp.arange(row_count, dtype=jnp.int32)
    near_qpos = seq_at * near_rows + jnp.arange(near_rows, dtype=jnp.int32)
    near_kpos = jnp.arange(seq_count * near_rows, dtype=jnp.int32)
    far_qpos = (outer_at * seq_count + seq_at) * far_rows + jnp.arange(far_rows, dtype=jnp.int32)
    key_slot = jnp.arange(seq_count * outer_count * far_rows, dtype=jnp.int32)
    key_block = key_slot // far_rows
    far_kpos = (
        key_block % outer_count * seq_count + key_block // outer_count
    ) * far_rows + key_slot % far_rows
    near_query = select_rows(query_h, NEAR_RATE, near_offsets)
    near_key = select_rows(key_h, NEAR_RATE, near_offsets)
    near_value = select_rows(value_h, NEAR_RATE, near_offsets)
    near_grad = select_rows(grad_h, NEAR_RATE, near_offsets)
    far_query = select_rows(query_h, FAR_RATE, far_offsets)
    far_key = select_rows(key_h, FAR_RATE, far_offsets)
    far_value = select_rows(value_h, FAR_RATE, far_offsets)
    far_grad = select_rows(grad_h, FAR_RATE, far_offsets)
    far_key_o, far_value_o = (
        lax.all_gather(far_key, "outer", axis=0, tiled=True),
        lax.all_gather(far_value, "outer", axis=0, tiled=True),
    )
    near_key_all, near_value_all, far_key_all, far_value_all = (
        lax.all_gather(near_key, "seq", axis=0, tiled=True),
        lax.all_gather(near_value, "seq", axis=0, tiled=True),
        lax.all_gather(far_key_o, "seq", axis=0, tiled=True),
        lax.all_gather(far_value_o, "seq", axis=0, tiled=True),
    )

    def local_forward(pieces):
        return attend_level(
            pieces[0], pieces[1], pieces[2], positions, positions, logit_scale_factor
        )

    local_parts = by_head_groups(local_forward, (query_h, key_h, value_h), head_count)
    near_parts = attend_level(
        near_query, near_key_all, near_value_all, near_qpos, near_kpos, logit_scale_factor
    )
    near_parts = spread_level(near_parts, NEAR_RATE, near_offsets)
    far_parts = attend_level(
        far_query, far_key_all, far_value_all, far_qpos, far_kpos, logit_scale_factor
    )
    far_parts = spread_level(far_parts, FAR_RATE, far_offsets)
    lse, out_full = merge_levels((local_parts, near_parts, far_parts))
    attn_out = out_full.reshape(row_count, -1).astype(jnp.bfloat16)
    delta = jnp.sum(grad_h.astype(jnp.float32) * out_full, axis=2)

    def local_backward(pieces):
        return all_grads(
            pieces[0],
            pieces[1],
            pieces[2],
            pieces[3],
            pieces[4],
            pieces[5],
            positions,
            positions,
            logit_scale_factor,
        )

    local_dq, local_dk, local_dv = by_head_groups(
        local_backward, (query_h, key_h, value_h, grad_h, lse, delta), head_count
    )
    near_lse = select_stat(lse, NEAR_RATE, near_offsets)
    near_delta = select_stat(delta, NEAR_RATE, near_offsets)
    far_lse = select_stat(lse, FAR_RATE, far_offsets)
    far_delta = select_stat(delta, FAR_RATE, far_offsets)
    near_dq, near_dk_all, near_dv_all = all_grads(
        near_query,
        near_key_all,
        near_value_all,
        near_grad,
        near_lse,
        near_delta,
        near_qpos,
        near_kpos,
        logit_scale_factor,
    )
    far_dq, far_dk_all, far_dv_all = all_grads(
        far_query,
        far_key_all,
        far_value_all,
        far_grad,
        far_lse,
        far_delta,
        far_qpos,
        far_kpos,
        logit_scale_factor,
    )
    near_dk, near_dv, far_dk_s, far_dv_s = (
        lax.psum_scatter(
            near_dk_all.astype(jnp.bfloat16), "seq", scatter_dimension=0, tiled=True
        ).astype(jnp.float32),
        lax.psum_scatter(
            near_dv_all.astype(jnp.bfloat16), "seq", scatter_dimension=0, tiled=True
        ).astype(jnp.float32),
        lax.psum_scatter(
            far_dk_all.astype(jnp.bfloat16), "seq", scatter_dimension=0, tiled=True
        ).astype(jnp.float32),
        lax.psum_scatter(
            far_dv_all.astype(jnp.bfloat16), "seq", scatter_dimension=0, tiled=True
        ).astype(jnp.float32),
    )
    far_dk, far_dv = (
        lax.psum_scatter(
            far_dk_s.astype(jnp.bfloat16), "outer", scatter_dimension=0, tiled=True
        ).astype(jnp.float32),
        lax.psum_scatter(
            far_dv_s.astype(jnp.bfloat16), "outer", scatter_dimension=0, tiled=True
        ).astype(jnp.float32),
    )
    query_grad = (
        local_dq
        + spread_rows(near_dq, NEAR_RATE, near_offsets, 0.0)
        + spread_rows(far_dq, FAR_RATE, far_offsets, 0.0)
    )
    key_grad = (
        local_dk
        + spread_rows(near_dk, NEAR_RATE, near_offsets, 0.0)
        + spread_rows(far_dk, FAR_RATE, far_offsets, 0.0)
    )
    value_grad = (
        local_dv
        + spread_rows(near_dv, NEAR_RATE, near_offsets, 0.0)
        + spread_rows(far_dv, FAR_RATE, far_offsets, 0.0)
    )
    return (
        attn_out,
        query_grad.reshape(row_count, -1).astype(jnp.bfloat16),
        key_grad.reshape(row_count, -1).astype(jnp.bfloat16),
        value_grad.reshape(row_count, -1).astype(jnp.bfloat16),
    )


def solution(mesh):
    return jax.shard_map(
        on_device,
        mesh=mesh,
        in_specs=(
            P(("outer", "seq"), None),
            P(("outer", "seq"), None),
            P(("outer", "seq"), None),
            P(("outer", "seq"), None),
            P(),
            P(),
        ),
        out_specs=(
            P(("outer", "seq"), None),
            P(("outer", "seq"), None),
            P(("outer", "seq"), None),
            P(("outer", "seq"), None),
        ),
        check_vma=False,
    )
```

profile of v0, /device:TPU:1, one launch (start us, length us, event | category | flops | bytes accessed | tf_op | source)
XLA Modules:
  0.0 1625.1 jit_solution(4342423857930765031)
XLA Ops:
  11.3 1.3 iota_compare_fusion.3
  12.6 2.0 copy.69
  14.7 2.5 reshape_reshape.24
  21.5 1.8 reshape_reshape.30
  24.5 19.3 %while.32 = (s32[]{:T(128)}, f32[4,256,4]{1,2,0:T(4,128)S(1)}, f32[4,256,4]{1,2,0:T(4,128)S(1)}, f32[4,256,4,64]{1,3,2,0:T(8,128)}, s32[4]{0:T(128)S(1)}, /*inde...) while((s32[]{:T(128)}, f32[4,256,4]{1,2,0:T(4,128)S(1)}, ...), condition=%wide.region_3.4_spmd.clone.clone, body=%wide.region_0.3_spmd.clone.clone.sunk | while | flops 69531648 | bytes 4097219 | solution.py:134
  25.8 1.3 select_reduce_fusion.4
  27.4 1.9 fusion.183
  30.6 1.3 select_reduce_fusion.4
  32.2 2.0 fusion.183
  35.5 1.3 select_reduce_fusion.4
  37.0 2.0 fusion.183
  40.3 1.3 select_reduce_fusion.4
  41.9 1.9 fusion.183
  47.0 2.9 copy.86
  49.9 29.9 %gather_fusion.5 = bf16[1024]{0:T(1024)(128)(2,1)S(1)} fusion(bf16[256,16,64]{2,1,0:T(8,128)(2,1)} %bitcast.327, s32[1024]{0:T(1024)S(1)} %reshape.1078), kind=kCustom, calls=%fused_computation.8.clone | custom fusion | bytes 16384 | tf_op jit(solution)/shard_map/jit(take_along_axis)/gather | solution.py:20
  80.0 2.9 copy.80
  82.9 29.9 %gather_fusion.3 = bf16[1024]{0:T(1024)(128)(2,1)S(1)} fusion(bf16[256,16,64]{2,1,0:T(8,128)(2,1)} %bitcast.328, s32[1024]{0:T(1024)S(1)} %reshape.1078), kind=kCustom, calls=%fused_computation.7.clone | custom fusion | bytes 16384 | tf_op jit(solution)/shard_map/jit(take_along_axis)/gather | solution.py:20
  112.9 2.9 copy.78
  115.8 29.9 %gather_fusion.2 = bf16[1024]{0:T(1024)(128)(2,1)S(1)} fusion(bf16[256,16,64]{2,1,0:T(8,128)(2,1)} %bitcast.329, s32[1024]{0:T(1024)S(1)} %reshape.1078), kind=kCustom, calls=%fused_computation.1.clone | custom fusion | bytes 16384 | tf_op jit(solution)/shard_map/jit(take_along_axis)/gather | solution.py:20
  145.9 2.9 copy.94
  148.8 29.9 %gather_fusion.10 = bf16[1024]{0:T(1024)(128)(2,1)S(1)} fusion(bf16[256,16,64]{2,1,0:T(8,128)(2,1)} %bitcast.326, s32[1024]{0:T(1024)S(1)} %reshape.1078), kind=kCustom, calls=%fused_computation.9.clone | custom fusion | bytes 16384 | tf_op jit(solution)/shard_map/jit(take_along_axis)/gather | solution.py:20
  178.9 15.9 all-gather.1
  194.8 12.8 all-gather.4
  207.6 41.1 %all-gather.5 = bf16[256,1,16,64]{3,2,1,0:T(8,128)(2,1)S(1)} all-gather(bf16[8,1,16,64]{3,2,1,0:T(8,128)(2,1)S(1)} %all-gather.4), channel_id=7, replica_groups=mesh['seq'=32,'outer'=8] {'seq'}, dimensions={0}, use_global_device_ids=true | all-gather | bytes 540672 | tf_op jit(solution)/shard_map/all_gather | solution.py:201
  248.7 37.0 %all-gather.2 = bf16[256,1,16,64]{3,2,1,0:T(8,128)(2,1)S(1)} all-gather(bf16[8,1,16,64]{3,2,1,0:T(8,128)(2,1)S(1)} %all-gather.1), channel_id=4, replica_groups=mesh['seq'=32,'outer'=8] {'seq'}, dimensions={0}, use_global_device_ids=true | all-gather | bytes 540672 | tf_op jit(solution)/shard_map/all_gather | solution.py:200
  288.6 1.3 multiply_reduce_fusion.1
  289.8 1.3 multiply_reduce_fusion.2
  291.1 124.4 %gather_fusion = bf16[4096]{0:T(1024)(128)(2,1)S(1)} fusion(bf16[4,64,16,64]{3,2,1,0:T(8,128)(2,1)} %reshape_reshape.24, s32[4096]{0:T(1024)S(1)} %reshape.1065), kind=kCustom, calls=%fused_computation.clone | custom fusion | bytes 81920 | tf_op jit(solution)/shard_map/jit(take_along_axis)/gather | solution.py:20
  415.6 45.0 %gather_fusion.1 = bf16[4096]{0:T(1024)(128)(2,1)S(1)} fusion(bf16[4,64,16,64]{3,2,1,0:T(8,128)(2,1)S(1)} %reshape_reshape.25, s32[4096]{0:T(1024)S(1)} %reshape.1065), kind=kCustom, calls=%fused_computation.4.clone | custom fusion | bytes 81920 | tf_op jit(solution)/shard_map/jit(take_along_axis)/gather | solution.py:20
  460.7 45.0 %gather_fusion.4 = bf16[4096]{0:T(1024)(128)(2,1)S(1)} fusion(bf16[4,64,16,64]{3,2,1,0:T(8,128)(2,1)S(1)} %reshape_reshape.28, s32[4096]{0:T(1024)S(1)} %reshape.1065), kind=kCustom, calls=%fused_computation.5.clone | custom fusion | bytes 81920 | tf_op jit(solution)/shard_map/jit(take_along_axis)/gather | solution.py:20
  505.8 45.0 %gather_fusion.7 = bf16[4096]{0:T(1024)(128)(2,1)S(1)} fusion(bf16[4,64,16,64]{3,2,1,0:T(8,128)(2,1)S(1)} %reshape_reshape.30, s32[4096]{0:T(1024)S(1)} %reshape.1065), kind=kCustom, calls=%fused_computation.6.clone | custom fusion | bytes 81920 | tf_op jit(solution)/shard_map/jit(take_along_axis)/gather | solution.py:20
  551.6 34.9 %all-gather = bf16[128,1,16,64]{3,2,1,0:T(8,128)(2,1)S(1)} all-gather(bf16[4,1,16,64]{3,2,1,0:T(8,128)(2,1)S(1)} %get-tuple-element.265), channel_id=2, replica_groups=mesh['seq'=32,'outer'=8] {'seq'}, dimensions={0}, use_global_device_ids=true | all-gather | bytes 270336 | tf_op jit(solution)/shard_map/all_gather | solution.py:198
  588.7 36.4 %all-gather.3 = bf16[128,1,16,64]{3,2,1,0:T(8,128)(2,1)S(1)} all-gather(bf16[4,1,16,64]{3,2,1,0:T(8,128)(2,1)S(1)} %get-tuple-element.266), channel_id=5, replica_groups=mesh['seq'=32,'outer'=8] {'seq'}, dimensions={0}, use_global_device_ids=true | all-gather | bytes 270336 | tf_op jit(solution)/shard_map/all_gather | solution.py:199
  627.1 1.2 broadcast_in_dim.426
  628.4 2.1 broadcast_in_dim.433
  631.3 2.2 fusion.65
  635.1 2.3 fusion.47
  637.5 1.5 fusion.46
  644.9 2.2 copy.99
  650.5 30.6 %while.31 = (s32[]{:T(128)}, f32[4,256,4,64]{1,3,2,0:T(8,128)}, f32[4,256,4,64]{1,3,2,0:T(8,128)}, f32[4,256,4,64]{1,3,2,0:T(8,128)}, s32[4]{0:T(128)S(1)}, /*in...) while((s32[]{:T(128)}, f32[4,256,4,64]{1,3,2,0:T(8,128)}, ...), condition=%wide.region_10.13_spmd.clone, body=%wide.region_9.12_spmd.clone.sunk | while | flops 169803776 | bytes 6580459 | solution.py:134
  651.8 1.3 fusion.175
  653.1 1.3 fusion.176
  656.2 1.9 fusion.177
  659.4 1.3 fusion.175
  660.8 1.3 fusion.176
  663.9 1.9 fusion.177
  667.1 1.3 fusion.175
  668.4 1.3 fusion.176
  671.5 1.9 fusion.177
  674.7 1.3 fusion.175
  676.1 1.3 fusion.176
  679.2 1.9 fusion.177
  681.3 209.7 %reduce-scatter.15.cloned.1.call-done = bf16[8,16,64]{2,1,0:T(8,128)(2,1)} async-done(((bf16[256,16,64]{2,1,0:T(8,128)(2,1)}), bf16[8,16,64]{2,1,0:T(8,128)(2,1)}) %reduce-scatter.15.cloned.1.call-update) | async-done | bytes 16400 | tf_op jit(solution)/shard_map/reduce_scatter | solution.py:274
  891.3 1.7 multiply_reduce_fusion
  893.1 214.4 %reduce-scatter.9.cloned.1.call-done = bf16[8,16,64]{2,1,0:T(8,128)(2,1)} async-done(((bf16[256,16,64]{2,1,0:T(8,128)(2,1)}), bf16[8,16,64]{2,1,0:T(8,128)(2,1)}) %reduce-scatter.9.cloned.1.call-update) | async-done | bytes 16400 | tf_op jit(solution)/shard_map/reduce_scatter | solution.py:271
  1107.6 2.1 broadcast_in_dim.427
  1111.2 2.1 broadcast_in_dim.445
  1113.4 209.3 %reduce-scatter.7.cloned.1.call-done = bf16[4,16,64]{2,1,0:T(8,128)(2,1)} async-done(((bf16[128,16,64]{2,1,0:T(8,128)(2,1)}), bf16[4,16,64]{2,1,0:T(8,128)(2,1)}) %reduce-scatter.7.cloned.1.call-update) | async-done | bytes 8208 | tf_op jit(solution)/shard_map/reduce_scatter | solution.py:265
  1324.8 2.1 broadcast_in_dim.456
  1326.9 212.0 %reduce-scatter.13.cloned.1.call-done = bf16[4,16,64]{2,1,0:T(8,128)(2,1)} async-done(((bf16[128,16,64]{2,1,0:T(8,128)(2,1)}), bf16[4,16,64]{2,1,0:T(8,128)(2,1)}) %reduce-scatter.13.cloned.1.call-update) | async-done | bytes 8208 | tf_op jit(solution)/shard_map/reduce_scatter | solution.py:268
  1541.2 2.1 broadcast_in_dim.461
  1543.3 32.2 %reduce-scatter.17.cloned.1.call-done = bf16[1,16,64]{2,1,0:T(8,128)(2,1)} async-done(((bf16[8,16,64]{2,1,0:T(8,128)(2,1)}), bf16[1,16,64]{2,1,0:T(8,128)(2,1)}) %reduce-scatter.17.cloned.1.call-update) | async-done | bytes 2064 | tf_op jit(solution)/shard_map/reduce_scatter | solution.py:282
  1576.2 33.3 %reduce-scatter.11.cloned.1.call-done = bf16[1,16,64]{2,1,0:T(8,128)(2,1)} async-done(((bf16[8,16,64]{2,1,0:T(8,128)(2,1)}), bf16[1,16,64]{2,1,0:T(8,128)(2,1)}) %reduce-scatter.11.cloned.1.call-update) | async-done | bytes 2064 | tf_op jit(solution)/shard_map/reduce_scatter | solution.py:279
  1610.3 3.6 fusion.60
  (281 shorter events, 57.7 us)
Async XLA Ops:
  7.2 10.0 copy-start.4
  7.2 883.9 %reduce-scatter.15.cloned.1.call-start = ((), (), s32[]{:S(2)}) async-start(), calls=%async_computation.10 | async-start | bytes 1081344 | tf_op jit(solution)/shard_map/reduce_scatter | solution.py:274
  7.9 542.9 %copy-start.52 = (s32[16]{0:T(128)}, s32[16]{0:T(128)S(1)}, u32[]{:S(2)}) copy-start(s32[16]{0:T(128)S(1)} %broadcast_add_fusion.1) | copy-start | bytes 196
  8.6 542.2 %copy-start.54 = (pred[16]{0:T(512)(128)(4,1)}, pred[16]{0:T(512)(128)(4,1)S(1)}, u32[]{:S(2)}) copy-start(pred[16]{0:T(512)(128)(4,1)S(1)} %broadcast_compare_fusion.1) | copy-start | bytes 52
  11.3 35.1 %copy-start.42 = (pred[64,16]{0,1:T(8,128)(4,1)}, pred[64,16]{0,1:T(8,128)(4,1)S(1)}, u32[]{:S(2)}) copy-start(pred[64,16]{0,1:T(8,128)(4,1)S(1)} %iota_compare_fusion.4) | copy-start | bytes 3076
  14.7 4.2 copy-start.5
  18.9 1.7 copy-start.6
  24.5 22.0 %copy-start.39 = (s32[16]{0:T(128)S(1)}, s32[16]{0:T(128)}, u32[]{:S(2)}) copy-start(s32[16]{0:T(128)} %param.23) | copy-start | bytes 196
  24.5 22.2 %copy-start.48 = (s32[16]{0:T(128)S(1)}, s32[16]{0:T(128)}, u32[]{:S(2)}) copy-start(s32[16]{0:T(128)} %param.22) | copy-start | bytes 196
  43.8 2.6 copy-start.21
  43.8 3.1 copy-start.19
  46.3 241.1 %copy-start.58 = (pred[256]{0:T(512)(128)(4,1)}, pred[256]{0:T(512)(128)(4,1)S(1)}, u32[]{:S(2)}) copy-start(pred[256]{0:T(512)(128)(4,1)S(1)} %fusion.135) | copy-start | bytes 772
  46.4 540.6 %copy-start.56 = (pred[4,128]{1,0:T(4,128)(4,1)}, pred[4,128]{1,0:T(4,128)(4,1)S(1)}, u32[]{:S(2)}) copy-start(pred[4,128]{1,0:T(4,128)(4,1)S(1)} %iota_compare_fusion.5) | copy-start | bytes 1540
  46.6 584.7 %copy-start.25 = (pred[256,16]{0,1:T(8,128)(4,1)}, pred[256,16]{0,1:T(8,128)(4,1)S(1)}, u32[]{:S(2)}) copy-start(pred[256,16]{0,1:T(8,128)(4,1)S(1)} %broadcast_in_dim.407) | copy-start | bytes 12292
  178.9 110.9 %copy-start.29 = (f32[16,64]{1,0:T(8,128)}, f32[16,64]{1,0:T(8,128)S(1)}, u32[]{:S(2)}) copy-start(f32[16,64]{1,0:T(8,128)S(1)} %get-tuple-element.263) | copy-start | bytes 12292
  178.9 110.9 %copy-start.31 = (f32[16,64]{1,0:T(8,128)}, f32[16,64]{1,0:T(8,128)S(1)}, u32[]{:S(2)}) copy-start(f32[16,64]{1,0:T(8,128)S(1)} %get-tuple-element.260) | copy-start | bytes 12292
  285.7 1.0 copy-start.2
  287.9 127.6 %copy-start.45 = (f32[16]{0:T(128)}, f32[16]{0:T(128)S(1)}, u32[]{:S(2)}) copy-start(f32[16]{0:T(128)S(1)} %select_reduce_fusion.1) | copy-start | bytes 196
  505.8 82.5 %copy-start.43 = (pred[64,16]{0,1:T(8,128)(4,1)S(1)}, pred[64,16]{0,1:T(8,128)(4,1)}, u32[]{:S(2)}) copy-start(pred[64,16]{0,1:T(8,128)(4,1)} %copy-done.42) | copy-start | bytes 3076
  551.5 36.8 %copy-start.23 = (bf16[4,16,64]{2,1,0:T(8,128)(2,1)}, bf16[4,16,64]{2,1,0:T(8,128)(2,1)S(1)}, u32[]{:S(2)}) copy-start(bf16[4,16,64]{2,1,0:T(8,128)(2,1)S(1)} %get-tuple-element.267) | copy-start | bytes 24580
  551.5 75.3 %copy-start.32 = (f32[256,16]{0,1:T(8,128)S(1)}, f32[256,16]{0,1:T(8,128)}, u32[]{:S(2)}) copy-start(f32[256,16]{0,1:T(8,128)} %reshape.898) | copy-start | bytes 49156
  551.5 75.3 %copy-start.33 = (f32[256,16]{0,1:T(8,128)S(1)}, f32[256,16]{0,1:T(8,128)}, u32[]{:S(2)}) copy-start(f32[256,16]{0,1:T(8,128)} %reshape.896) | copy-start | bytes 49156
  551.5 75.3 %copy-start.40 = (s32[16]{0:T(128)S(1)}, s32[16]{0:T(128)}, u32[]{:S(2)}) copy-start(s32[16]{0:T(128)} %param.23) | copy-start | bytes 196
  551.5 75.3 %copy-start.46 = (f32[16]{0:T(128)S(1)}, f32[16]{0:T(128)}, u32[]{:S(2)}) copy-start(f32[16]{0:T(128)} %copy-done.45) | copy-start | bytes 196
  551.5 75.3 %copy-start.50 = (f32[16]{0:T(128)S(1)}, f32[16]{0:T(128)}, u32[]{:S(2)}) copy-start(f32[16]{0:T(128)} %get-tuple-element.250) | copy-start | bytes 196
  625.6 1.4 copy-start.11
  626.9 4.3 copy-start.13
  627.0 4.2 copy-start.15
  627.1 4.2 copy-start.17
  628.3 2.2 copy-start.34
  628.3 2.2 copy-start.35
  628.3 3.0 copy-start
  628.3 3.0 copy-start.27
  628.4 3.0 copy-start.37
  630.5 3.7 copy-start.8
  630.5 3.7 copy-start.10
  633.5 4.0 copy-start.30
  635.0 4.1 copy-start.9
  635.0 4.1 copy-start.49
  635.0 4.1 copy-start.53
  635.0 4.1 copy-start.55
  635.0 4.2 copy-start.20
  635.0 4.3 copy-start.22
  635.0 4.5 copy-start.41
  635.1 4.5 copy-start.44
  635.1 4.5 copy-start.47
  635.1 4.5 copy-start.51
  637.4 470.0 %reduce-scatter.9.cloned.1.call-start = ((), (), s32[]{:S(2)}) async-start(), calls=%async_computation.7 | async-start | bytes 1081344 | tf_op jit(solution)/shard_map/reduce_scatter | solution.py:271
  639.1 683.6 %reduce-scatter.7.cloned.1.call-start = ((), (), s32[]{:S(2)}) async-start(), calls=%async_computation.6 | async-start | bytes 540672 | tf_op jit(solution)/shard_map/reduce_scatter | solution.py:265
  639.8 2.3 copy-start.12
  639.8 2.3 copy-start.36
  639.8 2.3 copy-start.57
  639.8 2.5 copy-start.24
  643.8 895.2 %reduce-scatter.13.cloned.1.call-start = ((), (), s32[]{:S(2)}) async-start(), calls=%async_computation.9 | async-start | bytes 540672 | tf_op jit(solution)/shard_map/reduce_scatter | solution.py:268
  644.9 5.6 copy-start.1
  647.1 928.4 %reduce-scatter.17.cloned.1.call-start = ((), (), s32[]{:S(2)}) async-start(), calls=%async_computation.11 | async-start | bytes 36864 | tf_op jit(solution)/shard_map/reduce_scatter | solution.py:282
  650.5 457.0 %copy-start.28 = (f32[16,64]{1,0:T(8,128)S(1)}, f32[16,64]{1,0:T(8,128)}, u32[]{:S(2)}) copy-start(f32[16,64]{1,0:T(8,128)} %multiply_reduce_fusion.2) | copy-start | bytes 12292
  891.1 718.5 %reduce-scatter.11.cloned.1.call-start = ((), (), s32[]{:S(2)}) async-start(), calls=%async_computation.8 | async-start | bytes 36864 | tf_op jit(solution)/shard_map/reduce_scatter | solution.py:279
  1541.1 69.2 %copy-start.3 = (f32[4,256,4,64]{1,3,2,0:T(8,128)S(1)}, f32[4,256,4,64]{1,3,2,0:T(8,128)}, u32[]{:S(2)}) copy-start(f32[4,256,4,64]{1,3,2,0:T(8,128)} %get-tuple-element.126) | copy-start | bytes 3145732
  1541.1 69.2 %copy-start.14 = (f32[256,16]{0,1:T(8,128)S(1)}, f32[256,16]{0,1:T(8,128)}, u32[]{:S(2)}) copy-start(f32[256,16]{0,1:T(8,128)} %copy-done.13) | copy-start | bytes 49156
  1541.1 69.2 %copy-start.16 = (f32[256,16]{0,1:T(8,128)S(1)}, f32[256,16]{0,1:T(8,128)}, u32[]{:S(2)}) copy-start(f32[256,16]{0,1:T(8,128)} %copy-done.15) | copy-start | bytes 49156
  1541.2 69.2 %copy-start.18 = (f32[256,16]{0,1:T(8,128)S(1)}, f32[256,16]{0,1:T(8,128)}, u32[]{:S(2)}) copy-start(f32[256,16]{0,1:T(8,128)} %copy-done.17) | copy-start | bytes 49156
  1541.2 69.2 %copy-start.26 = (pred[256,16]{0,1:T(8,128)(4,1)S(1)}, pred[256,16]{0,1:T(8,128)(4,1)}, u32[]{:S(2)}) copy-start(pred[256,16]{0,1:T(8,128)(4,1)} %copy-done.25) | copy-start | bytes 12292
  1541.2 69.2 %copy-start.38 = (pred[256,16]{0,1:T(8,128)(4,1)S(1)}, pred[256,16]{0,1:T(8,128)(4,1)}, u32[]{:S(2)}) copy-start(pred[256,16]{0,1:T(8,128)(4,1)} %iota_compare_fusion.3) | copy-start | bytes 12292
  (1 other events, 0.7 us)
Sparse Core Ops, SparseCore 0:
  637.5 253.4 reduce-scatter.14
  894.9 212.5 reduce-scatter.8
  1111.2 211.3 reduce-scatter.6
  1327.3 211.5 reduce-scatter.12
  1541.3 34.1 reduce-scatter.16
  1578.0 31.5 reduce-scatter.10
where the time goes:
time: 1640 us; the launch traced here: 1630 us
  waiting for transfers between devices  911 us (56%)
  local copies, waits for them, and re-layouts  448 us (27%)
  blocking collectives  178 us (11%)
  matrix products  41.4 us (3%)
  other arithmetic  25 us (2%)
    gather x25, local copies, waits for them, and re-layouts, select_rows(): return jnp.take_along_axis(shaped, choose_index, axis=1)[:, 0]  383 us
    reduce_scatter x1, waiting for transfers between devices, on_device(): lax.psum_scatter(far_dk_all.astype(jnp.bfloat16), 'seq', scatter_dimensio...  214 us
    reduce_scatter x1, waiting for transfers between devices, on_device(): lax.psum_scatter(near_dv_all.astype(jnp.bfloat16), 'seq', scatter_dimensi...  212 us
    reduce_scatter x1, waiting for transfers between devices, on_device(): lax.psum_scatter(far_dv_all.astype(jnp.bfloat16), 'seq', scatter_dimensio...  210 us
    reduce_scatter x1, waiting for transfers between devices, on_device(): lax.psum_scatter(near_dk_all.astype(jnp.bfloat16), 'seq', scatter_dimensi...  209 us
    all_gather x1, blocking collectives, on_device(): lax.all_gather(far_value_o, 'seq', axis=0, tiled=True)  41.1 us
    all_gather x1, blocking collectives, on_device(): lax.all_gather(far_key_o, 'seq', axis=0, tiled=True)  37 us
    all_gather x1, blocking collectives, on_device(): lax.all_gather(near_value, 'seq', axis=0, tiled=True)  36.4 us
  transfers between devices with their start and end apart: 6, of which 6 were waited for; matrix products, arithmetic and copies ran while one was open for 4% of the time, Pallas kernels for 0%

commit v1 on v0

v1 whole, which is shorter than its diff:
```python
import functools

import jax
import jax.numpy as jnp
from jax import lax
from jax.experimental import pallas as pl
from jax.experimental.pallas import tpu as pltpu
from jax.sharding import PartitionSpec as P

HEADS = 16
FEAT = 64
ROWS = 256
WIDTH = 1024
NEAR_RATE = 64
FAR_RATE = 256
SEQ = 32
OUTER = 8
SLOTS = 8
FAR_SLOT = 4
STAT_SLOT = 5
GROUP = 4
GROUPS = HEADS // GROUP
GLANES = GROUP * FEAT
GSLOTS = GROUP * SLOTS
SCALE = FEAT**-0.5
LOW = -1e30
F32 = jnp.float32
BF16 = jnp.bfloat16
VMEM_BYTES = 60 * 1024 * 1024


def iota(shape, axis):
    return lax.broadcasted_iota(jnp.int32, shape, axis)


def dot_nn(a, b):
    return lax.dot_general(a, b, (((1,), (0,)), ((), ())), preferred_element_type=F32)


def dot_nt(a, b):
    return lax.dot_general(a, b, (((1,), (1,)), ((), ())), preferred_element_type=F32)


def dot_tn(a, b):
    return lax.dot_general(a, b, (((0,), (0,)), ((), ())), preferred_element_type=F32)


def parts_of(value):
    high = value.astype(BF16).astype(F32)
    rest = value - high
    middle = rest.astype(BF16).astype(F32)
    return high, middle, rest - middle


def part_lanes(lse, d, at):
    out = jnp.zeros((lse.shape[0], at.shape[1]), F32)
    for index, part in enumerate(parts_of(lse) + parts_of(d)):
        out = jnp.where(at == index, part, out)
    return out


def read_parts(lanes, at):
    lse = jnp.sum(jnp.where((at >= 0) & (at < 3), lanes, 0.0), axis=1, keepdims=True)
    d = jnp.sum(jnp.where((at >= 3) & (at < 6), lanes, 0.0), axis=1, keepdims=True)
    return lse, d


def pack_stats(lse, d):
    rows = lse.shape[0]
    row, lane = iota((rows, 128), 0), iota((rows, 128), 1)
    at = jnp.where(lane // 8 == row % SLOTS, lane % 8, -1)
    spread = part_lanes(lse, d, at).reshape(rows // SLOTS, SLOTS, 128)
    total = jnp.sum(spread, axis=1, keepdims=True)
    return jnp.broadcast_to(total, spread.shape).reshape(rows, 128)


def unpack_stats(block):
    groups = block.shape[0]
    lanes = jnp.broadcast_to(block[:, STAT_SLOT : STAT_SLOT + 1, :], (groups, SLOTS, 128))
    lanes = lanes.reshape(groups * SLOTS, 128)
    row, lane = iota(lanes.shape, 0), iota(lanes.shape, 1)
    return read_parts(lanes, jnp.where(lane // 8 == row % SLOTS, lane % 8, -1))


def swap_halves(x):
    return pltpu.roll(x, FEAT, 1)


def slot_rows(near_ref, far_ref, first):
    index = iota((GSLOTS, 1), 0)
    slot = index % SLOTS
    near = jnp.zeros((GSLOTS, 1), jnp.int32)
    far = jnp.zeros((GSLOTS, 1), jnp.int32)
    for h in range(GROUP):
        here = index // SLOTS == h
        near = jnp.where(here, near_ref[first + h], near)
        far = jnp.where(here, far_ref[first + h], far)
    row = jnp.where(slot < FAR_SLOT, near + NEAR_RATE * slot, jnp.where(slot == FAR_SLOT, far, -1))
    repeat = (slot == FAR_SLOT) & (far % NEAR_RATE == near)
    return row, repeat, slot


def head_mask():
    return iota((GSLOTS, GLANES), 1) // FEAT == iota((GSLOTS, GLANES), 0) // SLOTS


def softmax_terms(scores, allowed, weight_grads):
    masked = jnp.where(allowed, scores, LOW)
    top = jnp.max(masked, axis=1, keepdims=True)
    weights = jnp.where(allowed, jnp.exp(masked - top), 0.0)
    total = jnp.sum(weights, axis=1, keepdims=True)
    return top, total, jnp.sum(weights * weight_grads, axis=1, keepdims=True)


def merge_terms(lse, d, top, total, grad_total):
    overall = jnp.maximum(lse, top)
    old, new = jnp.exp(lse - overall), jnp.exp(top - overall)
    mass = old + new * total
    return overall + jnp.log(mass), (old * d + new * grad_total) / mass


def select_kernel(near_ref, far_ref, q_ref, k_ref, v_ref, g_ref, pay_ref, qs_ref, gs_ref, s_ref, gv_ref):
    row, _, slot = slot_rows(near_ref, far_ref, pl.program_id(0) * GROUP)
    pick = jnp.where(iota((GSLOTS, ROWS), 1) == row, 1.0, 0.0).astype(BF16)
    mask = head_mask()

    def selected(ref):
        return jnp.where(mask, dot_nn(pick, ref[...]), 0.0)

    def folded(x):
        x = x[:, :128] + x[:, 128:]
        return x + swap_halves(x)

    qs, ks, vs, gs = selected(q_ref), selected(k_ref), selected(v_ref), selected(g_ref)
    qb, gb = qs.astype(BF16), gs.astype(BF16)
    qs_ref[0] = qb
    gs_ref[0] = gb
    allowed = iota((GSLOTS, ROWS), 1) <= row
    scores = jnp.where(allowed, dot_nt(qb, k_ref[...]) * SCALE, LOW)
    grads = dot_nt(gb, v_ref[...])
    s_ref[0] = scores
    gv_ref[0] = grads
    top, total, grad_total = softmax_terms(scores, allowed, grads)
    used = slot <= FAR_SLOT
    total = jnp.where(used, total, 1.0)
    lse = jnp.where(used, top + jnp.log(total), 0.0)
    stats = pack_stats(lse, jnp.where(used, grad_total / total, 0.0))
    low_half = iota((GSLOTS, 128), 1) < FEAT
    qk = jnp.where(low_half, folded(qs), folded(ks))
    vg = jnp.where(low_half, folded(vs), folded(gs))
    qk = jnp.where(slot == STAT_SLOT, stats, qk)
    block = jnp.concatenate(
        [qk.reshape(GROUP, SLOTS, 128), vg.reshape(GROUP, SLOTS, 128)], axis=1
    ).astype(BF16)
    pay_ref[0] = block
    pay_ref[1] = block


def select_call(near, far, q, k, v, g):
    smem = pl.BlockSpec(memory_space=pltpu.SMEM)
    cols = pl.BlockSpec((ROWS, GLANES), lambda b: (0, b))
    group = lambda: pl.BlockSpec((1, GSLOTS, ROWS), lambda b: (b, 0, 0))
    return pl.pallas_call(
        select_kernel,
        grid=(GROUPS,),
        in_specs=[smem, smem, cols, cols, cols, cols],
        out_specs=[pl.BlockSpec((2, GROUP, 2 * SLOTS, 128), lambda b: (0, b, 0, 0))] + [group()] * 4,
        out_shape=[
            jax.ShapeDtypeStruct((2, HEADS, 2 * SLOTS, 128), BF16),
            jax.ShapeDtypeStruct((GROUPS, GSLOTS, GLANES), BF16),
            jax.ShapeDtypeStruct((GROUPS, GSLOTS, GLANES), BF16),
            jax.ShapeDtypeStruct((GROUPS, GSLOTS, ROWS), F32),
            jax.ShapeDtypeStruct((GROUPS, GSLOTS, ROWS), F32),
        ],
        compiler_params=pltpu.CompilerParams(vmem_limit_bytes=VMEM_BYTES),
        name="select_rows",
    )(near, far, q, k, v, g)


def local_group(near_ref, far_ref, first, q_ref, k_ref, v_ref, g_ref):
    lane = iota((1, GLANES), 1)
    query = iota((1, ROWS), 1)
    allowed = iota((ROWS, ROWS), 0) <= iota((ROWS, ROWS), 1)
    q, k, v, g = q_ref[...], k_ref[...], v_ref[...], g_ref[...]
    q = (q.astype(F32) * SCALE).astype(BF16)
    row_of = iota((GLANES, 1), 0)
    kt, vt = jnp.transpose(k), jnp.transpose(v)
    zero = jnp.zeros((), BF16)
    out_t = jnp.zeros((GLANES, ROWS), F32)
    dq_t = jnp.zeros((GLANES, ROWS), F32)
    dk = jnp.zeros((ROWS, GLANES), F32)
    dv = jnp.zeros((ROWS, GLANES), F32)
    for h in range(GROUP):
        near, far = near_ref[first + h], far_ref[first + h]
        special = (query % NEAR_RATE == near) | (query == far)
        here = lane // FEAT == h
        here_t = row_of // FEAT == h
        scores = jnp.where(allowed, dot_nt(jnp.where(here, k, zero), q), LOW)
        grads = dot_nt(jnp.where(here, v, zero), g)
        weights = jnp.exp(scores - jnp.max(scores, axis=0, keepdims=True))
        total = jnp.sum(weights, axis=0, keepdims=True)
        weights = weights * jnp.where(special, 0.0, 1.0 / total)
        delta = jnp.sum(weights * grads, axis=0, keepdims=True)
        dscores = (weights * (grads - delta)).astype(BF16)
        weights = weights.astype(BF16)
        out_t += dot_nn(jnp.where(here_t, vt, zero), weights)
        dq_t += dot_nn(jnp.where(here_t, kt, zero), dscores)
        dk += dot_nn(dscores, jnp.where(here, q, zero))
        dv += dot_nn(weights, jnp.where(here, g, zero))
    return jnp.transpose(out_t), jnp.transpose(dq_t) * SCALE, dk, dv


def local_kernel(base, near_ref, far_ref, q_ref, k_ref, v_ref, g_ref, *refs):
    out_ref, dq_ref, dk_ref, dv_ref = refs[-4:]
    first = (pl.program_id(0) + base) * GROUP
    out, dq, dk, dv = local_group(near_ref, far_ref, first, q_ref, k_ref, v_ref, g_ref)
    out_ref[...] = out.astype(BF16)
    dq_ref[...] = dq.astype(BF16)
    dk_ref[...] = dk
    dv_ref[...] = dv


def local_call(base, count, near, far, q, k, v, g, done):
    smem = pl.BlockSpec(memory_space=pltpu.SMEM)
    cols = lambda: pl.BlockSpec((ROWS, GLANES), lambda b: (0, b + base))
    types = (BF16, BF16, F32, F32)
    return pl.pallas_call(
        functools.partial(local_kernel, base),
        grid=(count,),
        in_specs=[smem, smem] + [cols()] * 4 + [pl.BlockSpec(memory_space=pl.ANY)] * len(done),
        out_specs=[cols()] * 4,
        out_shape=[jax.ShapeDtypeStruct((ROWS, WIDTH), kind) for kind in types],
        input_output_aliases={6 + i: i for i in range(len(done))},
        compiler_params=pltpu.CompilerParams(vmem_limit_bytes=VMEM_BYTES),
        cost_estimate=pl.CostEstimate(
            flops=count * GROUP * 14 * ROWS * ROWS * FEAT,
            bytes_accessed=count * 7 * ROWS * GLANES * 2,
            transcendentals=count * GROUP * ROWS * ROWS,
        ),
        name="local_level",
    )(near, far, q, k, v, g, *done)


def slot_positions(near, far):
    col = iota((SEQ * SLOTS, 1), 0)
    line = iota((1, SEQ * SLOTS), 1)

    def position(index):
        slot = index % SLOTS
        return index // SLOTS * ROWS + jnp.where(slot < FAR_SLOT, near + NEAR_RATE * slot, far)

    return col, line, position(col), position(line)


def pair_halves(qk, vg):
    low = iota(qk.shape, 1) < FEAT
    q0 = jnp.where(low, qk, 0.0)
    k0 = jnp.where(low, swap_halves(qk), 0.0)
    g0 = jnp.where(low, swap_halves(vg), 0.0)
    v0 = jnp.where(low, vg, 0.0)
    k1 = jnp.where(low, 0.0, qk)
    g1 = jnp.where(low, 0.0, vg)
    return tuple(x.astype(BF16) for x in (q0, k0, v0, g0, k1, g1))


def near_kernel(near_ref, far_ref, got_ref, send_ref, stat_ref):
    head = lax.axis_index("seq") % HEADS
    near, far = near_ref[head], far_ref[head]
    got = got_ref[...].astype(F32)
    qk, vg = got[:, :SLOTS].reshape(SEQ * SLOTS, 128), got[:, SLOTS:].reshape(SEQ * SLOTS, 128)
    lse, d = unpack_stats(got)
    q0, k0, v0, g0, _, _ = pair_halves(qk, vg)
    col, line, col_at, line_at = slot_positions(near, far)
    asks = (col % SLOTS < FAR_SLOT) | ((col % SLOTS == FAR_SLOT) & (far % NEAR_RATE == near))
    allowed = asks & (line % SLOTS < FAR_SLOT) & (line_at <= col_at)
    terms = softmax_terms(dot_nt(q0, k0) * SCALE, allowed, dot_nt(g0, v0))
    lse, d = merge_terms(lse, d, *terms)
    lane = iota((SEQ * SLOTS, 128), 1)
    stats = part_lanes(lse, d, lane)
    stat_ref[...] = stats
    rows = SEQ * SLOTS
    pick = iota((SEQ, rows), 1) == iota((SEQ, rows), 0) * SLOTS + FAR_SLOT
    pick = jnp.where(pick, 1.0, 0.0).astype(BF16)
    block = jnp.concatenate([dot_nn(pick, x.astype(BF16)) for x in (qk, vg, stats)], axis=0)
    block = block.astype(BF16)
    for o in range(OUTER):
        send_ref[o] = block


def near_call(near, far, got):
    smem = pl.BlockSpec(memory_space=pltpu.SMEM)
    return pl.pallas_call(
        near_kernel,
        in_specs=[smem, smem, pl.BlockSpec(memory_space=pltpu.VMEM)],
        out_specs=[pl.BlockSpec(memory_space=pltpu.VMEM)] * 2,
        out_shape=[
            jax.ShapeDtypeStruct((OUTER, 3 * SEQ, 128), BF16),
            jax.ShapeDtypeStruct((SEQ * SLOTS, 128), F32),
        ],
        compiler_params=pltpu.CompilerParams(vmem_limit_bytes=VMEM_BYTES),
        name="near_forward",
    )(near, far, got)


def level_grads(halves, scores, allowed, grads, lse, delta):
    q0, k0, v0, g0, k1, g1 = halves
    weights = jnp.where(allowed, jnp.exp(jnp.where(allowed, scores - lse, 0.0)), 0.0)
    dscores = (weights * (grads - delta)).astype(BF16)
    weights = weights.astype(BF16)
    query_side = dot_nn(weights, v0) + dot_nn(dscores, k1)
    key_side = dot_tn(dscores, q0) + dot_tn(weights, g1)
    low = iota((1, 128), 1) < FEAT
    return query_side * jnp.where(low, 1.0, SCALE), key_side * jnp.where(low, SCALE, 1.0)


def owner_kernel(near_ref, far_ref, got_ref, stat_ref, far_got_ref, send_ref):
    head = lax.axis_index("seq") % HEADS
    segment = lax.axis_index("outer")
    near, far = near_ref[head], far_ref[head]
    rows = SEQ * SLOTS
    lane = iota((rows, 128), 1)

    far_qk = far_got_ref[:, :SEQ].reshape(rows, 128).astype(F32)
    far_vg = far_got_ref[:, SEQ : 2 * SEQ].reshape(rows, 128).astype(F32)
    far_stats = far_got_ref[:, 2 * SEQ :].reshape(rows, 128).astype(F32)
    far_halves = pair_halves(far_qk, far_vg)
    scores = dot_nt(far_halves[0], far_halves[1]) * SCALE
    grads = dot_nt(far_halves[3], far_halves[2])
    allowed = iota((rows, rows), 1) <= iota((rows, rows), 0)
    top, total, grad_total = softmax_terms(scores, allowed, grads)
    lse, delta = merge_terms(*read_parts(far_stats, lane), top, total, grad_total)
    query_side, key_side = level_grads(far_halves, scores, allowed, grads, lse, delta)
    own_stats = part_lanes(top + jnp.log(total), grad_total / total, lane).astype(BF16)

    row, column = iota((rows, rows), 0), iota((rows, rows), 1)
    own = column == segment * SEQ + row // SLOTS
    to_far = jnp.where(own & (row % SLOTS == FAR_SLOT), 1.0, 0.0).astype(BF16)
    to_all = jnp.where(own, 1.0, 0.0).astype(BF16)
    first = dot_nn(to_far, query_side.astype(BF16))
    second = dot_nn(to_far, key_side.astype(BF16))
    far_lse, far_d = read_parts(dot_nn(to_all, own_stats), lane)

    col, line, col_at, line_at = slot_positions(near, far)
    slot = col % SLOTS
    active = (slot == FAR_SLOT) | ((slot < FAR_SLOT) & (near + NEAR_RATE * slot == far))
    lse, d = read_parts(stat_ref[...], lane)
    merged_lse, merged_d = merge_terms(lse, d, far_lse, 1.0, far_d)
    lse, delta = jnp.where(active, merged_lse, lse), jnp.where(active, merged_d, d)

    got = got_ref[...].astype(F32)
    halves = pair_halves(got[:, :SLOTS].reshape(rows, 128), got[:, SLOTS:].reshape(rows, 128))
    allowed = (slot < FAR_SLOT) & (line % SLOTS < FAR_SLOT) & (line_at <= col_at)
    query_side, key_side = level_grads(
        halves, dot_nt(halves[0], halves[1]) * SCALE, allowed, dot_nt(halves[3], halves[2]), lse, delta
    )
    first += query_side
    second += key_side
    used = slot <= FAR_SLOT
    stats = pack_stats(jnp.where(used, lse, 0.0), jnp.where(used, delta, 0.0))
    first = jnp.where(slot == STAT_SLOT, stats, first)
    send_ref[...] = jnp.concatenate(
        [first.reshape(SEQ, SLOTS, 128), second.reshape(SEQ, SLOTS, 128)], axis=1
    ).astype(BF16)


def owner_call(near, far, got, stats, far_got):
    smem = pl.BlockSpec(memory_space=pltpu.SMEM)
    vmem = pl.BlockSpec(memory_space=pltpu.VMEM)
    return pl.pallas_call(
        owner_kernel,
        in_specs=[smem, smem, vmem, vmem, vmem],
        out_specs=vmem,
        out_shape=jax.ShapeDtypeStruct((SEQ, 2 * SLOTS, 128), BF16),
        compiler_params=pltpu.CompilerParams(vmem_limit_bytes=VMEM_BYTES),
        name="owner_level",
    )(near, far, got, stats, far_got)


def finish_kernel(
    near_ref, far_ref, got_ref, qs_ref, gs_ref, s_ref, gv_ref, k_ref, v_ref,
    out_in, dq_in, dk_in, dv_in, out_ref, dq_ref, dk_ref, dv_ref,
):
    row, repeat, slot = slot_rows(near_ref, far_ref, pl.program_id(0) * GROUP)
    pick = jnp.where(iota((GSLOTS, ROWS), 1) == row, 1.0, 0.0).astype(BF16)
    mask = head_mask()
    got = got_ref[...].astype(F32)
    lse, delta = unpack_stats(got)
    used = slot <= FAR_SLOT
    low = iota((GSLOTS, 128), 1) < FEAT

    def spread(x, keep_low):
        x = jnp.where(used & (low if keep_low else ~low), x, 0.0)
        x = x + swap_halves(x)
        return jnp.where(mask, jnp.concatenate([x, x], axis=1), 0.0)

    first = got[:, :SLOTS].reshape(GSLOTS, 128)
    second = got[:, SLOTS:].reshape(GSLOTS, 128)
    weights = jnp.where(repeat, 0.0, jnp.exp(s_ref[0] - lse))
    dscores = (weights * (gv_ref[0] - delta)).astype(BF16)
    weights = weights.astype(BF16)
    out = jnp.where(mask, dot_nn(weights, v_ref[...]), 0.0) + spread(first, True)
    dq = jnp.where(mask, dot_nn(dscores, k_ref[...]), 0.0) * SCALE + spread(first, False)
    out_ref[...] = (out_in[...].astype(F32) + dot_tn(pick, out.astype(BF16))).astype(BF16)
    dq_ref[...] = (dq_in[...].astype(F32) + dot_tn(pick, dq.astype(BF16))).astype(BF16)
    qs = (qs_ref[0].astype(F32) * SCALE).astype(BF16)
    dk = dot_tn(dscores, qs) + dot_tn(pick, spread(second, True).astype(BF16))
    dv = dot_tn(weights, gs_ref[0]) + dot_tn(pick, spread(second, False).astype(BF16))
    dk_ref[...] = (dk_in[...] + dk).astype(BF16)
    dv_ref[...] = (dv_in[...] + dv).astype(BF16)


def finish_call(near, far, got, qs, gs, s, gv, k, v, parts):
    smem = pl.BlockSpec(memory_space=pltpu.SMEM)
    cols = lambda: pl.BlockSpec((ROWS, GLANES), lambda b: (0, b))
    group = lambda: pl.BlockSpec((1, GSLOTS, ROWS), lambda b: (b, 0, 0))
    chunk = pl.BlockSpec((GROUP, 2 * SLOTS, 128), lambda b: (b, 0, 0))
    return pl.pallas_call(
        finish_kernel,
        grid=(GROUPS,),
        in_specs=[smem, smem, chunk] + [group()] * 4 + [cols()] * 6,
        out_specs=[cols()] * 4,
        out_shape=[jax.ShapeDtypeStruct((ROWS, WIDTH), BF16)] * 4,
        compiler_params=pltpu.CompilerParams(vmem_limit_bytes=VMEM_BYTES),
        name="finish_rows",
    )(near, far, got, qs, gs, s, gv, k, v, *parts)


def exchange(x, axis):
    return lax.all_to_all(x, axis, split_axis=0, concat_axis=0, tiled=True)


def on_device(queries, keys, values, out_grad, near_offsets, far_offsets):
    arrays = (queries, keys, values, out_grad)
    half = GROUPS // 2
    pay, qs, gs, s, gv = select_call(near_offsets, far_offsets, *arrays)
    got = exchange(pay.reshape(SEQ, 2 * SLOTS, 128), "seq")
    (near_1, far_1), _ = lax.optimization_barrier(((near_offsets, far_offsets), pay))
    parts = local_call(0, half, near_1, far_1, *arrays, ())
    got, parts = lax.optimization_barrier((got, parts))
    far_pay, stats = near_call(near_offsets, far_offsets, got)
    far_got = exchange(far_pay, "outer")
    back = owner_call(near_offsets, far_offsets, got, stats, far_got)
    (near_2, far_2), back = lax.optimization_barrier(((near_offsets, far_offsets), back))
    back_got = exchange(back, "seq")
    parts = local_call(half, GROUPS - half, near_2, far_2, *arrays, parts)
    return finish_call(
        near_offsets, far_offsets, back_got, qs, gs, s, gv, keys, values, parts
    )


def solution(mesh):
    split = P(("outer", "seq"), None)
    return jax.shard_map(
        on_device,
        mesh=mesh,
        in_specs=(split, split, split, split, P(), P()),
        out_specs=(split, split, split, split),
        check_vma=False,
    )
```

time: 1640 us -> 65.9 us (0.04)
  waiting for transfers between devices: 911 us -> 7.16 us
  local copies, waits for them, and re-layouts: 448 us -> 1.3 us
  blocking collectives: 178 us -> 12.5 us
  matrix products: 41.4 us -> 0 us
  Pallas kernels: 0 us -> 27 us
  other arithmetic: 25 us -> 0 us
    reduce_scatter x6 -> x0, waiting for transfers between devices: 911 us -> none  [the longest x1 214 us: on_device(): lax.psum_scatter(far_dk_all.astype(jnp.bfloat16), 'seq', scatter_dimensio...]
    gather x25 -> x0, local copies, waits for them, and re-layouts: 383 us -> none  [select_rows(): return jnp.take_along_axis(shaped, choose_index, axis=1)[:, 0]]
    all_gather x6 -> x0, blocking collectives: 178 us -> none  [the longest x1 41.1 us: on_device(): lax.all_gather(far_value_o, 'seq', axis=0, tiled=True)]
    dot_general x34 -> x0, matrix products: 41.4 us -> none  [the longest x5 8.75 us: attend_level(): jnp.einsum('cue,eco->uco', attention_weight.astype(jnp.bfloat16), value_p...]
    pallas_call x0 -> x6, Pallas kernels: none -> 27 us  [the longest x2 11.6 us: local_call(): pl.pallas_call(functools.partial(local_kernel, base), grid=(count,), in_s...]
    another operation x21 -> x0, local copies, waits for them, and re-layouts: 21.9 us -> none  [the longest x8 17.3 us: select_rows(): source.reshape((source.shape[0] // dilation, dilation) + source.shape[1:])]
    broadcast_in_dim x19 -> x0, local copies, waits for them, and re-layouts: 17.7 us -> none  [spread_rows(): spread = jnp.where(chosen, source[:, None], filler)]
    all_to_all x0 -> x2, starting transfers between devices: none -> 16.7 us  [exchange(): return lax.all_to_all(x, axis, split_axis=0, concat_axis=0, tiled=True)]
  transfers between devices with their start and end apart: 6 -> 2, of which waited for: 6 -> 2; matrix products, arithmetic and copies ran while one was open for 4% -> 0% of each run, Pallas kernels for 0% -> 18%
where the time goes in v1:
time: 65.9 us; the launch traced here: 65.4 us
  Pallas kernels  27 us (41%)
  starting transfers between devices  16.7 us (25%)
  blocking collectives  12.5 us (19%)
  waiting for transfers between devices  7.16 us (11%)
  local copies, waits for them, and re-layouts  1.3 us (2%)
    all_to_all x2, starting transfers between devices, exchange(): return lax.all_to_all(x, axis, split_axis=0, concat_axis=0, tiled=True)  16.7 us
    all_to_all x1, blocking collectives, exchange(): return lax.all_to_all(x, axis, split_axis=0, concat_axis=0, tiled=True)  12.5 us
    pallas_call x2, Pallas kernels, local_call(): pl.pallas_call(functools.partial(local_kernel, base), grid=(count,), in_s...  11.6 us
    all_to_all x2, waiting for transfers between devices, exchange(): return lax.all_to_all(x, axis, split_axis=0, concat_axis=0, tiled=True)  7.16 us
    pallas_call x1, Pallas kernels, finish_call(): pl.pallas_call(finish_kernel, grid=(GROUPS,), in_specs=[smem, smem, chunk...  5.34 us
    pallas_call x1, Pallas kernels, select_call(): pl.pallas_call(select_kernel, grid=(GROUPS,), in_specs=[smem, smem, cols,...  4.55 us
    pallas_call x1, Pallas kernels, owner_call(): pl.pallas_call(owner_kernel, in_specs=[smem, smem, vmem, vmem, vmem], out...  3.27 us
    pallas_call x1, Pallas kernels, near_call(): pl.pallas_call(near_kernel, in_specs=[smem, smem, pl.BlockSpec(memory_spa...  2.27 us
  transfers between devices with their start and end apart: 2, of which 2 were waited for; matrix products, arithmetic and copies ran while one was open for 0% of the time, Pallas kernels for 18%

profile of v1, /device:TPU:1, one launch (start us, length us, event | category | flops | bytes accessed | tf_op | source)
XLA Modules:
  0.0 65.4 jit_solution(6991969511512209735)
XLA Ops:
  0.6 4.5 %select_rows.1 = (bf16[2,16,16,128]{3,2,1,0:T(8,128)(2,1)}, bf16[4,32,256]{2,1,0:T(8,128)(2,1)}, bf16[4,32,256]{2,1,0:T(8,128)(2,1)}, f32[4,32,256]{2,1,0:T(8,128)}, f32[4,32,256]{2,1,0:T(8,128)}) custom-call(s32[16]{0:T(128)} %near_ref.9, s32[16]{0:T(128)} %far_ref.9, bf16[256,1024]{1,0:T(8,128)(2,1)} %q_ref.5, bf16[256,1024]{1,0:T(8,128)(2,1)} %k_ref.7, ...), custom_call_target="tpu_custom_call" | custom-call | tf_op jit(solution)/shard_map/select_rows/pallas_call | solution.py:163
  5.2 11.9 %all-to-all-start = ((bf16[32,16,128]{2,1,0:T(8,128)(2,1)}), bf16[32,16,128]{2,1,0:T(8,128)(2,1)S(1)}, u32[]{:S(2)}, u32[]{:S(2)}) async-start(bf16[32,16,128]{2,1,0:T(8,128)(2,1)} %bitcast.1), calls=%async_computation | async-start | bytes 262144 | tf_op jit(solution)/shard_map/all_to_all | solution.py:429
  17.1 5.8 %local_level.2 = (bf16[256,1024]{1,0:T(8,128)(2,1)}, bf16[256,1024]{1,0:T(8,128)(2,1)}, f32[256,1024]{1,0:T(8,128)}, f32[256,1024]{1,0:T(8,128)}) custom-call(s32[16]{0:T(128)} %near_ref.9, s32[16]{0:T(128)} %far_ref.9, bf16[256,1024]{1,0:T(8,128)(2,1)} %q_ref.5, bf16[256,1024]{1,0:T(8,128)(2,1)} %k_ref.7, bf16[256,1024]{1,0:T(8,128)(2,1)} %v_ref.7, ...), custom_call_target="tpu_custom_call" | custom-call | flops 469762048 | bytes 1835008 | tf_op jit(solution)/shard_map/local_level/pallas_call | solution.py:227
  22.8 3.6 %all-to-all-done.got_ref = bf16[32,16,128]{2,1,0:T(8,128)(2,1)S(1)} async-done(((bf16[32,16,128]{2,1,0:T(8,128)(2,1)}), bf16[32,16,128]{2,1,0:T(8,128)(2,1)S(1)}, u32[]{:S(2)}, u32[]{:S(2)}) %all-to-all-start) | async-done | bytes 131104 | tf_op jit(solution)/shard_map/all_to_all | solution.py:429
  26.4 0.0 copy-start
  26.4 0.7 copy-done
  27.1 2.3 %near_forward.1 = (bf16[8,96,128]{2,1,0:T(8,128)(2,1)}, f32[256,128]{1,0:T(8,128)}) custom-call(s32[16]{0:T(128)} %near_ref.9, s32[16]{0:T(128)} %far_ref.9, bf16[32,16,128]{2,1,0:T(8,128)(2,1)} %copy-done), custom_call_target="tpu_custom_call" | custom-call | tf_op jit(solution)/shard_map/near_forward/pallas_call | solution.py:292
  29.3 12.5 %all_to_all.15.far_got_ref = bf16[8,96,128]{2,1,0:T(8,128)(2,1)} all-to-all(bf16[8,96,128]{2,1,0:T(8,128)(2,1)} %get-tuple-element.38), channel_id=1, replica_groups=mesh['seq'=32,'outer'=8] {'outer'}, dimensions={0} | all-to-all | bytes 393216 | tf_op jit(solution)/shard_map/all_to_all | solution.py:429
  41.9 3.3 %owner_level.1 = bf16[32,16,128]{2,1,0:T(8,128)(2,1)} custom-call(s32[16]{0:T(128)} %near_ref.9, s32[16]{0:T(128)} %far_ref.9, bf16[32,16,128]{2,1,0:T(8,128)(2,1)} %copy-done, f32[256,128]{1,0:T(8,128)} %get-tuple-element.37.stat_ref, bf16[8,96,128]{2,1,0:T(8,128)(2,1)} %all_to_all.15.far_got_ref), custom_call_target="tpu_custom_call" | custom-call | tf_op jit(solution)/shard_map/owner_level/pallas_call | solution.py:369
  45.1 4.8 %all-to-all-start.2 = ((bf16[32,16,128]{2,1,0:T(8,128)(2,1)}), bf16[32,16,128]{2,1,0:T(8,128)(2,1)S(1)}, u32[]{:S(2)}, u32[]{:S(2)}) async-start(bf16[32,16,128]{2,1,0:T(8,128)(2,1)} %owner_level.1), calls=%async_computation.2 | async-start | bytes 262144 | tf_op jit(solution)/shard_map/all_to_all | solution.py:429
  49.9 5.8 %local_level.3 = (bf16[256,1024]{1,0:T(8,128)(2,1)}, bf16[256,1024]{1,0:T(8,128)(2,1)}, f32[256,1024]{1,0:T(8,128)}, f32[256,1024]{1,0:T(8,128)}) custom-call(s32[16]{0:T(128)} %near_ref.9, s32[16]{0:T(128)} %far_ref.9, bf16[256,1024]{1,0:T(8,128)(2,1)} %q_ref.5, ...), custom_call_target="tpu_custom_call", output_to_operand_aliasing={{0}: (6, {}), {1}: (7, {}), {2}: (8, {}), {3}: (9, {})} | custom-call | flops 469762048 | bytes 1835008 | tf_op jit(solution)/shard_map/local_level/pallas_call | solution.py:227
  55.8 3.6 %all-to-all-done.2.got_ref = bf16[32,16,128]{2,1,0:T(8,128)(2,1)S(1)} async-done(((bf16[32,16,128]{2,1,0:T(8,128)(2,1)}), bf16[32,16,128]{2,1,0:T(8,128)(2,1)S(1)}, u32[]{:S(2)}, u32[]{:S(2)}) %all-to-all-start.2) | async-done | bytes 131104 | tf_op jit(solution)/shard_map/all_to_all | solution.py:429
  59.4 0.0 copy-start.1
  59.4 0.6 copy-done.1
  60.0 5.3 %finish_rows.1 = (bf16[256,1024]{1,0:T(8,128)(2,1)}, bf16[256,1024]{1,0:T(8,128)(2,1)}, bf16[256,1024]{1,0:T(8,128)(2,1)}, bf16[256,1024]{1,0:T(8,128)(2,1)}) custom-call(s32[16]{0:T(128)} %near_ref.9, s32[16]{0:T(128)} %far_ref.9, bf16[32,16,128]{2,1,0:T(8,128)(2,1)} %copy-done.1, bf16[4,32,256]{2,1,0:T(8,128)(2,1)} %get-tuple-element.40.qs_ref, ...), custom_call_target="tpu_custom_call" | custom-call | tf_op jit(solution)/shard_map/finish_rows/pallas_call | solution.py:417
Async XLA Ops:
  5.2 21.2 %all-to-all-start = ((bf16[32,16,128]{2,1,0:T(8,128)(2,1)}), bf16[32,16,128]{2,1,0:T(8,128)(2,1)S(1)}, u32[]{:S(2)}, u32[]{:S(2)}) async-start(bf16[32,16,128]{2,1,0:T(8,128)(2,1)} %bitcast.1), calls=%async_computation | async-start | bytes 262144 | tf_op jit(solution)/shard_map/all_to_all | solution.py:429
  26.4 0.7 %copy-start = (bf16[32,16,128]{2,1,0:T(8,128)(2,1)}, bf16[32,16,128]{2,1,0:T(8,128)(2,1)S(1)}, u32[]{:S(2)}) copy-start(bf16[32,16,128]{2,1,0:T(8,128)(2,1)S(1)} %all-to-all-done.got_ref) | copy-start | bytes 393220
  45.1 14.2 %all-to-all-start.2 = ((bf16[32,16,128]{2,1,0:T(8,128)(2,1)}), bf16[32,16,128]{2,1,0:T(8,128)(2,1)S(1)}, u32[]{:S(2)}, u32[]{:S(2)}) async-start(bf16[32,16,128]{2,1,0:T(8,128)(2,1)} %owner_level.1), calls=%async_computation.2 | async-start | bytes 262144 | tf_op jit(solution)/shard_map/all_to_all | solution.py:429
  59.4 0.7 copy-start.1

commit v2 on v1

--- a/solution.py
+++ b/solution.py
@@ -18,6 +18,8 @@
 SLOTS = 8
 FAR_SLOT = 4
 STAT_SLOT = 5
+NEAR_LANE = 48
+FAR_LANE = 49
 GROUP = 4
 GROUPS = HEADS // GROUP
 GLANES = GROUP * FEAT
@@ -26,7 +28,11 @@
 LOW = -1e30
 F32 = jnp.float32
 BF16 = jnp.bfloat16
-VMEM_BYTES = 60 * 1024 * 1024
+VMEM_BYTES = 24 * 1024 * 1024
+
+
+def pinned(space, *arrays):
+    return tuple(pltpu.with_memory_space_constraint(x, space) for x in arrays)
 
 
 def iota(shape, axis):
@@ -86,15 +92,20 @@
     return pltpu.roll(x, FEAT, 1)
 
 
-def slot_rows(near_ref, far_ref, first):
+def group_offsets(near_ref, far_ref, first):
     index = iota((GSLOTS, 1), 0)
-    slot = index % SLOTS
     near = jnp.zeros((GSLOTS, 1), jnp.int32)
     far = jnp.zeros((GSLOTS, 1), jnp.int32)
     for h in range(GROUP):
         here = index // SLOTS == h
         near = jnp.where(here, near_ref[first + h], near)
         far = jnp.where(here, far_ref[first + h], far)
+    return near, far
+
+
+def slot_rows(near_ref, far_ref, first):
+    near, far = group_offsets(near_ref, far_ref, first)
+    slot = iota((GSLOTS, 1), 0) % SLOTS
     row = jnp.where(slot < FAR_SLOT, near + NEAR_RATE * slot, jnp.where(slot == FAR_SLOT, far, -1))
     repeat = (slot == FAR_SLOT) & (far % NEAR_RATE == near)
     return row, repeat, slot
@@ -119,69 +130,115 @@
     return overall + jnp.log(mass), (old * d + new * grad_total) / mass
 
 
-def select_kernel(near_ref, far_ref, q_ref, k_ref, v_ref, g_ref, pay_ref, qs_ref, gs_ref, s_ref, gv_ref):
-    row, _, slot = slot_rows(near_ref, far_ref, pl.program_id(0) * GROUP)
-    pick = jnp.where(iota((GSLOTS, ROWS), 1) == row, 1.0, 0.0).astype(BF16)
+OFFSET_SCRATCH = [
+    pltpu.SMEM((HEADS,), jnp.int32),
+    pltpu.SMEM((HEADS,), jnp.int32),
+    pltpu.SemaphoreType.DMA((2,)),
+]
+
+
+def start_offsets(near_in, far_in, near_ref, far_ref, sems):
+    copies = [
+        pltpu.make_async_copy(near_in, near_ref, sems.at[0]),
+        pltpu.make_async_copy(far_in, far_ref, sems.at[1]),
+    ]
+    for copy in copies:
+        copy.start()
+    return copies
+
+
+def start_copies(sources, base, count, buffer, sems):
+    copies = []
+    for b in range(count):
+        here = pl.ds(b * GLANES, GLANES)
+        there = pl.ds((base + b) * GLANES, GLANES)
+        copies.append(
+            [
+                pltpu.make_async_copy(source.at[:, there], buffer.at[i, :, here], sems.at[b, i])
+                for i, source in enumerate(sources)
+            ]
+        )
+    for group in copies:
+        for copy in group:
+            copy.start()
+    return copies
+
+
+def start_whole(sources, buffer, sems):
+    copies = [
+        pltpu.make_async_copy(source, buffer.at[i], sems.at[i]) for i, source in enumerate(sources)
+    ]
+    for copy in copies:
+        copy.start()
+    return copies
+
+
+def select_kernel(
+    near_in, far_in, q_ref, k_ref, v_ref, g_ref, pay_ref, near_ref, far_ref, offset_sems, buffer, sems
+):
+    offset_copies = start_offsets(near_in, far_in, near_ref, far_ref, offset_sems)
+    copies = start_whole((q_ref, k_ref, v_ref, g_ref), buffer, sems)
+    for copy in offset_copies:
+        copy.wait()
     mask = head_mask()
-
-    def selected(ref):
-        return jnp.where(mask, dot_nn(pick, ref[...]), 0.0)
-
-    def folded(x):
-        x = x[:, :128] + x[:, 128:]
-        return x + swap_halves(x)
-
-    qs, ks, vs, gs = selected(q_ref), selected(k_ref), selected(v_ref), selected(g_ref)
-    qb, gb = qs.astype(BF16), gs.astype(BF16)
-    qs_ref[0] = qb
-    gs_ref[0] = gb
-    allowed = iota((GSLOTS, ROWS), 1) <= row
-    scores = jnp.where(allowed, dot_nt(qb, k_ref[...]) * SCALE, LOW)
-    grads = dot_nt(gb, v_ref[...])
-    s_ref[0] = scores
-    gv_ref[0] = grads
-    top, total, grad_total = softmax_terms(scores, allowed, grads)
-    used = slot <= FAR_SLOT
-    total = jnp.where(used, total, 1.0)
-    lse = jnp.where(used, top + jnp.log(total), 0.0)
-    stats = pack_stats(lse, jnp.where(used, grad_total / total, 0.0))
-    low_half = iota((GSLOTS, 128), 1) < FEAT
-    qk = jnp.where(low_half, folded(qs), folded(ks))
-    vg = jnp.where(low_half, folded(vs), folded(gs))
-    qk = jnp.where(slot == STAT_SLOT, stats, qk)
-    block = jnp.concatenate(
-        [qk.reshape(GROUP, SLOTS, 128), vg.reshape(GROUP, SLOTS, 128)], axis=1
-    ).astype(BF16)
-    pay_ref[0] = block
-    pay_ref[1] = block
+    for b in range(GROUPS):
+        row, _, slot = slot_rows(near_ref, far_ref, b * GROUP)
+        pick = jnp.where(iota((GSLOTS, ROWS), 1) == row, 1.0, 0.0).astype(BF16)
+        if b == 0:
+            for copy in copies:
+                copy.wait()
+        q, k, v, g = (buffer[i, :, b * GLANES : (b + 1) * GLANES] for i in range(4))
+
+        def selected(x):
+            return jnp.where(mask, dot_nn(pick, x), 0.0)
+
+        def folded(x):
+            x = x[:, :128] + x[:, 128:]
+            return x + swap_halves(x)
+
+        qs, ks, vs, gs = selected(q), selected(k), selected(v), selected(g)
+        qb, gb = qs.astype(BF16), gs.astype(BF16)
+        allowed = iota((GSLOTS, ROWS), 1) <= row
+        scores = jnp.where(allowed, dot_nt(qb, k) * SCALE, LOW)
+        grads = dot_nt(gb, v)
+        top, total, grad_total = softmax_terms(scores, allowed, grads)
+        used = slot <= FAR_SLOT
+        total = jnp.where(used, total, 1.0)
+        lse = jnp.where(used, top + jnp.log(total), 0.0)
+        stats = pack_stats(lse, jnp.where(used, grad_total / total, 0.0))
+        lane = iota((GSLOTS, 128), 1)
+        near, far = group_offsets(near_ref, far_ref, b * GROUP)
+        stats = jnp.where(lane == NEAR_LANE, near, jnp.where(lane == FAR_LANE, far, stats))
+        low_half = iota((GSLOTS, 128), 1) < FEAT
+        qk = jnp.where(low_half, folded(qs), folded(ks))
+        vg = jnp.where(low_half, folded(vs), folded(gs))
+        qk = jnp.where(slot == STAT_SLOT, stats, qk)
+        block = jnp.concatenate(
+            [qk.reshape(GROUP, SLOTS, 128), vg.reshape(GROUP, SLOTS, 128)], axis=1
+        ).astype(BF16)
+        pay_ref[0, b * GROUP : (b + 1) * GROUP] = block
+        pay_ref[1, b * GROUP : (b + 1) * GROUP] = block
 
 
 def select_call(near, far, q, k, v, g):
-    smem = pl.BlockSpec(memory_space=pltpu.SMEM)
-    cols = pl.BlockSpec((ROWS, GLANES), lambda b: (0, b))
-    group = lambda: pl.BlockSpec((1, GSLOTS, ROWS), lambda b: (b, 0, 0))
+    hbm = pl.BlockSpec(memory_space=pltpu.HBM)
+    vmem = pl.BlockSpec(memory_space=pltpu.VMEM)
     return pl.pallas_call(
         select_kernel,
-        grid=(GROUPS,),
-        in_specs=[smem, smem, cols, cols, cols, cols],
-        out_specs=[pl.BlockSpec((2, GROUP, 2 * SLOTS, 128), lambda b: (0, b, 0, 0))] + [group()] * 4,
-        out_shape=[
-            jax.ShapeDtypeStruct((2, HEADS, 2 * SLOTS, 128), BF16),
-            jax.ShapeDtypeStruct((GROUPS, GSLOTS, GLANES), BF16),
-            jax.ShapeDtypeStruct((GROUPS, GSLOTS, GLANES), BF16),
-            jax.ShapeDtypeStruct((GROUPS, GSLOTS, ROWS), F32),
-            jax.ShapeDtypeStruct((GROUPS, GSLOTS, ROWS), F32),
-        ],
+        in_specs=[hbm] * 6,
+        out_specs=vmem,
+        out_shape=pltpu.VMEM((2, HEADS, 2 * SLOTS, 128), BF16),
+        scratch_shapes=OFFSET_SCRATCH
+        + [pltpu.VMEM((4, ROWS, WIDTH), BF16), pltpu.SemaphoreType.DMA((4,))],
         compiler_params=pltpu.CompilerParams(vmem_limit_bytes=VMEM_BYTES),
         name="select_rows",
-    )(near, far, q, k, v, g)
-
-
-def local_group(near_ref, far_ref, first, q_ref, k_ref, v_ref, g_ref):
+    )(*pinned(pltpu.HBM, near, far, q, k, v, g))
+
+
+def local_group(near_ref, far_ref, first, q, k, v, g):
     lane = iota((1, GLANES), 1)
     query = iota((1, ROWS), 1)
     allowed = iota((ROWS, ROWS), 0) <= iota((ROWS, ROWS), 1)
-    q, k, v, g = q_ref[...], k_ref[...], v_ref[...], g_ref[...]
     q = (q.astype(F32) * SCALE).astype(BF16)
     row_of = iota((GLANES, 1), 0)
     kt, vt = jnp.transpose(k), jnp.transpose(v)
@@ -210,27 +267,54 @@
     return jnp.transpose(out_t), jnp.transpose(dq_t) * SCALE, dk, dv
 
 
-def local_kernel(base, near_ref, far_ref, q_ref, k_ref, v_ref, g_ref, *refs):
-    out_ref, dq_ref, dk_ref, dv_ref = refs[-4:]
-    first = (pl.program_id(0) + base) * GROUP
-    out, dq, dk, dv = local_group(near_ref, far_ref, first, q_ref, k_ref, v_ref, g_ref)
-    out_ref[...] = out.astype(BF16)
-    dq_ref[...] = dq.astype(BF16)
-    dk_ref[...] = dk
-    dv_ref[...] = dv
-
-
-def local_call(base, count, near, far, q, k, v, g, done):
-    smem = pl.BlockSpec(memory_space=pltpu.SMEM)
-    cols = lambda: pl.BlockSpec((ROWS, GLANES), lambda b: (0, b + base))
-    types = (BF16, BF16, F32, F32)
+def local_kernel(
+    base, count, near_in, far_in, q_ref, k_ref, v_ref, g_ref,
+    query_ref, key_ref, near_ref, far_ref, offset_sems, buffer, sems
+):
+    offset_copies = start_offsets(near_in, far_in, near_ref, far_ref, offset_sems)
+    start_copies((q_ref, k_ref, v_ref, g_ref), base, count, buffer, sems)
+    for copy in offset_copies:
+        copy.wait()
+
+    def one_group(b, carry):
+        here = pl.ds(pl.multiple_of(b * GLANES, GLANES), GLANES)
+        for i, source in enumerate((q_ref, k_ref, v_ref, g_ref)):
+            there = pl.ds(pl.multiple_of((base + b) * GLANES, GLANES), GLANES)
+            pltpu.make_async_copy(source.at[:, there], buffer.at[i, :, here], sems.at[b, i]).wait()
+        arrays = tuple(buffer[i, :, here] for i in range(4))
+        row, _, _ = slot_rows(near_ref, far_ref, (base + b) * GROUP)
+        pick = jnp.where(iota((GSLOTS, ROWS), 1) == row, 1.0, 0.0).astype(BF16)
+        mask = head_mask()
+        qs = jnp.where(mask, dot_nn(pick, arrays[0]), 0.0)
+        gs = jnp.where(mask, dot_nn(pick, arrays[3]), 0.0)
+        scores = dot_nt(qs.astype(BF16), arrays[1]) * SCALE
+        scores = jnp.where(iota((GSLOTS, ROWS), 1) <= row, scores, LOW)
+        slots = (scores, dot_nt(gs.astype(BF16), arrays[2]), qs * SCALE, gs)
+        key_ref[2 * ROWS :, here] = jnp.concatenate(slots, axis=0)
+        out, dq, dk, dv = local_group(near_ref, far_ref, (base + b) * GROUP, *arrays)
+        query_ref[0, :, here] = out.astype(BF16)
+        query_ref[1, :, here] = dq.astype(BF16)
+        key_ref[:ROWS, here] = dk
+        key_ref[ROWS : 2 * ROWS, here] = dv
+        return carry
+
+    lax.fori_loop(0, count, one_group, 0)
+
+
+def local_call(base, count, near, far, q, k, v, g):
+    hbm = pl.BlockSpec(memory_space=pltpu.HBM)
+    vmem = pl.BlockSpec(memory_space=pltpu.VMEM)
+    shape = (ROWS, count * GLANES)
     return pl.pallas_call(
-        functools.partial(local_kernel, base),
-        grid=(count,),
-        in_specs=[smem, smem] + [cols()] * 4 + [pl.BlockSpec(memory_space=pl.ANY)] * len(done),
-        out_specs=[cols()] * 4,
-        out_shape=[jax.ShapeDtypeStruct((ROWS, WIDTH), kind) for kind in types],
-        input_output_aliases={6 + i: i for i in range(len(done))},
+        functools.partial(local_kernel, base, count),
+        in_specs=[hbm] * 6,
+        out_specs=[vmem] * 2,
+        out_shape=[
+            pltpu.VMEM((2,) + shape, BF16),
+            pltpu.VMEM((2 * ROWS + 4 * GSLOTS, count * GLANES), F32),
+        ],
+        scratch_shapes=OFFSET_SCRATCH
+        + [pltpu.VMEM((4,) + shape, BF16), pltpu.SemaphoreType.DMA((count, 4))],
         compiler_params=pltpu.CompilerParams(vmem_limit_bytes=VMEM_BYTES),
         cost_estimate=pl.CostEstimate(
             flops=count * GROUP * 14 * ROWS * ROWS * FEAT,
@@ -238,7 +322,7 @@
             transcendentals=count * GROUP * ROWS * ROWS,
         ),
         name="local_level",
-    )(near, far, q, k, v, g, *done)
+    )(*pinned(pltpu.HBM, near, far, q, k, v, g))
 
 
 def slot_positions(near, far):
@@ -263,10 +347,14 @@
     return tuple(x.astype(BF16) for x in (q0, k0, v0, g0, k1, g1))
 
 
-def near_kernel(near_ref, far_ref, got_ref, send_ref, stat_ref):
-    head = lax.axis_index("seq") % HEADS
-    near, far = near_ref[head], far_ref[head]
+def read_offsets(got):
+    line = got[0, STAT_SLOT : STAT_SLOT + 1, :].astype(jnp.int32)
+    return line[:, NEAR_LANE : NEAR_LANE + 1], line[:, FAR_LANE : FAR_LANE + 1]
+
+
+def near_kernel(got_ref, send_ref, stat_ref):
     got = got_ref[...].astype(F32)
+    near, far = read_offsets(got)
     qk, vg = got[:, :SLOTS].reshape(SEQ * SLOTS, 128), got[:, SLOTS:].reshape(SEQ * SLOTS, 128)
     lse, d = unpack_stats(got)
     q0, k0, v0, g0, _, _ = pair_halves(qk, vg)
@@ -287,19 +375,18 @@
         send_ref[o] = block
 
 
-def near_call(near, far, got):
-    smem = pl.BlockSpec(memory_space=pltpu.SMEM)
+def near_call(got):
     return pl.pallas_call(
         near_kernel,
-        in_specs=[smem, smem, pl.BlockSpec(memory_space=pltpu.VMEM)],
+        in_specs=[pl.BlockSpec(memory_space=pltpu.VMEM)],
         out_specs=[pl.BlockSpec(memory_space=pltpu.VMEM)] * 2,
         out_shape=[
-            jax.ShapeDtypeStruct((OUTER, 3 * SEQ, 128), BF16),
-            jax.ShapeDtypeStruct((SEQ * SLOTS, 128), F32),
+            pltpu.VMEM((OUTER, 3 * SEQ, 128), BF16),
+            pltpu.VMEM((SEQ * SLOTS, 128), F32),
         ],
         compiler_params=pltpu.CompilerParams(vmem_limit_bytes=VMEM_BYTES),
         name="near_forward",
-    )(near, far, got)
+    )(got)
 
 
 def level_grads(halves, scores, allowed, grads, lse, delta):
@@ -313,10 +400,10 @@
     return query_side * jnp.where(low, 1.0, SCALE), key_side * jnp.where(low, SCALE, 1.0)
 
 
-def owner_kernel(near_ref, far_ref, got_ref, stat_ref, far_got_ref, send_ref):
-    head = lax.axis_index("seq") % HEADS
+def owner_kernel(got_ref, stat_ref, far_got_ref, send_ref):
     segment = lax.axis_index("outer")
-    near, far = near_ref[head], far_ref[head]
+    got = got_ref[...].astype(F32)
+    near, far = read_offsets(got)
     rows = SEQ * SLOTS
     lane = iota((rows, 128), 1)
 
@@ -347,7 +434,6 @@
     merged_lse, merged_d = merge_terms(lse, d, far_lse, 1.0, far_d)
     lse, delta = jnp.where(active, merged_lse, lse), jnp.where(active, merged_d, d)
 
-    got = got_ref[...].astype(F32)
     halves = pair_halves(got[:, :SLOTS].reshape(rows, 128), got[:, SLOTS:].reshape(rows, 128))
     allowed = (slot < FAR_SLOT) & (line % SLOTS < FAR_SLOT) & (line_at <= col_at)
     query_side, key_side = level_grads(
@@ -363,66 +449,107 @@
     ).astype(BF16)
 
 
-def owner_call(near, far, got, stats, far_got):
-    smem = pl.BlockSpec(memory_space=pltpu.SMEM)
+def owner_call(got, stats, far_got):
     vmem = pl.BlockSpec(memory_space=pltpu.VMEM)
     return pl.pallas_call(
         owner_kernel,
-        in_specs=[smem, smem, vmem, vmem, vmem],
+        in_specs=[vmem, vmem, vmem],
         out_specs=vmem,
-        out_shape=jax.ShapeDtypeStruct((SEQ, 2 * SLOTS, 128), BF16),
+        out_shape=pltpu.VMEM((SEQ, 2 * SLOTS, 128), BF16),
         compiler_params=pltpu.CompilerParams(vmem_limit_bytes=VMEM_BYTES),
         name="owner_level",
-    )(near, far, got, stats, far_got)
+    )(got, stats, far_got)
 
 
 def finish_kernel(
-    near_ref, far_ref, got_ref, qs_ref, gs_ref, s_ref, gv_ref, k_ref, v_ref,
-    out_in, dq_in, dk_in, dv_in, out_ref, dq_ref, dk_ref, dv_ref,
+    near_in, far_in, got_ref, k_ref, v_ref, *refs
 ):
-    row, repeat, slot = slot_rows(near_ref, far_ref, pl.program_id(0) * GROUP)
-    pick = jnp.where(iota((GSLOTS, ROWS), 1) == row, 1.0, 0.0).astype(BF16)
+    parts, outs = (refs[:2], refs[2:4]), refs[4:8]
+    near_ref, far_ref, offset_sems, buffer, sems, results, out_sems = refs[8:]
+    offset_copies = start_offsets(near_in, far_in, near_ref, far_ref, offset_sems)
+    copies = start_whole((k_ref, v_ref), buffer, sems)
+    for copy in offset_copies:
+        copy.wait()
     mask = head_mask()
-    got = got_ref[...].astype(F32)
-    lse, delta = unpack_stats(got)
-    used = slot <= FAR_SLOT
     low = iota((GSLOTS, 128), 1) < FEAT
-
-    def spread(x, keep_low):
-        x = jnp.where(used & (low if keep_low else ~low), x, 0.0)
-        x = x + swap_halves(x)
-        return jnp.where(mask, jnp.concatenate([x, x], axis=1), 0.0)
-
-    first = got[:, :SLOTS].reshape(GSLOTS, 128)
-    second = got[:, SLOTS:].reshape(GSLOTS, 128)
-    weights = jnp.where(repeat, 0.0, jnp.exp(s_ref[0] - lse))
-    dscores = (weights * (gv_ref[0] - delta)).astype(BF16)
-    weights = weights.astype(BF16)
-    out = jnp.where(mask, dot_nn(weights, v_ref[...]), 0.0) + spread(first, True)
-    dq = jnp.where(mask, dot_nn(dscores, k_ref[...]), 0.0) * SCALE + spread(first, False)
-    out_ref[...] = (out_in[...].astype(F32) + dot_tn(pick, out.astype(BF16))).astype(BF16)
-    dq_ref[...] = (dq_in[...].astype(F32) + dot_tn(pick, dq.astype(BF16))).astype(BF16)
-    qs = (qs_ref[0].astype(F32) * SCALE).astype(BF16)
-    dk = dot_tn(dscores, qs) + dot_tn(pick, spread(second, True).astype(BF16))
-    dv = dot_tn(weights, gs_ref[0]) + dot_tn(pick, spread(second, False).astype(BF16))
-    dk_ref[...] = (dk_in[...] + dk).astype(BF16)
-    dv_ref[...] = (dv_in[...] + dv).astype(BF16)
-
-
-def finish_call(near, far, got, qs, gs, s, gv, k, v, parts):
-    smem = pl.BlockSpec(memory_space=pltpu.SMEM)
-    cols = lambda: pl.BlockSpec((ROWS, GLANES), lambda b: (0, b))
-    group = lambda: pl.BlockSpec((1, GSLOTS, ROWS), lambda b: (b, 0, 0))
-    chunk = pl.BlockSpec((GROUP, 2 * SLOTS, 128), lambda b: (b, 0, 0))
+    sends = []
+
+    def finished(i, b, value):
+        here = slice(b * GLANES, (b + 1) * GLANES)
+        results[i, :, here] = value.astype(BF16)
+        send = pltpu.make_async_copy(results.at[i, :, here], outs[i].at[:, here], out_sems.at[b, i])
+        send.start()
+        sends.append(send)
+
+    held = []
+    for b in range(GROUPS):
+        row, repeat, slot = slot_rows(near_ref, far_ref, b * GROUP)
+        pick = jnp.where(iota((GSLOTS, ROWS), 1) == row, 1.0, 0.0).astype(BF16)
+        got = got_ref[b * GROUP : (b + 1) * GROUP].astype(F32)
+        lse, delta = unpack_stats(got)
+        used = slot <= FAR_SLOT
+
+        def spread(x, keep_low):
+            x = jnp.where(used & (low if keep_low else ~low), x, 0.0)
+            x = x + swap_halves(x)
+            return jnp.where(mask, jnp.concatenate([x, x], axis=1), 0.0)
+
+        first = got[:, :SLOTS].reshape(GSLOTS, 128)
+        second = got[:, SLOTS:].reshape(GSLOTS, 128)
+        half, at = divmod(b, GROUPS // 2)
+        there = slice(at * GLANES, (at + 1) * GLANES)
+        query_part, key_part = parts[half]
+        scores, grads, qs, gs = (
+            key_part[2 * ROWS + i * GSLOTS : 2 * ROWS + (i + 1) * GSLOTS, there] for i in range(4)
+        )
+        weights = jnp.where(repeat, 0.0, jnp.exp(scores - lse))
+        dscores = (weights * (grads - delta)).astype(BF16)
+        weights = weights.astype(BF16)
+
+        def key_side(slots, rows, extra):
+            left = jnp.concatenate([slots, pick], axis=0)
+            right = jnp.concatenate([rows.astype(BF16), extra.astype(BF16)], axis=0)
+            return dot_tn(left, right)
+
+        finished(2, b, key_part[:ROWS, there] + key_side(dscores, qs, spread(second, True)))
+        finished(
+            3, b, key_part[ROWS : 2 * ROWS, there] + key_side(weights, gs, spread(second, False))
+        )
+        held.append((pick, weights, dscores, spread(first, True), spread(first, False)))
+    for copy in copies:
+        copy.wait()
+    for b in range(GROUPS):
+        here = slice(b * GLANES, (b + 1) * GLANES)
+        pick, weights, dscores, out, dq = held[b]
+        half, at = divmod(b, GROUPS // 2)
+        there = slice(at * GLANES, (at + 1) * GLANES)
+        query_part = parts[half][0]
+        out += jnp.where(mask, dot_nn(weights, buffer[1, :, here]), 0.0)
+        dq += jnp.where(mask, dot_nn(dscores, buffer[0, :, here]), 0.0) * SCALE
+        finished(0, b, query_part[0, :, there].astype(F32) + dot_tn(pick, out.astype(BF16)))
+        finished(1, b, query_part[1, :, there].astype(F32) + dot_tn(pick, dq.astype(BF16)))
+    for send in sends:
+        send.wait()
+
+
+def finish_call(near, far, got, k, v, parts):
+    hbm = pl.BlockSpec(memory_space=pltpu.HBM)
+    vmem = pl.BlockSpec(memory_space=pltpu.VMEM)
     return pl.pallas_call(
         finish_kernel,
-        grid=(GROUPS,),
-        in_specs=[smem, smem, chunk] + [group()] * 4 + [cols()] * 6,
-        out_specs=[cols()] * 4,
+        in_specs=[hbm, hbm, vmem, hbm, hbm] + [vmem] * 4,
+        out_specs=[hbm] * 4,
         out_shape=[jax.ShapeDtypeStruct((ROWS, WIDTH), BF16)] * 4,
+        scratch_shapes=OFFSET_SCRATCH
+        + [
+            pltpu.VMEM((2, ROWS, WIDTH), BF16),
+            pltpu.SemaphoreType.DMA((2,)),
+            pltpu.VMEM((4, ROWS, WIDTH), BF16),
+            pltpu.SemaphoreType.DMA((GROUPS, 4)),
+        ],
         compiler_params=pltpu.CompilerParams(vmem_limit_bytes=VMEM_BYTES),
         name="finish_rows",
-    )(near, far, got, qs, gs, s, gv, k, v, *parts)
+    )(*pinned(pltpu.HBM, near, far), got, *pinned(pltpu.HBM, k, v), *pinned(pltpu.VMEM, *parts))
 
 
 def exchange(x, axis):
@@ -432,20 +559,18 @@
 def on_device(queries, keys, values, out_grad, near_offsets, far_offsets):
     arrays = (queries, keys, values, out_grad)
     half = GROUPS // 2
-    pay, qs, gs, s, gv = select_call(near_offsets, far_offsets, *arrays)
+    pay = select_call(near_offsets, far_offsets, *arrays)
     got = exchange(pay.reshape(SEQ, 2 * SLOTS, 128), "seq")
     (near_1, far_1), _ = lax.optimization_barrier(((near_offsets, far_offsets), pay))
-    parts = local_call(0, half, near_1, far_1, *arrays, ())
+    parts = tuple(local_call(0, half, near_1, far_1, *arrays))
     got, parts = lax.optimization_barrier((got, parts))
-    far_pay, stats = near_call(near_offsets, far_offsets, got)
+    far_pay, stats = near_call(got)
     far_got = exchange(far_pay, "outer")
-    back = owner_call(near_offsets, far_offsets, got, stats, far_got)
+    back = owner_call(got, stats, far_got)
     (near_2, far_2), back = lax.optimization_barrier(((near_offsets, far_offsets), back))
     back_got = exchange(back, "seq")
-    parts = local_call(half, GROUPS - half, near_2, far_2, *arrays, parts)
-    return finish_call(
-        near_offsets, far_offsets, back_got, qs, gs, s, gv, keys, values, parts
-    )
+    parts += tuple(local_call(half, GROUPS - half, near_2, far_2, *arrays))
+    return finish_call(near_offsets, far_offsets, back_got, keys, values, parts)
 
 
 def solution(mesh):

time: 65.9 us -> 58.8 us (0.89)
  Pallas kernels: 27 us -> 19.9 us
    pallas_call x6, Pallas kernels: 27 us -> 19.9 us  [the longest x2 10.3 us: local_call(): pl.pallas_call(functools.partial(local_kernel, base, count), in_specs=[hb...]
where the time goes in v2:
time: 58.8 us; the launch traced here: 58.4 us
  Pallas kernels  19.9 us (34%)
  starting transfers between devices  16.1 us (27%)
  blocking collectives  12.2 us (21%)
  waiting for transfers between devices  7.66 us (13%)
  local copies, waits for them, and re-layouts  1.83 us (3%)
  between operations  0.69 us (1%)
    all_to_all x2, starting transfers between devices, exchange(): return lax.all_to_all(x, axis, split_axis=0, concat_axis=0, tiled=True)  16.1 us
    all_to_all x1, blocking collectives, exchange(): return lax.all_to_all(x, axis, split_axis=0, concat_axis=0, tiled=True)  12.2 us
    pallas_call x2, Pallas kernels, local_call(): pl.pallas_call(functools.partial(local_kernel, base, count), in_specs=[hb...  10.3 us
    all_to_all x2, waiting for transfers between devices, exchange(): return lax.all_to_all(x, axis, split_axis=0, concat_axis=0, tiled=True)  7.66 us
    pallas_call x1, Pallas kernels, finish_call(): pl.pallas_call(finish_kernel, in_specs=[hbm, hbm, vmem, hbm, hbm] + [vmem...  3.42 us
    pallas_call x1, Pallas kernels, select_call(): pl.pallas_call(select_kernel, in_specs=[hbm] * 6, out_specs=vmem, out_sha...  3.24 us
    pallas_call x1, Pallas kernels, owner_call(): pl.pallas_call(owner_kernel, in_specs=[vmem, vmem, vmem], out_specs=vmem,...  2.22 us
    unnamed x4, local copies, waits for them, and re-layouts  1.83 us
  transfers between devices with their start and end apart: 2, of which 2 were waited for; matrix products, arithmetic and copies ran while one was open for 0% of the time, Pallas kernels for 18%

profile of v2, /device:TPU:1, one launch (start us, length us, event | category | flops | bytes accessed | tf_op | source)
XLA Modules:
  0.0 58.4 jit_solution(9348806822443357665)
XLA Ops:
  0.6 3.2 %select_rows.1 = bf16[2,16,16,128]{3,2,1,0:T(8,128)(2,1)} custom-call(s32[16]{0:T(128)} %near_in.5, s32[16]{0:T(128)} %far_in.5, bf16[256,1024]{1,0:T(8,128)(2,1)} %q_ref.5, bf16[256,1024]{1,0:T(8,128)(2,1)} %k_ref.7, bf16[256,1024]{1,0:T(8,128)(2,1)} %v_ref.7, bf16[256,1024]{1,0:T(8,128)(2,1)} %g_ref.5), custom_call_target="tpu_custom_call" | custom-call | tf_op jit(solution)/shard_map/select_rows/pallas_call | solution.py:226
  3.9 11.9 %all-to-all-start = ((bf16[32,16,128]{2,1,0:T(8,128)(2,1)}), bf16[32,16,128]{2,1,0:T(8,128)(2,1)S(1)}, u32[]{:S(2)}, u32[]{:S(2)}) async-start(bf16[32,16,128]{2,1,0:T(8,128)(2,1)} %bitcast), calls=%async_computation | async-start | bytes 262144 | tf_op jit(solution)/shard_map/all_to_all | solution.py:556
  15.8 5.1 %local_level.2 = (bf16[2,256,512]{2,1,0:T(8,128)(2,1)S(1)}, f32[640,512]{1,0:T(8,128)S(1)}) custom-call(s32[16]{0:T(128)} %near_in.5, s32[16]{0:T(128)} %far_in.5, bf16[256,1024]{1,0:T(8,128)(2,1)} %q_ref.5, bf16[256,1024]{1,0:T(8,128)(2,1)} %k_ref.7, bf16[256,1024]{1,0:T(8,128)(2,1)} %v_ref.7, bf16[256,1024]{1,0:T(8,128)(2,1)} %g_ref.5), custom_call_target="tpu_custom_call" | custom-call | flops 469762048 | bytes 1835008 | tf_op jit(solution)/shard_map/local_level/pallas_call | solution.py:308
  20.9 4.2 %all-to-all-done.got_ref = bf16[32,16,128]{2,1,0:T(8,128)(2,1)S(1)} async-done(((bf16[32,16,128]{2,1,0:T(8,128)(2,1)}), bf16[32,16,128]{2,1,0:T(8,128)(2,1)S(1)}, u32[]{:S(2)}, u32[]{:S(2)}) %all-to-all-start) | async-done | bytes 131104 | tf_op jit(solution)/shard_map/all_to_all | solution.py:556
  25.1 0.7 %near_forward.1 = (bf16[8,96,128]{2,1,0:T(8,128)(2,1)S(1)}, f32[256,128]{1,0:T(8,128)S(1)}) custom-call(bf16[32,16,128]{2,1,0:T(8,128)(2,1)S(1)} %all-to-all-done.got_ref), custom_call_target="tpu_custom_call" | custom-call | tf_op jit(solution)/shard_map/near_forward/pallas_call | solution.py:379
  25.8 12.2 %all_to_all.15.far_got_ref = bf16[8,96,128]{2,1,0:T(8,128)(2,1)S(1)} all-to-all(bf16[8,96,128]{2,1,0:T(8,128)(2,1)S(1)} %get-tuple-element.24), channel_id=1, replica_groups=mesh['seq'=32,'outer'=8] {'outer'}, dimensions={0} | all-to-all | bytes 393216 | tf_op jit(solution)/shard_map/all_to_all | solution.py:556
  38.1 2.2 %owner_level.1 = bf16[32,16,128]{2,1,0:T(8,128)(2,1)} custom-call(bf16[32,16,128]{2,1,0:T(8,128)(2,1)S(1)} %all-to-all-done.got_ref, f32[256,128]{1,0:T(8,128)S(1)} %get-tuple-element.23.stat_ref, bf16[8,96,128]{2,1,0:T(8,128)(2,1)S(1)} %all_to_all.15.far_got_ref), custom_call_target="tpu_custom_call" | custom-call | tf_op jit(solution)/shard_map/owner_level/pallas_call | solution.py:454
  40.3 4.2 %all-to-all-start.2 = ((bf16[32,16,128]{2,1,0:T(8,128)(2,1)}), bf16[32,16,128]{2,1,0:T(8,128)(2,1)S(1)}, u32[]{:S(2)}, u32[]{:S(2)}) async-start(bf16[32,16,128]{2,1,0:T(8,128)(2,1)} %owner_level.1), calls=%async_computation.2 | async-start | bytes 262144 | tf_op jit(solution)/shard_map/all_to_all | solution.py:556
  44.5 5.1 %local_level.3 = (bf16[2,256,512]{2,1,0:T(8,128)(2,1)S(1)}, f32[640,512]{1,0:T(8,128)S(1)}) custom-call(s32[16]{0:T(128)} %near_in.5, s32[16]{0:T(128)} %far_in.5, bf16[256,1024]{1,0:T(8,128)(2,1)} %q_ref.5, bf16[256,1024]{1,0:T(8,128)(2,1)} %k_ref.7, bf16[256,1024]{1,0:T(8,128)(2,1)} %v_ref.7, bf16[256,1024]{1,0:T(8,128)(2,1)} %g_ref.5), custom_call_target="tpu_custom_call" | custom-call | flops 469762048 | bytes 1835008 | tf_op jit(solution)/shard_map/local_level/pallas_call | solution.py:308
  49.6 0.0 copy-start
  49.7 0.8 %copy-done = bf16[2,256,512]{2,1,0:T(8,128)(2,1)} copy-done((bf16[2,256,512]{2,1,0:T(8,128)(2,1)}, bf16[2,256,512]{2,1,0:T(8,128)(2,1)S(1)}, u32[]{:S(2)}) %copy-start) | copy-done | bytes 524312
  50.4 3.5 %all-to-all-done.2.got_ref = bf16[32,16,128]{2,1,0:T(8,128)(2,1)S(1)} async-done(((bf16[32,16,128]{2,1,0:T(8,128)(2,1)}), bf16[32,16,128]{2,1,0:T(8,128)(2,1)S(1)}, u32[]{:S(2)}, u32[]{:S(2)}) %all-to-all-start.2) | async-done | bytes 131104 | tf_op jit(solution)/shard_map/all_to_all | solution.py:556
  53.9 0.0 copy-start.1
  53.9 1.0 %copy-done.1 = bf16[2,256,512]{2,1,0:T(8,128)(2,1)S(1)} copy-done((bf16[2,256,512]{2,1,0:T(8,128)(2,1)S(1)}, bf16[2,256,512]{2,1,0:T(8,128)(2,1)}, u32[]{:S(2)}) %copy-start.1) | copy-done | bytes 524312
  54.9 3.4 %finish_rows.1 = (bf16[256,1024]{1,0:T(8,128)(2,1)}, bf16[256,1024]{1,0:T(8,128)(2,1)}, bf16[256,1024]{1,0:T(8,128)(2,1)}, bf16[256,1024]{1,0:T(8,128)(2,1)}) custom-call(s32[16]{0:T(128)} %near_in.5, s32[16]{0:T(128)} %far_in.5, bf16[32,16,128]{2,1,0:T(8,128)(2,1)S(1)} %all-to-all-done.2.got_ref, bf16[256,1024]{1,0:T(8,128)(2,1)} %k_ref.7, ...), custom_call_target="tpu_custom_call" | custom-call | tf_op jit(solution)/shard_map/finish_rows/pallas_call | solution.py:538
Async XLA Ops:
  3.9 21.2 %all-to-all-start = ((bf16[32,16,128]{2,1,0:T(8,128)(2,1)}), bf16[32,16,128]{2,1,0:T(8,128)(2,1)S(1)}, u32[]{:S(2)}, u32[]{:S(2)}) async-start(bf16[32,16,128]{2,1,0:T(8,128)(2,1)} %bitcast), calls=%async_computation | async-start | bytes 262144 | tf_op jit(solution)/shard_map/all_to_all | solution.py:556
  40.3 13.6 %all-to-all-start.2 = ((bf16[32,16,128]{2,1,0:T(8,128)(2,1)}), bf16[32,16,128]{2,1,0:T(8,128)(2,1)S(1)}, u32[]{:S(2)}, u32[]{:S(2)}) async-start(bf16[32,16,128]{2,1,0:T(8,128)(2,1)} %owner_level.1), calls=%async_computation.2 | async-start | bytes 262144 | tf_op jit(solution)/shard_map/all_to_all | solution.py:556
  49.6 0.8 %copy-start = (bf16[2,256,512]{2,1,0:T(8,128)(2,1)}, bf16[2,256,512]{2,1,0:T(8,128)(2,1)S(1)}, u32[]{:S(2)}) copy-start(bf16[2,256,512]{2,1,0:T(8,128)(2,1)S(1)} %get-tuple-element.30.refs_2_) | copy-start | bytes 1572868
  53.9 1.0 %copy-start.1 = (bf16[2,256,512]{2,1,0:T(8,128)(2,1)S(1)}, bf16[2,256,512]{2,1,0:T(8,128)(2,1)}, u32[]{:S(2)}) copy-start(bf16[2,256,512]{2,1,0:T(8,128)(2,1)} %copy-done) | copy-start | bytes 1572868

commit v3 on v2

--- a/solution.py
+++ b/solution.py
@@ -26,6 +26,7 @@
 GSLOTS = GROUP * SLOTS
 SCALE = FEAT**-0.5
 LOW = -1e30
+SLOT_PARTS = 8
 F32 = jnp.float32
 BF16 = jnp.bfloat16
 VMEM_BYTES = 24 * 1024 * 1024
@@ -145,6 +146,21 @@
     for copy in copies:
         copy.start()
     return copies
+
+
+def pick_matrix(row):
+    return jnp.where(iota((GSLOTS, ROWS), 1) == row, 1.0, 0.0).astype(BF16)
+
+
+def slot_stats(scores, row, grads, live):
+    allowed = iota((GSLOTS, ROWS), 1) <= row
+    masked = jnp.where(allowed, scores, LOW)
+    top = jnp.max(masked, axis=1, keepdims=True)
+    weights = jnp.where(allowed & live, jnp.exp(masked - top), 0.0)
+    total = jnp.where(live, jnp.sum(weights, axis=1, keepdims=True), 1.0)
+    scale = 1.0 / total
+    d = jnp.sum(weights * grads, axis=1, keepdims=True) * scale
+    return jnp.where(live, top + jnp.log(total), 0.0), d, weights * scale, grads - d
 
 
 def start_copies(sources, base, count, buffer, sems):
@@ -177,41 +193,38 @@
     near_in, far_in, q_ref, k_ref, v_ref, g_ref, pay_ref, near_ref, far_ref, offset_sems, buffer, sems
 ):
     offset_copies = start_offsets(near_in, far_in, near_ref, far_ref, offset_sems)
-    copies = start_whole((q_ref, k_ref, v_ref, g_ref), buffer, sems)
+    copies = start_whole((q_ref, g_ref, k_ref, v_ref), buffer, sems)
     for copy in offset_copies:
         copy.wait()
+    groups = range(GROUPS)
+    rows = [slot_rows(near_ref, far_ref, b * GROUP)[0] for b in groups]
+    picks = [pick_matrix(row) for row in rows]
     mask = head_mask()
-    for b in range(GROUPS):
-        row, _, slot = slot_rows(near_ref, far_ref, b * GROUP)
-        pick = jnp.where(iota((GSLOTS, ROWS), 1) == row, 1.0, 0.0).astype(BF16)
-        if b == 0:
-            for copy in copies:
-                copy.wait()
-        q, k, v, g = (buffer[i, :, b * GLANES : (b + 1) * GLANES] for i in range(4))
-
-        def selected(x):
-            return jnp.where(mask, dot_nn(pick, x), 0.0)
-
-        def folded(x):
-            x = x[:, :128] + x[:, 128:]
-            return x + swap_halves(x)
-
-        qs, ks, vs, gs = selected(q), selected(k), selected(v), selected(g)
-        qb, gb = qs.astype(BF16), gs.astype(BF16)
-        allowed = iota((GSLOTS, ROWS), 1) <= row
-        scores = jnp.where(allowed, dot_nt(qb, k) * SCALE, LOW)
-        grads = dot_nt(gb, v)
-        top, total, grad_total = softmax_terms(scores, allowed, grads)
-        used = slot <= FAR_SLOT
-        total = jnp.where(used, total, 1.0)
-        lse = jnp.where(used, top + jnp.log(total), 0.0)
-        stats = pack_stats(lse, jnp.where(used, grad_total / total, 0.0))
-        lane = iota((GSLOTS, 128), 1)
+    lane = iota((GSLOTS, 128), 1)
+    slot = iota((GSLOTS, 1), 0) % SLOTS
+
+    def columns(i, b):
+        return buffer[i, :, b * GLANES : (b + 1) * GLANES]
+
+    def selected(i):
+        copies[i].wait()
+        return [jnp.where(mask, dot_nn(picks[b], columns(i, b)), 0.0) for b in groups]
+
+    def folded(x):
+        x = x[:, :128] + x[:, 128:]
+        return x + swap_halves(x)
+
+    qs, gs, ks = selected(0), selected(1), selected(2)
+    scores = [dot_nt(qs[b].astype(BF16), columns(2, b)) * SCALE for b in groups]
+    vs = selected(3)
+    grads = [dot_nt(gs[b].astype(BF16), columns(3, b)) for b in groups]
+    for b in groups:
+        lse, d, _, _ = slot_stats(scores[b], rows[b], grads[b], slot <= FAR_SLOT)
+        stats = pack_stats(lse, d)
         near, far = group_offsets(near_ref, far_ref, b * GROUP)
         stats = jnp.where(lane == NEAR_LANE, near, jnp.where(lane == FAR_LANE, far, stats))
-        low_half = iota((GSLOTS, 128), 1) < FEAT
-        qk = jnp.where(low_half, folded(qs), folded(ks))
-        vg = jnp.where(low_half, folded(vs), folded(gs))
+        qk = jnp.where(lane < FEAT, folded(qs[b]), folded(ks[b]))
+        vg = jnp.where(lane < FEAT, folded(vs[b]), folded(gs[b]))
         qk = jnp.where(slot == STAT_SLOT, stats, qk)
         block = jnp.concatenate(
             [qk.reshape(GROUP, SLOTS, 128), vg.reshape(GROUP, SLOTS, 128)], axis=1
@@ -235,86 +248,143 @@
     )(*pinned(pltpu.HBM, near, far, q, k, v, g))
 
 
+def local_head(head, here, near_ref, far_ref, q, k, v, g):
+    half = ROWS // 2
+    query = iota((1, ROWS), 1)
+    zero = jnp.zeros((), BF16)
+    special = (query % NEAR_RATE == near_ref[head]) | (query == far_ref[head])
+    kh, vh, qh, gh = (jnp.where(here, x, zero) for x in (k, v, q, g))
+    triangle = iota((half, half), 0) <= iota((half, half), 1)
+    top, bottom = dot_nt(kh[:half], q), dot_nt(kh[half:], q[half:])
+    early, late = jnp.where(triangle, top[:, :half], LOW), top[:, half:]
+    bottom = jnp.where(triangle, bottom, LOW)
+    early_top = jnp.max(early, axis=0, keepdims=True)
+    late_top = jnp.maximum(jnp.max(late, axis=0, keepdims=True), jnp.max(bottom, axis=0, keepdims=True))
+    early, late, bottom = jnp.exp(early - early_top), jnp.exp(late - late_top), jnp.exp(bottom - late_top)
+    early_total = jnp.sum(early, axis=0, keepdims=True)
+    late_total = jnp.sum(late, axis=0, keepdims=True) + jnp.sum(bottom, axis=0, keepdims=True)
+    scale = jnp.where(special, 0.0, 1.0 / jnp.concatenate([early_total, late_total], axis=1))
+    grads, grads_b = dot_nt(vh[:half], g), dot_nt(vh[half:], g[half:])
+    top = jnp.concatenate([early, late], axis=1) * scale
+    bottom = bottom * scale[:, half:]
+    delta = jnp.sum(top * grads, axis=0, keepdims=True)
+    late_delta = delta[:, half:] + jnp.sum(bottom * grads_b, axis=0, keepdims=True)
+    delta = jnp.concatenate([delta[:, :half], late_delta], axis=1)
+    blank = jnp.zeros((half, half), BF16)
+
+    def square(top, bottom):
+        bottom = jnp.concatenate([blank, bottom.astype(BF16)], axis=1)
+        return jnp.concatenate([top.astype(BF16), bottom], axis=0)
+
+    dscores = square(top * (grads - delta), bottom * (grads_b - late_delta))
+    return square(top, bottom), dscores, qh, kh, vh, gh
+
+
+def joined(heads):
+    weights, dscores, q, k, v, g = zip(*heads)
+    over_keys = jnp.concatenate(weights, axis=0), jnp.concatenate(dscores, axis=0)
+    over_queries = jnp.concatenate(weights, axis=1), jnp.concatenate(dscores, axis=1)
+    out = dot_tn(over_keys[0], jnp.concatenate(v, axis=0))
+    dq = dot_tn(over_keys[1], jnp.concatenate(k, axis=0)) * SCALE
+    dk = dot_nn(over_queries[1], jnp.concatenate(q, axis=0))
+    return out, dq, dk, dot_nn(over_queries[0], jnp.concatenate(g, axis=0))
+
+
 def local_group(near_ref, far_ref, first, q, k, v, g):
-    lane = iota((1, GLANES), 1)
+    half = ROWS // 2
     query = iota((1, ROWS), 1)
-    allowed = iota((ROWS, ROWS), 0) <= iota((ROWS, ROWS), 1)
     q = (q.astype(F32) * SCALE).astype(BF16)
-    row_of = iota((GLANES, 1), 0)
-    kt, vt = jnp.transpose(k), jnp.transpose(v)
     zero = jnp.zeros((), BF16)
-    out_t = jnp.zeros((GLANES, ROWS), F32)
-    dq_t = jnp.zeros((GLANES, ROWS), F32)
-    dk = jnp.zeros((ROWS, GLANES), F32)
-    dv = jnp.zeros((ROWS, GLANES), F32)
-    for h in range(GROUP):
-        near, far = near_ref[first + h], far_ref[first + h]
-        special = (query % NEAR_RATE == near) | (query == far)
-        here = lane // FEAT == h
-        here_t = row_of // FEAT == h
-        scores = jnp.where(allowed, dot_nt(jnp.where(here, k, zero), q), LOW)
-        grads = dot_nt(jnp.where(here, v, zero), g)
-        weights = jnp.exp(scores - jnp.max(scores, axis=0, keepdims=True))
-        total = jnp.sum(weights, axis=0, keepdims=True)
-        weights = weights * jnp.where(special, 0.0, 1.0 / total)
-        delta = jnp.sum(weights * grads, axis=0, keepdims=True)
-        dscores = (weights * (grads - delta)).astype(BF16)
-        weights = weights.astype(BF16)
-        out_t += dot_nn(jnp.where(here_t, vt, zero), weights)
-        dq_t += dot_nn(jnp.where(here_t, kt, zero), dscores)
-        dk += dot_nn(dscores, jnp.where(here, q, zero))
-        dv += dot_nn(weights, jnp.where(here, g, zero))
-    return jnp.transpose(out_t), jnp.transpose(dq_t) * SCALE, dk, dv
+    triangle = iota((half, half), 0) <= iota((half, half), 1)
+    blank = jnp.zeros((half, half), BF16)
+    lane = iota((1, GLANES), 1) // FEAT
+    heads = [local_head(first + h, lane == h, near_ref, far_ref, q, k, v, g) for h in range(GROUP)]
+    return joined(heads)
+
+
+def slot_part(i, count=1):
+    return slice(i * GSLOTS, (i + count) * GSLOTS)
 
 
 def local_kernel(
-    base, count, near_in, far_in, q_ref, k_ref, v_ref, g_ref,
-    query_ref, key_ref, near_ref, far_ref, offset_sems, buffer, sems
+    base, count, near_in, far_in, q_ref, k_ref, v_ref, g_ref, query_ref, key_ref, slot_ref,
+    near_ref, far_ref, offset_sems, buffer, sems, *query_scratch
 ):
     offset_copies = start_offsets(near_in, far_in, near_ref, far_ref, offset_sems)
     start_copies((q_ref, k_ref, v_ref, g_ref), base, count, buffer, sems)
     for copy in offset_copies:
         copy.wait()
+    mask = head_mask()
+
+    query_buffer = query_scratch[0] if query_scratch else query_ref
+
+    def query_copy(b):
+        _, query_sems = query_scratch
+        here = pl.ds(pl.multiple_of(b * GLANES, GLANES), GLANES)
+        return pltpu.make_async_copy(query_buffer.at[:, :, here], query_ref.at[:, :, here], query_sems.at[b])
 
     def one_group(b, carry):
         here = pl.ds(pl.multiple_of(b * GLANES, GLANES), GLANES)
         for i, source in enumerate((q_ref, k_ref, v_ref, g_ref)):
             there = pl.ds(pl.multiple_of((base + b) * GLANES, GLANES), GLANES)
             pltpu.make_async_copy(source.at[:, there], buffer.at[i, :, here], sems.at[b, i]).wait()
-        arrays = tuple(buffer[i, :, here] for i in range(4))
-        row, _, _ = slot_rows(near_ref, far_ref, (base + b) * GROUP)
-        pick = jnp.where(iota((GSLOTS, ROWS), 1) == row, 1.0, 0.0).astype(BF16)
-        mask = head_mask()
-        qs = jnp.where(mask, dot_nn(pick, arrays[0]), 0.0)
-        gs = jnp.where(mask, dot_nn(pick, arrays[3]), 0.0)
-        scores = dot_nt(qs.astype(BF16), arrays[1]) * SCALE
-        scores = jnp.where(iota((GSLOTS, ROWS), 1) <= row, scores, LOW)
-        slots = (scores, dot_nt(gs.astype(BF16), arrays[2]), qs * SCALE, gs)
-        key_ref[2 * ROWS :, here] = jnp.concatenate(slots, axis=0)
-        out, dq, dk, dv = local_group(near_ref, far_ref, (base + b) * GROUP, *arrays)
-        query_ref[0, :, here] = out.astype(BF16)
-        query_ref[1, :, here] = dq.astype(BF16)
+        q, k, v, g = (buffer[i, :, here] for i in range(4))
+        first = (base + b) * GROUP
+        row, repeat, slot = slot_rows(near_ref, far_ref, first)
+        pick = pick_matrix(row)
+        qs = jnp.where(mask, dot_nn(pick, q), 0.0)
+        gs = jnp.where(mask, dot_nn(pick, g), 0.0)
+        live = (slot <= FAR_SLOT) & ~repeat
+        scores = dot_nt(qs.astype(BF16), k) * SCALE
+        grads = dot_nt(gs.astype(BF16), v)
+        lse, d, weights, grads = slot_stats(scores, row, grads, live)
+        dscores = (weights * grads).astype(BF16)
+        weights = weights.astype(BF16)
+        lane = iota((GSLOTS, GLANES), 1)
+        parts = (
+            weights,
+            dscores,
+            pick,
+            (qs * SCALE).astype(BF16),
+            gs.astype(BF16),
+            jnp.where(mask, dot_nn(weights, v), 0.0).astype(BF16),
+            (jnp.where(mask, dot_nn(dscores, k), 0.0) * SCALE).astype(BF16),
+            (jnp.where(mask, dot_nn(weights, k), 0.0) * SCALE).astype(BF16),
+        )
+        for i, part in enumerate(parts):
+            slot_ref[slot_part(i), here] = part
+        key_ref[2 * ROWS :, here] = jnp.where(lane == 0, jnp.where(live, lse, LOW), d)
+        out, dq, dk, dv = local_group(near_ref, far_ref, first, q, k, v, g)
+        query_buffer[0, :, here] = out.astype(BF16)
+        query_buffer[1, :, here] = dq.astype(BF16)
+        if query_scratch:
+            query_copy(b).start()
         key_ref[:ROWS, here] = dk
         key_ref[ROWS : 2 * ROWS, here] = dv
         return carry
 
     lax.fori_loop(0, count, one_group, 0)
-
-
-def local_call(base, count, near, far, q, k, v, g):
+    if query_scratch:
+        for b in range(count):
+            query_copy(b).wait()
+
+
+def local_call(base, count, near, far, q, k, v, g, keep):
     hbm = pl.BlockSpec(memory_space=pltpu.HBM)
     vmem = pl.BlockSpec(memory_space=pltpu.VMEM)
     shape = (ROWS, count * GLANES)
     return pl.pallas_call(
         functools.partial(local_kernel, base, count),
         in_specs=[hbm] * 6,
-        out_specs=[vmem] * 2,
+        out_specs=[vmem if keep else hbm, vmem, vmem],
         out_shape=[
-            pltpu.VMEM((2,) + shape, BF16),
-            pltpu.VMEM((2 * ROWS + 4 * GSLOTS, count * GLANES), F32),
+            (pltpu.VMEM if keep else pltpu.HBM)((2,) + shape, BF16),
+            pltpu.VMEM((2 * ROWS + GSLOTS, count * GLANES), F32),
+            pltpu.VMEM((SLOT_PARTS * GSLOTS, count * GLANES), BF16),
         ],
         scratch_shapes=OFFSET_SCRATCH
-        + [pltpu.VMEM((4,) + shape, BF16), pltpu.SemaphoreType.DMA((count, 4))],
+        + [pltpu.VMEM((4,) + shape, BF16), pltpu.SemaphoreType.DMA((count, 4))]
+        + ([] if keep else [pltpu.VMEM((2,) + shape, BF16), pltpu.SemaphoreType.DMA((count,))]),
         compiler_params=pltpu.CompilerParams(vmem_limit_bytes=VMEM_BYTES),
         cost_estimate=pl.CostEstimate(
             flops=count * GROUP * 14 * ROWS * ROWS * FEAT,
@@ -461,17 +531,15 @@
     )(got, stats, far_got)
 
 
-def finish_kernel(
-    near_in, far_in, got_ref, k_ref, v_ref, *refs
-):
-    parts, outs = (refs[:2], refs[2:4]), refs[4:8]
-    near_ref, far_ref, offset_sems, buffer, sems, results, out_sems = refs[8:]
-    offset_copies = start_offsets(near_in, far_in, near_ref, far_ref, offset_sems)
-    copies = start_whole((k_ref, v_ref), buffer, sems)
-    for copy in offset_copies:
-        copy.wait()
+def finish_kernel(got_ref, *refs):
+    early, keys, slots, late = refs[0], (refs[1], refs[4]), (refs[2], refs[5]), refs[3]
+    outs, (held, held_sem, results, out_sems) = refs[6:10], refs[10:]
+    early_copy = pltpu.make_async_copy(early, held, held_sem)
+    early_copy.start()
     mask = head_mask()
     low = iota((GSLOTS, 128), 1) < FEAT
+    used = iota((GSLOTS, 128), 0) % SLOTS <= FAR_SLOT
+    zero = jnp.zeros((GSLOTS, GLANES), F32)
     sends = []
 
     def finished(i, b, value):
@@ -481,75 +549,69 @@
         send.start()
         sends.append(send)
 
-    held = []
+    def spread(x, keep_low):
+        x = jnp.where(used & (low if keep_low else ~low), x, 0.0)
+        x = x + swap_halves(x)
+        return jnp.where(mask, jnp.concatenate([x, x], axis=1), 0.0)
+
+    picked = []
     for b in range(GROUPS):
-        row, repeat, slot = slot_rows(near_ref, far_ref, b * GROUP)
-        pick = jnp.where(iota((GSLOTS, ROWS), 1) == row, 1.0, 0.0).astype(BF16)
         got = got_ref[b * GROUP : (b + 1) * GROUP].astype(F32)
         lse, delta = unpack_stats(got)
-        used = slot <= FAR_SLOT
-
-        def spread(x, keep_low):
-            x = jnp.where(used & (low if keep_low else ~low), x, 0.0)
-            x = x + swap_halves(x)
-            return jnp.where(mask, jnp.concatenate([x, x], axis=1), 0.0)
-
         first = got[:, :SLOTS].reshape(GSLOTS, 128)
         second = got[:, SLOTS:].reshape(GSLOTS, 128)
         half, at = divmod(b, GROUPS // 2)
         there = slice(at * GLANES, (at + 1) * GLANES)
-        query_part, key_part = parts[half]
-        scores, grads, qs, gs = (
-            key_part[2 * ROWS + i * GSLOTS : 2 * ROWS + (i + 1) * GSLOTS, there] for i in range(4)
+        key_part, slot_ref = keys[half], slots[half]
+        qs, gs, out, dq, mean = (slot_ref[slot_part(i), there].astype(F32) for i in range(3, 8))
+        stats = key_part[2 * ROWS :, there]
+        factor = jnp.exp(stats[:, :1] - lse)
+        shift = factor * (stats[:, 1:2] - delta)
+        left = slot_ref[slot_part(0, 3), there]
+        right = jnp.concatenate(
+            [
+                jnp.concatenate([shift * qs, factor * qs, spread(second, True)], axis=0),
+                jnp.concatenate([factor * gs, zero, spread(second, False)], axis=0),
+            ],
+            axis=1,
         )
-        weights = jnp.where(repeat, 0.0, jnp.exp(scores - lse))
-        dscores = (weights * (grads - delta)).astype(BF16)
-        weights = weights.astype(BF16)
-
-        def key_side(slots, rows, extra):
-            left = jnp.concatenate([slots, pick], axis=0)
-            right = jnp.concatenate([rows.astype(BF16), extra.astype(BF16)], axis=0)
-            return dot_tn(left, right)
-
-        finished(2, b, key_part[:ROWS, there] + key_side(dscores, qs, spread(second, True)))
-        finished(
-            3, b, key_part[ROWS : 2 * ROWS, there] + key_side(weights, gs, spread(second, False))
-        )
-        held.append((pick, weights, dscores, spread(first, True), spread(first, False)))
-    for copy in copies:
-        copy.wait()
-    for b in range(GROUPS):
-        here = slice(b * GLANES, (b + 1) * GLANES)
-        pick, weights, dscores, out, dq = held[b]
+        sums = dot_tn(left, right.astype(BF16))
+        finished(2, b, key_part[:ROWS, there] + sums[:, :GLANES])
+        finished(3, b, key_part[ROWS : 2 * ROWS, there] + sums[:, GLANES:])
+        out = factor * out + spread(first, True)
+        dq = factor * dq + shift * mean + spread(first, False)
+        right = jnp.concatenate([out, dq], axis=1).astype(BF16)
+        picked.append((left[2 * GSLOTS :], right))
+    for b in (2, 3, 0, 1):
         half, at = divmod(b, GROUPS // 2)
         there = slice(at * GLANES, (at + 1) * GLANES)
-        query_part = parts[half][0]
-        out += jnp.where(mask, dot_nn(weights, buffer[1, :, here]), 0.0)
-        dq += jnp.where(mask, dot_nn(dscores, buffer[0, :, here]), 0.0) * SCALE
-        finished(0, b, query_part[0, :, there].astype(F32) + dot_tn(pick, out.astype(BF16)))
-        finished(1, b, query_part[1, :, there].astype(F32) + dot_tn(pick, dq.astype(BF16)))
+        if b == 0:
+            early_copy.wait()
+        query_part = late if half else held
+        sums = dot_tn(*picked[b])
+        finished(0, b, query_part[0, :, there].astype(F32) + sums[:, :GLANES])
+        finished(1, b, query_part[1, :, there].astype(F32) + sums[:, GLANES:])
     for send in sends:
         send.wait()
 
 
-def finish_call(near, far, got, k, v, parts):
+def finish_call(got, parts):
     hbm = pl.BlockSpec(memory_space=pltpu.HBM)
     vmem = pl.BlockSpec(memory_space=pltpu.VMEM)
     return pl.pallas_call(
         finish_kernel,
-        in_specs=[hbm, hbm, vmem, hbm, hbm] + [vmem] * 4,
+        in_specs=[vmem, hbm] + [vmem] * 5,
         out_specs=[hbm] * 4,
         out_shape=[jax.ShapeDtypeStruct((ROWS, WIDTH), BF16)] * 4,
-        scratch_shapes=OFFSET_SCRATCH
-        + [
-            pltpu.VMEM((2, ROWS, WIDTH), BF16),
-            pltpu.SemaphoreType.DMA((2,)),
+        scratch_shapes=[
+            pltpu.VMEM((2, ROWS, WIDTH // 2), BF16),
+            pltpu.SemaphoreType.DMA,
             pltpu.VMEM((4, ROWS, WIDTH), BF16),
             pltpu.SemaphoreType.DMA((GROUPS, 4)),
         ],
         compiler_params=pltpu.CompilerParams(vmem_limit_bytes=VMEM_BYTES),
         name="finish_rows",
-    )(*pinned(pltpu.HBM, near, far), got, *pinned(pltpu.HBM, k, v), *pinned(pltpu.VMEM, *parts))
+    )(got, *pinned(pltpu.HBM, parts[0]), *parts[1:])
 
 
 def exchange(x, axis):
@@ -562,15 +624,15 @@
     pay = select_call(near_offsets, far_offsets, *arrays)
     got = exchange(pay.reshape(SEQ, 2 * SLOTS, 128), "seq")
     (near_1, far_1), _ = lax.optimization_barrier(((near_offsets, far_offsets), pay))
-    parts = tuple(local_call(0, half, near_1, far_1, *arrays))
+    parts = tuple(local_call(0, half, near_1, far_1, *arrays, False))
     got, parts = lax.optimization_barrier((got, parts))
     far_pay, stats = near_call(got)
     far_got = exchange(far_pay, "outer")
     back = owner_call(got, stats, far_got)
     (near_2, far_2), back = lax.optimization_barrier(((near_offsets, far_offsets), back))
     back_got = exchange(back, "seq")
-    parts += tuple(local_call(half, GROUPS - half, near_2, far_2, *arrays))
-    return finish_call(near_offsets, far_offsets, back_got, keys, values, parts)
+    parts += tuple(local_call(half, GROUPS - half, near_2, far_2, *arrays, True))
+    return finish_call(back_got, parts)
 
 
 def solution(mesh):

time: 58.8 us -> 57.2 us (0.973)
  local copies, waits for them, and re-layouts: 1.83 us -> 0 us
  waiting for transfers between devices: 7.66 us -> 9.2 us
  Pallas kernels: 19.9 us -> 18.8 us
    unnamed x4 -> x0, local copies, waits for them, and re-layouts: 1.83 us -> none
    all_to_all x2, waiting for transfers between devices: 7.66 us -> 9.2 us  [exchange(): return lax.all_to_all(x, axis, split_axis=0, concat_axis=0, tiled=True)]
    pallas_call x2, Pallas kernels: 10.3 us -> 9.54 us  [local_call(): pl.pallas_call(functools.partial(local_kernel, base, count), in_specs=[hb...]
  transfers between devices with their start and end apart: 2 -> 2, of which waited for: 2 -> 2; matrix products, arithmetic and copies ran while one was open for 0% -> 0% of each run, Pallas kernels for 18% -> 17%
where the time goes in v3:
time: 57.2 us; the launch traced here: 56.9 us
  Pallas kernels  18.8 us (33%)
  starting transfers between devices  15.9 us (28%)
  blocking collectives  12.2 us (21%)
  waiting for transfers between devices  9.2 us (16%)
  between operations  0.68 us (1%)
    all_to_all x2, starting transfers between devices, exchange(): return lax.all_to_all(x, axis, split_axis=0, concat_axis=0, tiled=True)  15.9 us
    all_to_all x1, blocking collectives, exchange(): return lax.all_to_all(x, axis, split_axis=0, concat_axis=0, tiled=True)  12.2 us
    pallas_call x2, Pallas kernels, local_call(): pl.pallas_call(functools.partial(local_kernel, base, count), in_specs=[hb...  9.54 us
    all_to_all x2, waiting for transfers between devices, exchange(): return lax.all_to_all(x, axis, split_axis=0, concat_axis=0, tiled=True)  9.2 us
    pallas_call x1, Pallas kernels, finish_call(): pl.pallas_call(finish_kernel, in_specs=[vmem, hbm] + [vmem] * 5, out_spec...  3.33 us
    pallas_call x1, Pallas kernels, select_call(): pl.pallas_call(select_kernel, in_specs=[hbm] * 6, out_specs=vmem, out_sha...  3.01 us
    pallas_call x1, Pallas kernels, owner_call(): pl.pallas_call(owner_kernel, in_specs=[vmem, vmem, vmem], out_specs=vmem,...  2.22 us
  transfers between devices with their start and end apart: 2, of which 2 were waited for; matrix products, arithmetic and copies ran while one was open for 0% of the time, Pallas kernels for 17%

profile of v3, /device:TPU:1, one launch (start us, length us, event | category | flops | bytes accessed | tf_op | source)
XLA Modules:
  0.0 56.9 jit_solution(7350276751378687829)
XLA Ops:
  0.6 3.0 %select_rows.1 = bf16[2,16,16,128]{3,2,1,0:T(8,128)(2,1)} custom-call(s32[16]{0:T(128)} %near_in.3, s32[16]{0:T(128)} %far_in.3, bf16[256,1024]{1,0:T(8,128)(2,1)} %q_ref.5, bf16[256,1024]{1,0:T(8,128)(2,1)} %k_ref.5, bf16[256,1024]{1,0:T(8,128)(2,1)} %v_ref.5, bf16[256,1024]{1,0:T(8,128)(2,1)} %g_ref.5), custom_call_target="tpu_custom_call" | custom-call | tf_op jit(solution)/shard_map/select_rows/pallas_call | solution.py:239
  3.6 11.9 %all-to-all-start = ((bf16[32,16,128]{2,1,0:T(8,128)(2,1)}), bf16[32,16,128]{2,1,0:T(8,128)(2,1)S(1)}, u32[]{:S(2)}, u32[]{:S(2)}) async-start(bf16[32,16,128]{2,1,0:T(8,128)(2,1)} %bitcast), calls=%async_computation | async-start | bytes 262144 | tf_op jit(solution)/shard_map/all_to_all | solution.py:618
  15.5 5.0 %local_level.2 = (bf16[2,256,512]{2,1,0:T(8,128)(2,1)}, f32[544,512]{1,0:T(8,128)S(1)}, bf16[256,512]{1,0:T(8,128)(2,1)S(1)}) custom-call(s32[16]{0:T(128)} %near_in.3, s32[16]{0:T(128)} %far_in.3, bf16[256,1024]{1,0:T(8,128)(2,1)} %q_ref.5, bf16[256,1024]{1,0:T(8,128)(2,1)} %k_ref.5, bf16[256,1024]{1,0:T(8,128)(2,1)} %v_ref.5, bf16[256,1024]{1,0:T(8,128)(2,1)} %g_ref.5), custom_call_target="tpu_custom_call" | custom-call | flops 469762048 | bytes 1835008 | tf_op jit(solution)/shard_map/local_level/pallas_call | solution.py:376
  20.5 4.3 %all-to-all-done.got_ref = bf16[32,16,128]{2,1,0:T(8,128)(2,1)S(1)} async-done(((bf16[32,16,128]{2,1,0:T(8,128)(2,1)}), bf16[32,16,128]{2,1,0:T(8,128)(2,1)S(1)}, u32[]{:S(2)}, u32[]{:S(2)}) %all-to-all-start) | async-done | bytes 131104 | tf_op jit(solution)/shard_map/all_to_all | solution.py:618
  24.9 0.7 %near_forward.1 = (bf16[8,96,128]{2,1,0:T(8,128)(2,1)S(1)}, f32[256,128]{1,0:T(8,128)S(1)}) custom-call(bf16[32,16,128]{2,1,0:T(8,128)(2,1)S(1)} %all-to-all-done.got_ref), custom_call_target="tpu_custom_call" | custom-call | tf_op jit(solution)/shard_map/near_forward/pallas_call | solution.py:449
  25.6 12.2 %all_to_all.15.far_got_ref = bf16[8,96,128]{2,1,0:T(8,128)(2,1)S(1)} all-to-all(bf16[8,96,128]{2,1,0:T(8,128)(2,1)S(1)} %get-tuple-element.28), channel_id=1, replica_groups=mesh['seq'=32,'outer'=8] {'outer'}, dimensions={0} | all-to-all | bytes 393216 | tf_op jit(solution)/shard_map/all_to_all | solution.py:618
  37.8 2.2 %owner_level.1 = bf16[32,16,128]{2,1,0:T(8,128)(2,1)} custom-call(bf16[32,16,128]{2,1,0:T(8,128)(2,1)S(1)} %all-to-all-done.got_ref, f32[256,128]{1,0:T(8,128)S(1)} %get-tuple-element.27.stat_ref, bf16[8,96,128]{2,1,0:T(8,128)(2,1)S(1)} %all_to_all.15.far_got_ref), custom_call_target="tpu_custom_call" | custom-call | tf_op jit(solution)/shard_map/owner_level/pallas_call | solution.py:524
  40.0 4.1 %all-to-all-start.2 = ((bf16[32,16,128]{2,1,0:T(8,128)(2,1)}), bf16[32,16,128]{2,1,0:T(8,128)(2,1)S(1)}, u32[]{:S(2)}, u32[]{:S(2)}) async-start(bf16[32,16,128]{2,1,0:T(8,128)(2,1)} %owner_level.1), calls=%async_computation.2 | async-start | bytes 262144 | tf_op jit(solution)/shard_map/all_to_all | solution.py:618
  44.1 4.5 %local_level.3 = (bf16[2,256,512]{2,1,0:T(8,128)(2,1)S(1)}, f32[544,512]{1,0:T(8,128)S(1)}, bf16[256,512]{1,0:T(8,128)(2,1)S(1)}) custom-call(s32[16]{0:T(128)} %near_in.3, s32[16]{0:T(128)} %far_in.3, bf16[256,1024]{1,0:T(8,128)(2,1)} %q_ref.5, bf16[256,1024]{1,0:T(8,128)(2,1)} %k_ref.5, bf16[256,1024]{1,0:T(8,128)(2,1)} %v_ref.5, bf16[256,1024]{1,0:T(8,128)(2,1)} %g_ref.5), custom_call_target="tpu_custom_call" | custom-call | flops 469762048 | bytes 1835008 | tf_op jit(solution)/shard_map/local_level/pallas_call | solution.py:376
  48.7 4.9 %all-to-all-done.2.got_ref = bf16[32,16,128]{2,1,0:T(8,128)(2,1)S(1)} async-done(((bf16[32,16,128]{2,1,0:T(8,128)(2,1)}), bf16[32,16,128]{2,1,0:T(8,128)(2,1)S(1)}, u32[]{:S(2)}, u32[]{:S(2)}) %all-to-all-start.2) | async-done | bytes 131104 | tf_op jit(solution)/shard_map/all_to_all | solution.py:618
  53.5 3.3 %finish_rows.1 = (bf16[256,1024]{1,0:T(8,128)(2,1)}, bf16[256,1024]{1,0:T(8,128)(2,1)}, bf16[256,1024]{1,0:T(8,128)(2,1)}, bf16[256,1024]{1,0:T(8,128)(2,1)}) custom-call(bf16[32,16,128]{2,1,0:T(8,128)(2,1)S(1)} %all-to-all-done.2.got_ref, bf16[2,256,512]{2,1,0:T(8,128)(2,1)} %get-tuple-element.30.refs_0_, f32[544,512]{1,0:T(8,128)S(1)} %get-tuple-element.31.refs_1_, ...), custom_call_target="tpu_custom_call" | custom-call | tf_op jit(solution)/shard_map/finish_rows/pallas_call | solution.py:601
Async XLA Ops:
  3.6 21.2 %all-to-all-start = ((bf16[32,16,128]{2,1,0:T(8,128)(2,1)}), bf16[32,16,128]{2,1,0:T(8,128)(2,1)S(1)}, u32[]{:S(2)}, u32[]{:S(2)}) async-start(bf16[32,16,128]{2,1,0:T(8,128)(2,1)} %bitcast), calls=%async_computation | async-start | bytes 262144 | tf_op jit(solution)/shard_map/all_to_all | solution.py:618
  40.0 13.5 %all-to-all-start.2 = ((bf16[32,16,128]{2,1,0:T(8,128)(2,1)}), bf16[32,16,128]{2,1,0:T(8,128)(2,1)S(1)}, u32[]{:S(2)}, u32[]{:S(2)}) async-start(bf16[32,16,128]{2,1,0:T(8,128)(2,1)} %owner_level.1), calls=%async_computation.2 | async-start | bytes 262144 | tf_op jit(solution)/shard_map/all_to_all | solution.py:618

commit v4 on v3

--- a/solution.py
+++ b/solution.py
@@ -20,13 +20,15 @@
 STAT_SLOT = 5
 NEAR_LANE = 48
 FAR_LANE = 49
+COPY_LANE = 50
 GROUP = 4
 GROUPS = HEADS // GROUP
 GLANES = GROUP * FEAT
 GSLOTS = GROUP * SLOTS
 SCALE = FEAT**-0.5
 LOW = -1e30
-SLOT_PARTS = 8
+SLOT_PARTS = 5
+TERMS = 4 * GSLOTS
 F32 = jnp.float32
 BF16 = jnp.bfloat16
 VMEM_BYTES = 24 * 1024 * 1024
@@ -81,10 +83,9 @@
     return jnp.broadcast_to(total, spread.shape).reshape(rows, 128)
 
 
-def unpack_stats(block):
-    groups = block.shape[0]
-    lanes = jnp.broadcast_to(block[:, STAT_SLOT : STAT_SLOT + 1, :], (groups, SLOTS, 128))
-    lanes = lanes.reshape(groups * SLOTS, 128)
+def unpack_stats(block, at=STAT_SLOT):
+    lanes = jnp.broadcast_to(block[:, at : at + 1, :], (block.shape[0], SLOTS, 128))
+    lanes = lanes.reshape(block.shape[0] * SLOTS, 128)
     row, lane = iota(lanes.shape, 0), iota(lanes.shape, 1)
     return read_parts(lanes, jnp.where(lane // 8 == row % SLOTS, lane % 8, -1))
 
@@ -230,7 +231,8 @@
             [qk.reshape(GROUP, SLOTS, 128), vg.reshape(GROUP, SLOTS, 128)], axis=1
         ).astype(BF16)
         pay_ref[0, b * GROUP : (b + 1) * GROUP] = block
-        pay_ref[1, b * GROUP : (b + 1) * GROUP] = block
+        mark = (iota(block.shape, 1) == STAT_SLOT) & (iota(block.shape, 2) == COPY_LANE)
+        pay_ref[1, b * GROUP : (b + 1) * GROUP] = jnp.where(mark, jnp.ones((), BF16), block)
 
 
 def select_call(near, far, q, k, v, g):
@@ -307,21 +309,15 @@
 
 
 def local_kernel(
-    base, count, near_in, far_in, q_ref, k_ref, v_ref, g_ref, query_ref, key_ref, slot_ref,
-    near_ref, far_ref, offset_sems, buffer, sems, *query_scratch
+    base, count, near_in, far_in, q_ref, k_ref, v_ref, g_ref, query_ref, key_ref, stat_ref, slot_ref,
+    left_ref, place_ref, near_ref, far_ref, offset_sems, buffer, sems
 ):
+    place_ref[...] = jnp.full(place_ref.shape, lax.axis_index("outer") * SEQ, jnp.int32)
     offset_copies = start_offsets(near_in, far_in, near_ref, far_ref, offset_sems)
     start_copies((q_ref, k_ref, v_ref, g_ref), base, count, buffer, sems)
     for copy in offset_copies:
         copy.wait()
     mask = head_mask()
-
-    query_buffer = query_scratch[0] if query_scratch else query_ref
-
-    def query_copy(b):
-        _, query_sems = query_scratch
-        here = pl.ds(pl.multiple_of(b * GLANES, GLANES), GLANES)
-        return pltpu.make_async_copy(query_buffer.at[:, :, here], query_ref.at[:, :, here], query_sems.at[b])
 
     def one_group(b, carry):
         here = pl.ds(pl.multiple_of(b * GLANES, GLANES), GLANES)
@@ -341,10 +337,12 @@
         dscores = (weights * grads).astype(BF16)
         weights = weights.astype(BF16)
         lane = iota((GSLOTS, GLANES), 1)
+        near, far = group_offsets(near_ref, far_ref, first)
+        key_row = jnp.where(slot >= FAR_SLOT, near + NEAR_RATE * (slot - FAR_SLOT), -1)
+        key_pick = pick_matrix(jnp.where(slot == 0, far, key_row))
+        left = jnp.concatenate([weights, dscores, pick, key_pick], axis=0)
+        left_ref[:, pl.ds(pl.multiple_of(b * TERMS, TERMS), TERMS)] = jnp.transpose(left)
         parts = (
-            weights,
-            dscores,
-            pick,
             (qs * SCALE).astype(BF16),
             gs.astype(BF16),
             jnp.where(mask, dot_nn(weights, v), 0.0).astype(BF16),
@@ -353,38 +351,35 @@
         )
         for i, part in enumerate(parts):
             slot_ref[slot_part(i), here] = part
-        key_ref[2 * ROWS :, here] = jnp.where(lane == 0, jnp.where(live, lse, LOW), d)
+        stat_ref[:, here] = jnp.where(lane == 0, jnp.where(live, lse, LOW), d)
         out, dq, dk, dv = local_group(near_ref, far_ref, first, q, k, v, g)
-        query_buffer[0, :, here] = out.astype(BF16)
-        query_buffer[1, :, here] = dq.astype(BF16)
-        if query_scratch:
-            query_copy(b).start()
-        key_ref[:ROWS, here] = dk
-        key_ref[ROWS : 2 * ROWS, here] = dv
+        query_ref[0, :, here] = out.astype(BF16)
+        query_ref[1, :, here] = dq.astype(BF16)
+        key_ref[0, :, here] = dk.astype(key_ref.dtype)
+        key_ref[1, :, here] = dv.astype(key_ref.dtype)
         return carry
 
     lax.fori_loop(0, count, one_group, 0)
-    if query_scratch:
-        for b in range(count):
-            query_copy(b).wait()
-
-
-def local_call(base, count, near, far, q, k, v, g, keep):
+
+
+def local_call(base, count, near, far, q, k, v, g, key_type):
     hbm = pl.BlockSpec(memory_space=pltpu.HBM)
     vmem = pl.BlockSpec(memory_space=pltpu.VMEM)
     shape = (ROWS, count * GLANES)
     return pl.pallas_call(
         functools.partial(local_kernel, base, count),
         in_specs=[hbm] * 6,
-        out_specs=[vmem if keep else hbm, vmem, vmem],
+        out_specs=[vmem] * 6,
         out_shape=[
-            (pltpu.VMEM if keep else pltpu.HBM)((2,) + shape, BF16),
-            pltpu.VMEM((2 * ROWS + GSLOTS, count * GLANES), F32),
+            pltpu.VMEM((2,) + shape, BF16),
+            pltpu.VMEM((2,) + shape, key_type),
+            pltpu.VMEM((GSLOTS, count * GLANES), F32),
             pltpu.VMEM((SLOT_PARTS * GSLOTS, count * GLANES), BF16),
+            pltpu.VMEM((ROWS, count * TERMS), BF16),
+            pltpu.VMEM((8, 128), jnp.int32),
         ],
         scratch_shapes=OFFSET_SCRATCH
-        + [pltpu.VMEM((4,) + shape, BF16), pltpu.SemaphoreType.DMA((count, 4))]
-        + ([] if keep else [pltpu.VMEM((2,) + shape, BF16), pltpu.SemaphoreType.DMA((count,))]),
+        + [pltpu.VMEM((4,) + shape, BF16), pltpu.SemaphoreType.DMA((count, 4))],
         compiler_params=pltpu.CompilerParams(vmem_limit_bytes=VMEM_BYTES),
         cost_estimate=pl.CostEstimate(
             flops=count * GROUP * 14 * ROWS * ROWS * FEAT,
@@ -419,12 +414,12 @@
 
 def read_offsets(got):
     line = got[0, STAT_SLOT : STAT_SLOT + 1, :].astype(jnp.int32)
-    return line[:, NEAR_LANE : NEAR_LANE + 1], line[:, FAR_LANE : FAR_LANE + 1]
+    return tuple(line[:, at : at + 1] for at in (NEAR_LANE, FAR_LANE, COPY_LANE))
 
 
 def near_kernel(got_ref, send_ref, stat_ref):
     got = got_ref[...].astype(F32)
-    near, far = read_offsets(got)
+    near, far, _ = read_offsets(got)
     qk, vg = got[:, :SLOTS].reshape(SEQ * SLOTS, 128), got[:, SLOTS:].reshape(SEQ * SLOTS, 128)
     lse, d = unpack_stats(got)
     q0, k0, v0, g0, _, _ = pair_halves(qk, vg)
@@ -470,10 +465,10 @@
     return query_side * jnp.where(low, 1.0, SCALE), key_side * jnp.where(low, SCALE, 1.0)
 
 
-def owner_kernel(got_ref, stat_ref, far_got_ref, send_ref):
-    segment = lax.axis_index("outer")
+def owner_kernel(place_ref, got_ref, stat_ref, far_got_ref, send_ref):
+    place = place_ref[:1, :1]
     got = got_ref[...].astype(F32)
-    near, far = read_offsets(got)
+    near, far, copy = read_offsets(got)
     rows = SEQ * SLOTS
     lane = iota((rows, 128), 1)
 
@@ -490,7 +485,7 @@
     own_stats = part_lanes(top + jnp.log(total), grad_total / total, lane).astype(BF16)
 
     row, column = iota((rows, rows), 0), iota((rows, rows), 1)
-    own = column == segment * SEQ + row // SLOTS
+    own = column == place + row // SLOTS
     to_far = jnp.where(own & (row % SLOTS == FAR_SLOT), 1.0, 0.0).astype(BF16)
     to_all = jnp.where(own, 1.0, 0.0).astype(BF16)
     first = dot_nn(to_far, query_side.astype(BF16))
@@ -513,86 +508,80 @@
     second += key_side
     used = slot <= FAR_SLOT
     stats = pack_stats(jnp.where(used, lse, 0.0), jnp.where(used, delta, 0.0))
-    first = jnp.where(slot == STAT_SLOT, stats, first)
-    send_ref[...] = jnp.concatenate(
-        [first.reshape(SEQ, SLOTS, 128), second.reshape(SEQ, SLOTS, 128)], axis=1
-    ).astype(BF16)
-
-
-def owner_call(got, stats, far_got):
+    near_block = jnp.where(slot < FAR_SLOT, first, pltpu.roll(second, FAR_SLOT, 0))
+    far_block = jnp.where(slot == 0, pltpu.roll(second, rows - FAR_SLOT, 0), stats)
+    far_block = jnp.where(slot == FAR_SLOT, first, far_block)
+    send_ref[...] = jnp.where(copy == 0, near_block, far_block).astype(BF16)
+
+
+def owner_call(place, got, stats, far_got):
     vmem = pl.BlockSpec(memory_space=pltpu.VMEM)
     return pl.pallas_call(
         owner_kernel,
-        in_specs=[vmem, vmem, vmem],
+        in_specs=[vmem, vmem, vmem, vmem],
         out_specs=vmem,
-        out_shape=pltpu.VMEM((SEQ, 2 * SLOTS, 128), BF16),
+        out_shape=pltpu.VMEM((SEQ * SLOTS, 128), BF16),
         compiler_params=pltpu.CompilerParams(vmem_limit_bytes=VMEM_BYTES),
         name="owner_level",
-    )(got, stats, far_got)
+    )(place, got, stats, far_got)
 
 
 def finish_kernel(got_ref, *refs):
-    early, keys, slots, late = refs[0], (refs[1], refs[4]), (refs[2], refs[5]), refs[3]
-    outs, (held, held_sem, results, out_sems) = refs[6:10], refs[10:]
-    early_copy = pltpu.make_async_copy(early, held, held_sem)
-    early_copy.start()
+    halves, outs, (results, out_sems) = (refs[:5], refs[5:10]), refs[10:14], refs[14:]
     mask = head_mask()
     low = iota((GSLOTS, 128), 1) < FEAT
-    used = iota((GSLOTS, 128), 0) % SLOTS <= FAR_SLOT
+    slot = iota((GSLOTS, 128), 0) % SLOTS
     zero = jnp.zeros((GSLOTS, GLANES), F32)
     sends = []
 
     def finished(i, b, value):
-        here = slice(b * GLANES, (b + 1) * GLANES)
-        results[i, :, here] = value.astype(BF16)
-        send = pltpu.make_async_copy(results.at[i, :, here], outs[i].at[:, here], out_sems.at[b, i])
-        send.start()
-        sends.append(send)
-
-    def spread(x, keep_low):
-        x = jnp.where(used & (low if keep_low else ~low), x, 0.0)
-        x = x + swap_halves(x)
-        return jnp.where(mask, jnp.concatenate([x, x], axis=1), 0.0)
-
-    picked = []
+        results[i, :, b * GLANES : (b + 1) * GLANES] = value.astype(BF16)
+
+    def send(arrays, first, count):
+        here = slice(first * GLANES, (first + count) * GLANES)
+        for i in arrays:
+            copy = pltpu.make_async_copy(
+                results.at[i, :, here], outs[i].at[:, here], out_sems.at[first, i]
+            )
+            copy.start()
+            sends.append(copy)
+
+    def spread(x):
+        swapped = swap_halves(x)
+        for half in (jnp.where(low, x, swapped), jnp.where(low, swapped, x)):
+            yield jnp.where(mask, jnp.concatenate([half, half], axis=1), 0.0)
+
     for b in range(GROUPS):
-        got = got_ref[b * GROUP : (b + 1) * GROUP].astype(F32)
-        lse, delta = unpack_stats(got)
-        first = got[:, :SLOTS].reshape(GSLOTS, 128)
-        second = got[:, SLOTS:].reshape(GSLOTS, 128)
         half, at = divmod(b, GROUPS // 2)
         there = slice(at * GLANES, (at + 1) * GLANES)
-        key_part, slot_ref = keys[half], slots[half]
-        qs, gs, out, dq, mean = (slot_ref[slot_part(i), there].astype(F32) for i in range(3, 8))
-        stats = key_part[2 * ROWS :, there]
+        query_part, key_part, stat_ref, slot_ref, left_ref = halves[half]
+        near = got_ref[b * GSLOTS : (b + 1) * GSLOTS].astype(F32)
+        far = got_ref[HEADS * SLOTS + b * GSLOTS : HEADS * SLOTS + (b + 1) * GSLOTS].astype(F32)
+        lse, delta = unpack_stats(far.reshape(GROUP, SLOTS, 128), 2)
+        query_side = tuple(spread(jnp.where(slot < FAR_SLOT, near, far)))
+        key_side = tuple(spread(jnp.where(slot < FAR_SLOT, far, near)))
+        qs, gs, out, dq, mean = (slot_ref[slot_part(i), there].astype(F32) for i in range(5))
+        stats = stat_ref[:, there]
         factor = jnp.exp(stats[:, :1] - lse)
         shift = factor * (stats[:, 1:2] - delta)
-        left = slot_ref[slot_part(0, 3), there]
-        right = jnp.concatenate(
-            [
-                jnp.concatenate([shift * qs, factor * qs, spread(second, True)], axis=0),
-                jnp.concatenate([factor * gs, zero, spread(second, False)], axis=0),
-            ],
-            axis=1,
+        out = factor * out + query_side[0]
+        dq = factor * dq + shift * mean + query_side[1]
+        right = (
+            (zero, zero, shift * qs, factor * gs),
+            (zero, zero, factor * qs, zero),
+            (out, dq, zero, zero),
+            (zero, zero) + key_side,
         )
-        sums = dot_tn(left, right.astype(BF16))
-        finished(2, b, key_part[:ROWS, there] + sums[:, :GLANES])
-        finished(3, b, key_part[ROWS : 2 * ROWS, there] + sums[:, GLANES:])
-        out = factor * out + spread(first, True)
-        dq = factor * dq + shift * mean + spread(first, False)
-        right = jnp.concatenate([out, dq], axis=1).astype(BF16)
-        picked.append((left[2 * GSLOTS :], right))
-    for b in (2, 3, 0, 1):
-        half, at = divmod(b, GROUPS // 2)
-        there = slice(at * GLANES, (at + 1) * GLANES)
-        if b == 0:
-            early_copy.wait()
-        query_part = late if half else held
-        sums = dot_tn(*picked[b])
-        finished(0, b, query_part[0, :, there].astype(F32) + sums[:, :GLANES])
-        finished(1, b, query_part[1, :, there].astype(F32) + sums[:, GLANES:])
-    for send in sends:
-        send.wait()
+        right = jnp.concatenate([jnp.concatenate(x, axis=1) for x in right], axis=0)
+        sums = dot_nn(left_ref[:, at * TERMS : (at + 1) * TERMS], right.astype(BF16))
+        if b:
+            send((0, 1, 2, 3), b - 1, 1)
+        for i in range(4):
+            bulk = (query_part if i < 2 else key_part)[i % 2, :, there].astype(F32)
+            finished(i, b, bulk + sums[:, i * GLANES : (i + 1) * GLANES])
+    send((0, 1, 2, 3), 3, 1)
+    for copy in sends:
+        copy.wait()
 
 
 def finish_call(got, parts):
@@ -600,18 +589,16 @@
     vmem = pl.BlockSpec(memory_space=pltpu.VMEM)
     return pl.pallas_call(
         finish_kernel,
-        in_specs=[vmem, hbm] + [vmem] * 5,
+        in_specs=[vmem] * 11,
         out_specs=[hbm] * 4,
         out_shape=[jax.ShapeDtypeStruct((ROWS, WIDTH), BF16)] * 4,
         scratch_shapes=[
-            pltpu.VMEM((2, ROWS, WIDTH // 2), BF16),
-            pltpu.SemaphoreType.DMA,
             pltpu.VMEM((4, ROWS, WIDTH), BF16),
             pltpu.SemaphoreType.DMA((GROUPS, 4)),
         ],
         compiler_params=pltpu.CompilerParams(vmem_limit_bytes=VMEM_BYTES),
         name="finish_rows",
-    )(got, *pinned(pltpu.HBM, parts[0]), *parts[1:])
+    )(got, *parts)
 
 
 def exchange(x, axis):
@@ -624,14 +611,14 @@
     pay = select_call(near_offsets, far_offsets, *arrays)
     got = exchange(pay.reshape(SEQ, 2 * SLOTS, 128), "seq")
     (near_1, far_1), _ = lax.optimization_barrier(((near_offsets, far_offsets), pay))
-    parts = tuple(local_call(0, half, near_1, far_1, *arrays, False))
-    got, parts = lax.optimization_barrier((got, parts))
+    *parts, place = local_call(0, half, near_1, far_1, *arrays, BF16)
+    got, parts, place = lax.optimization_barrier((got, parts, place))
     far_pay, stats = near_call(got)
     far_got = exchange(far_pay, "outer")
-    back = owner_call(got, stats, far_got)
+    back = owner_call(place, got, stats, far_got)
     (near_2, far_2), back = lax.optimization_barrier(((near_offsets, far_offsets), back))
     back_got = exchange(back, "seq")
-    parts += tuple(local_call(half, GROUPS - half, near_2, far_2, *arrays, True))
+    parts += local_call(half, GROUPS - half, near_2, far_2, *arrays, F32)[:-1]
     return finish_call(back_got, parts)
 
 

time: 57.2 us -> 55.2 us (0.965)
  Pallas kernels: 18.8 us -> 17.1 us
    pallas_call x2, Pallas kernels: 5.55 us -> 4.29 us  [the longest x1 2.23 us: owner_call(): pl.pallas_call(owner_kernel, in_specs=[vmem, vmem, vmem, vmem], out_specs...]
where the time goes in v4:
time: 55.2 us; the launch traced here: 54.9 us
  Pallas kernels  17.1 us (31%)
  starting transfers between devices  15.7 us (28%)
  blocking collectives  12.2 us (22%)
  waiting for transfers between devices  9.1 us (16%)
  between operations  0.68 us (1%)
    all_to_all x2, starting transfers between devices, exchange(): return lax.all_to_all(x, axis, split_axis=0, concat_axis=0, tiled=True)  15.7 us
    all_to_all x1, blocking collectives, exchange(): return lax.all_to_all(x, axis, split_axis=0, concat_axis=0, tiled=True)  12.2 us
    pallas_call x2, Pallas kernels, local_call(): pl.pallas_call(functools.partial(local_kernel, base, count), in_specs=[hb...  9.1 us
    all_to_all x2, waiting for transfers between devices, exchange(): return lax.all_to_all(x, axis, split_axis=0, concat_axis=0, tiled=True)  9.1 us
    pallas_call x1, Pallas kernels, select_call(): pl.pallas_call(select_kernel, in_specs=[hbm] * 6, out_specs=vmem, out_sha...  3.01 us
    pallas_call x1, Pallas kernels, owner_call(): pl.pallas_call(owner_kernel, in_specs=[vmem, vmem, vmem, vmem], out_specs...  2.23 us
    pallas_call x1, Pallas kernels, finish_call(): pl.pallas_call(finish_kernel, in_specs=[vmem] * 11, out_specs=[hbm] * 4,...  2.06 us
  transfers between devices with their start and end apart: 2, of which 2 were waited for; matrix products, arithmetic and copies ran while one was open for 0% of the time, Pallas kernels for 17%

profile of v4, /device:TPU:1, one launch (start us, length us, event | category | flops | bytes accessed | tf_op | source)
XLA Modules:
  0.0 54.9 jit_solution(16112229514748882085)
XLA Ops:
  0.6 3.0 %select_rows.1 = bf16[2,16,16,128]{3,2,1,0:T(8,128)(2,1)} custom-call(s32[16]{0:T(128)} %near_in.3, s32[16]{0:T(128)} %far_in.3, bf16[256,1024]{1,0:T(8,128)(2,1)} %q_ref.5, bf16[256,1024]{1,0:T(8,128)(2,1)} %k_ref.5, bf16[256,1024]{1,0:T(8,128)(2,1)} %v_ref.5, bf16[256,1024]{1,0:T(8,128)(2,1)} %g_ref.5), custom_call_target="tpu_custom_call" | custom-call | tf_op jit(solution)/shard_map/select_rows/pallas_call | solution.py:241
  3.6 11.9 %all-to-all-start = ((bf16[32,16,128]{2,1,0:T(8,128)(2,1)}), bf16[32,16,128]{2,1,0:T(8,128)(2,1)S(1)}, u32[]{:S(2)}, u32[]{:S(2)}) async-start(bf16[32,16,128]{2,1,0:T(8,128)(2,1)} %bitcast), calls=%async_computation | async-start | bytes 262144 | tf_op jit(solution)/shard_map/all_to_all | solution.py:605
  15.5 4.5 %local_level.2 = (bf16[2,256,512]{2,1,0:T(8,128)(2,1)S(1)}, bf16[2,256,512]{2,1,0:T(8,128)(2,1)S(1)}, f32[32,512]{1,0:T(8,128)S(1)}, bf16[160,512]{1,0:T(8,128)(...) custom-call(s32[16]{0:T(128)} %near_in.3, s32[16]{0:T(128)} %far_in.3, bf16[256,1024]{1,0:T(8,128)(2,1)} %q_ref.5, ...), custom_call_target="tpu_custom_call" | custom-call | flops 469762048 | bytes 1835008 | tf_op jit(solution)/shard_map/local_level/pallas_call | solution.py:369
  20.1 4.8 %all-to-all-done.got_ref = bf16[32,16,128]{2,1,0:T(8,128)(2,1)S(1)} async-done(((bf16[32,16,128]{2,1,0:T(8,128)(2,1)}), bf16[32,16,128]{2,1,0:T(8,128)(2,1)S(1)}, u32[]{:S(2)}, u32[]{:S(2)}) %all-to-all-start) | async-done | bytes 131104 | tf_op jit(solution)/shard_map/all_to_all | solution.py:605
  24.9 0.7 %near_forward.1 = (bf16[8,96,128]{2,1,0:T(8,128)(2,1)S(1)}, f32[256,128]{1,0:T(8,128)S(1)}) custom-call(bf16[32,16,128]{2,1,0:T(8,128)(2,1)S(1)} %all-to-all-done.got_ref), custom_call_target="tpu_custom_call" | custom-call | tf_op jit(solution)/shard_map/near_forward/pallas_call | solution.py:444
  25.6 12.2 %all_to_all.21.far_got_ref = bf16[8,96,128]{2,1,0:T(8,128)(2,1)S(1)} all-to-all(bf16[8,96,128]{2,1,0:T(8,128)(2,1)S(1)} %get-tuple-element.40), channel_id=1, replica_groups=mesh['seq'=32,'outer'=8] {'outer'}, dimensions={0} | all-to-all | bytes 393216 | tf_op jit(solution)/shard_map/all_to_all | solution.py:605
  37.8 2.2 %owner_level.1 = bf16[256,128]{1,0:T(8,128)(2,1)} custom-call(s32[8,128]{1,0:T(8,128)S(1)} %get-tuple-element.37.place_ref, bf16[32,16,128]{2,1,0:T(8,128)(2,1)S(1)} %all-to-all-done.got_ref, f32[256,128]{1,0:T(8,128)S(1)} %get-tuple-element.39.stat_ref, bf16[8,96,128]{2,1,0:T(8,128)(2,1)S(1)} %all_to_all.21.far_got_ref), custom_call_target="tpu_custom_call" | custom-call | tf_op jit(solution)/shard_map/owner_level/pallas_call | solution.py:519
  40.1 3.9 %all-to-all-start.2 = ((bf16[32,8,128]{2,1,0:T(8,128)(2,1)}), bf16[32,8,128]{2,1,0:T(8,128)(2,1)S(1)}, u32[]{:S(2)}, u32[]{:S(2)}) async-start(bf16[32,8,128]{2,1,0:T(8,128)(2,1)} %bitcast.1), calls=%async_computation.2 | async-start | bytes 131072 | tf_op jit(solution)/shard_map/all_to_all | solution.py:605
  43.9 4.6 %local_level.3 = (bf16[2,256,512]{2,1,0:T(8,128)(2,1)S(1)}, f32[2,256,512]{2,1,0:T(8,128)S(1)}, f32[32,512]{1,0:T(8,128)S(1)}, bf16[160,512]{1,0:T(8,128)(2,1)S(...) custom-call(s32[16]{0:T(128)} %near_in.3, s32[16]{0:T(128)} %far_in.3, bf16[256,1024]{1,0:T(8,128)(2,1)} %q_ref.5, ...), custom_call_target="tpu_custom_call" | custom-call | flops 469762048 | bytes 1835008 | tf_op jit(solution)/shard_map/local_level/pallas_call | solution.py:369
  48.5 4.3 %all-to-all-done.2 = bf16[32,8,128]{2,1,0:T(8,128)(2,1)S(1)} async-done(((bf16[32,8,128]{2,1,0:T(8,128)(2,1)}), bf16[32,8,128]{2,1,0:T(8,128)(2,1)S(1)}, u32[]{:S(2)}, u32[]{:S(2)}) %all-to-all-start.2) | async-done | bytes 65568 | tf_op jit(solution)/shard_map/all_to_all | solution.py:605
  52.8 2.1 %finish_rows.1 = (bf16[256,1024]{1,0:T(8,128)(2,1)}, bf16[256,1024]{1,0:T(8,128)(2,1)}, bf16[256,1024]{1,0:T(8,128)(2,1)}, bf16[256,1024]{1,0:T(8,128)(2,1)}) custom-call(bf16[256,128]{1,0:T(8,128)(2,1)S(1)} %bitcast.3, bf16[2,256,512]{2,1,0:T(8,128)(2,1)S(1)} %get-tuple-element.42.refs_0_, bf16[2,256,512]{2,1,0:T(8,128)(2,1)S(1)} %get-tuple-element.43.refs_1_, ...), custom_call_target="tpu_custom_call" | custom-call | tf_op jit(solution)/shard_map/finish_rows/pallas_call | solution.py:590
Async XLA Ops:
  3.6 21.2 %all-to-all-start = ((bf16[32,16,128]{2,1,0:T(8,128)(2,1)}), bf16[32,16,128]{2,1,0:T(8,128)(2,1)S(1)}, u32[]{:S(2)}, u32[]{:S(2)}) async-start(bf16[32,16,128]{2,1,0:T(8,128)(2,1)} %bitcast), calls=%async_computation | async-start | bytes 262144 | tf_op jit(solution)/shard_map/all_to_all | solution.py:605
  40.1 12.7 %all-to-all-start.2 = ((bf16[32,8,128]{2,1,0:T(8,128)(2,1)}), bf16[32,8,128]{2,1,0:T(8,128)(2,1)S(1)}, u32[]{:S(2)}, u32[]{:S(2)}) async-start(bf16[32,8,128]{2,1,0:T(8,128)(2,1)} %bitcast.1), calls=%async_computation.2 | async-start | bytes 131072 | tf_op jit(solution)/shard_map/all_to_all | solution.py:605

commit v5 on v4

--- a/solution.py
+++ b/solution.py
@@ -23,6 +23,7 @@
 COPY_LANE = 50
 GROUP = 4
 GROUPS = HEADS // GROUP
+EARLY = 0
 GLANES = GROUP * FEAT
 GSLOTS = GROUP * SLOTS
 SCALE = FEAT**-0.5
@@ -310,9 +311,8 @@
 
 def local_kernel(
     base, count, near_in, far_in, q_ref, k_ref, v_ref, g_ref, query_ref, key_ref, stat_ref, slot_ref,
-    left_ref, place_ref, near_ref, far_ref, offset_sems, buffer, sems
+    left_ref, near_ref, far_ref, offset_sems, buffer, sems
 ):
-    place_ref[...] = jnp.full(place_ref.shape, lax.axis_index("outer") * SEQ, jnp.int32)
     offset_copies = start_offsets(near_in, far_in, near_ref, far_ref, offset_sems)
     start_copies((q_ref, k_ref, v_ref, g_ref), base, count, buffer, sems)
     for copy in offset_copies:
@@ -369,14 +369,13 @@
     return pl.pallas_call(
         functools.partial(local_kernel, base, count),
         in_specs=[hbm] * 6,
-        out_specs=[vmem] * 6,
+        out_specs=[vmem] * 5,
         out_shape=[
             pltpu.VMEM((2,) + shape, BF16),
             pltpu.VMEM((2,) + shape, key_type),
             pltpu.VMEM((GSLOTS, count * GLANES), F32),
             pltpu.VMEM((SLOT_PARTS * GSLOTS, count * GLANES), BF16),
             pltpu.VMEM((ROWS, count * TERMS), BF16),
-            pltpu.VMEM((8, 128), jnp.int32),
         ],
         scratch_shapes=OFFSET_SCRATCH
         + [pltpu.VMEM((4,) + shape, BF16), pltpu.SemaphoreType.DMA((count, 4))],
@@ -465,8 +464,8 @@
     return query_side * jnp.where(low, 1.0, SCALE), key_side * jnp.where(low, SCALE, 1.0)
 
 
-def owner_kernel(place_ref, got_ref, stat_ref, far_got_ref, send_ref):
-    place = place_ref[:1, :1]
+def owner_kernel(got_ref, stat_ref, far_got_ref, send_ref):
+    place = lax.axis_index("outer") * SEQ
     got = got_ref[...].astype(F32)
     near, far, copy = read_offsets(got)
     rows = SEQ * SLOTS
@@ -514,20 +513,20 @@
     send_ref[...] = jnp.where(copy == 0, near_block, far_block).astype(BF16)
 
 
-def owner_call(place, got, stats, far_got):
+def owner_call(got, stats, far_got):
     vmem = pl.BlockSpec(memory_space=pltpu.VMEM)
     return pl.pallas_call(
         owner_kernel,
-        in_specs=[vmem, vmem, vmem, vmem],
+        in_specs=[vmem, vmem, vmem],
         out_specs=vmem,
         out_shape=pltpu.VMEM((SEQ * SLOTS, 128), BF16),
         compiler_params=pltpu.CompilerParams(vmem_limit_bytes=VMEM_BYTES),
         name="owner_level",
-    )(place, got, stats, far_got)
+    )(got, stats, far_got)
 
 
 def finish_kernel(got_ref, *refs):
-    halves, outs, (results, out_sems) = (refs[:5], refs[5:10]), refs[10:14], refs[14:]
+    halves, outs, (results, out_sems) = (refs[:5],), refs[5:9], refs[9:]
     mask = head_mask()
     low = iota((GSLOTS, 128), 1) < FEAT
     slot = iota((GSLOTS, 128), 0) % SLOTS
@@ -552,7 +551,7 @@
             yield jnp.where(mask, jnp.concatenate([half, half], axis=1), 0.0)
 
     for b in range(GROUPS):
-        half, at = divmod(b, GROUPS // 2)
+        half, at = 0, b
         there = slice(at * GLANES, (at + 1) * GLANES)
         query_part, key_part, stat_ref, slot_ref, left_ref = halves[half]
         near = got_ref[b * GSLOTS : (b + 1) * GSLOTS].astype(F32)
@@ -589,7 +588,7 @@
     vmem = pl.BlockSpec(memory_space=pltpu.VMEM)
     return pl.pallas_call(
         finish_kernel,
-        in_specs=[vmem] * 11,
+        in_specs=[vmem] * 6,
         out_specs=[hbm] * 4,
         out_shape=[jax.ShapeDtypeStruct((ROWS, WIDTH), BF16)] * 4,
         scratch_shapes=[
@@ -607,18 +606,15 @@
 
 def on_device(queries, keys, values, out_grad, near_offsets, far_offsets):
     arrays = (queries, keys, values, out_grad)
-    half = GROUPS // 2
     pay = select_call(near_offsets, far_offsets, *arrays)
     got = exchange(pay.reshape(SEQ, 2 * SLOTS, 128), "seq")
-    (near_1, far_1), _ = lax.optimization_barrier(((near_offsets, far_offsets), pay))
-    *parts, place = local_call(0, half, near_1, far_1, *arrays, BF16)
-    got, parts, place = lax.optimization_barrier((got, parts, place))
+    parts = []
     far_pay, stats = near_call(got)
     far_got = exchange(far_pay, "outer")
-    back = owner_call(place, got, stats, far_got)
+    back = owner_call(got, stats, far_got)
     (near_2, far_2), back = lax.optimization_barrier(((near_offsets, far_offsets), back))
     back_got = exchange(back, "seq")
-    parts += local_call(half, GROUPS - half, near_2, far_2, *arrays, F32)[:-1]
+    parts += local_call(EARLY, GROUPS - EARLY, near_2, far_2, *arrays, BF16)
     return finish_call(back_got, parts)
 
 

time: 55.2 us -> 54.2 us (0.982)
  blocking collectives: 12.2 us -> 33.2 us
  starting transfers between devices: 15.7 us -> 3.86 us
  waiting for transfers between devices: 9.1 us -> 0.84 us
  Pallas kernels: 17.1 us -> 15.4 us
    all_to_all x1 -> x2, blocking collectives: 12.2 us -> 33.2 us  [exchange(): return lax.all_to_all(x, axis, split_axis=0, concat_axis=0, tiled=True)]
    all_to_all x2 -> x1, starting transfers between devices: 15.7 us -> 3.86 us  [exchange(): return lax.all_to_all(x, axis, split_axis=0, concat_axis=0, tiled=True)]
    all_to_all x2 -> x1, waiting for transfers between devices: 9.1 us -> 0.84 us  [exchange(): return lax.all_to_all(x, axis, split_axis=0, concat_axis=0, tiled=True)]
    pallas_call x2 -> x1, Pallas kernels: 9.1 us -> 8.03 us  [local_call(): pl.pallas_call(functools.partial(local_kernel, base, count), in_specs=[hb...]
    pallas_call x1, Pallas kernels: 3.01 us -> 2.36 us  [select_call(): pl.pallas_call(select_kernel, in_specs=[hbm] * 6, out_specs=vmem, out_sha...]
  transfers between devices with their start and end apart: 2 -> 1, of which waited for: 2 -> 1; matrix products, arithmetic and copies ran while one was open for 0% -> 0% of each run, Pallas kernels for 17% -> 15%
where the time goes in v5:
time: 54.2 us; the launch traced here: 54 us
  blocking collectives  33.2 us (61%)
  Pallas kernels  15.4 us (28%)
  starting transfers between devices  3.86 us (7%)
  waiting for transfers between devices  0.84 us (2%)
  between operations  0.66 us (1%)
    all_to_all x2, blocking collectives, exchange(): return lax.all_to_all(x, axis, split_axis=0, concat_axis=0, tiled=True)  33.2 us
    pallas_call x1, Pallas kernels, local_call(): pl.pallas_call(functools.partial(local_kernel, base, count), in_specs=[hb...  8.03 us
    all_to_all x1, starting transfers between devices, exchange(): return lax.all_to_all(x, axis, split_axis=0, concat_axis=0, tiled=True)  3.86 us
    pallas_call x1, Pallas kernels, select_call(): pl.pallas_call(select_kernel, in_specs=[hbm] * 6, out_specs=vmem, out_sha...  2.36 us
    pallas_call x1, Pallas kernels, owner_call(): pl.pallas_call(owner_kernel, in_specs=[vmem, vmem, vmem], out_specs=vmem,...  2.23 us
    pallas_call x1, Pallas kernels, finish_call(): pl.pallas_call(finish_kernel, in_specs=[vmem] * 6, out_specs=[hbm] * 4, o...  2.06 us
  transfers between devices with their start and end apart: 1, of which 1 were waited for; matrix products, arithmetic and copies ran while one was open for 0% of the time, Pallas kernels for 15%

profile of v5, /device:TPU:1, one launch (start us, length us, event | category | flops | bytes accessed | tf_op | source)
XLA Modules:
  0.0 54.0 jit_solution(11859469779315903721)
XLA Ops:
  0.6 2.4 %select_rows.1 = bf16[2,16,16,128]{3,2,1,0:T(8,128)(2,1)S(1)} custom-call(s32[16]{0:T(128)} %near_in.2, s32[16]{0:T(128)} %far_in.2, bf16[256,1024]{1,0:T(8,128)(2,1)} %q_ref.3, bf16[256,1024]{1,0:T(8,128)(2,1)} %k_ref.3, bf16[256,1024]{1,0:T(8,128)(2,1)} %v_ref.3, bf16[256,1024]{1,0:T(8,128)(2,1)} %g_ref.3), custom_call_target="tpu_custom_call" | custom-call | tf_op jit(solution)/shard_map/select_rows/pallas_call | solution.py:242
  3.0 21.0 %all_to_all.21.got_ref = bf16[32,16,128]{2,1,0:T(8,128)(2,1)S(1)} all-to-all(bf16[32,16,128]{2,1,0:T(8,128)(2,1)S(1)} %bitcast.3), channel_id=1, replica_groups=mesh['seq'=32,'outer'=8] {'seq'}, dimensions={0} | all-to-all | bytes 262144 | tf_op jit(solution)/shard_map/all_to_all | solution.py:604
  24.0 0.7 %near_forward.1 = (bf16[8,96,128]{2,1,0:T(8,128)(2,1)S(1)}, f32[256,128]{1,0:T(8,128)S(1)}) custom-call(bf16[32,16,128]{2,1,0:T(8,128)(2,1)S(1)} %all_to_all.21.got_ref), custom_call_target="tpu_custom_call" | custom-call | tf_op jit(solution)/shard_map/near_forward/pallas_call | solution.py:443
  24.7 12.2 %all_to_all.22.far_got_ref = bf16[8,96,128]{2,1,0:T(8,128)(2,1)S(1)} all-to-all(bf16[8,96,128]{2,1,0:T(8,128)(2,1)S(1)} %get-tuple-element.15), channel_id=1, replica_groups=mesh['seq'=32,'outer'=8] {'outer'}, dimensions={0} | all-to-all | bytes 393216 | tf_op jit(solution)/shard_map/all_to_all | solution.py:604
  37.0 2.2 %owner_level.1 = bf16[256,128]{1,0:T(8,128)(2,1)} custom-call(bf16[32,16,128]{2,1,0:T(8,128)(2,1)S(1)} %all_to_all.21.got_ref, f32[256,128]{1,0:T(8,128)S(1)} %get-tuple-element.14.stat_ref, bf16[8,96,128]{2,1,0:T(8,128)(2,1)S(1)} %all_to_all.22.far_got_ref), custom_call_target="tpu_custom_call" | custom-call | tf_op jit(solution)/shard_map/owner_level/pallas_call | solution.py:518
  39.2 3.9 %all-to-all-start.2 = ((bf16[32,8,128]{2,1,0:T(8,128)(2,1)}), bf16[32,8,128]{2,1,0:T(8,128)(2,1)S(1)}, u32[]{:S(2)}, u32[]{:S(2)}) async-start(bf16[32,8,128]{2,1,0:T(8,128)(2,1)} %bitcast.1), calls=%async_computation.2 | async-start | bytes 131072 | tf_op jit(solution)/shard_map/all_to_all | solution.py:604
  43.0 8.0 %local_level.1 = (bf16[2,256,1024]{2,1,0:T(8,128)(2,1)S(1)}, bf16[2,256,1024]{2,1,0:T(8,128)(2,1)S(1)}, f32[32,1024]{1,0:T(8,128)S(1)}, bf16[160,1024]{1,0:T(8,128)(2,1)S(1)}, bf16[256,512]{1,0:T(8,128)(2,1)S(1)}) custom-call(s32[16]{0:T(128)} %near_in.2, s32[16]{0:T(128)} %far_in.2, bf16[256,1024]{1,0:T(8,128)(2,1)} %q_ref.3, bf16[256,1024]{1,0:T(8,128)(2,1)} %k_ref.3, ...), custom_call_target="tpu_custom_call" | custom-call | flops 939524096 | bytes 3670016 | tf_op jit(solution)/shard_map/local_level/pallas_call | solution.py:369
  51.1 0.8 %all-to-all-done.2 = bf16[32,8,128]{2,1,0:T(8,128)(2,1)S(1)} async-done(((bf16[32,8,128]{2,1,0:T(8,128)(2,1)}), bf16[32,8,128]{2,1,0:T(8,128)(2,1)S(1)}, u32[]{:S(2)}, u32[]{:S(2)}) %all-to-all-start.2) | async-done | bytes 65568 | tf_op jit(solution)/shard_map/all_to_all | solution.py:604
  51.9 2.1 %finish_rows.1 = (bf16[256,1024]{1,0:T(8,128)(2,1)}, bf16[256,1024]{1,0:T(8,128)(2,1)}, bf16[256,1024]{1,0:T(8,128)(2,1)}, bf16[256,1024]{1,0:T(8,128)(2,1)}) custom-call(bf16[256,128]{1,0:T(8,128)(2,1)S(1)} %bitcast.4, bf16[2,256,1024]{2,1,0:T(8,128)(2,1)S(1)} %get-tuple-element.19.refs_0_, bf16[2,256,1024]{2,1,0:T(8,128)(2,1)S(1)} %get-tuple-element.20.refs_1_, ...), custom_call_target="tpu_custom_call" | custom-call | tf_op jit(solution)/shard_map/finish_rows/pallas_call | solution.py:589
Async XLA Ops:
  39.2 12.7 %all-to-all-start.2 = ((bf16[32,8,128]{2,1,0:T(8,128)(2,1)}), bf16[32,8,128]{2,1,0:T(8,128)(2,1)S(1)}, u32[]{:S(2)}, u32[]{:S(2)}) async-start(bf16[32,8,128]{2,1,0:T(8,128)(2,1)} %bitcast.1), calls=%async_computation.2 | async-start | bytes 131072 | tf_op jit(solution)/shard_map/all_to_all | solution.py:604

commit v6 on v5

--- a/solution.py
+++ b/solution.py
@@ -23,11 +23,12 @@
 COPY_LANE = 50
 GROUP = 4
 GROUPS = HEADS // GROUP
-EARLY = 0
+EARLY = 2
 GLANES = GROUP * FEAT
 GSLOTS = GROUP * SLOTS
 SCALE = FEAT**-0.5
 LOW = -1e30
+BACKWARDS = [list(range(SEQ - 1, -1, -1))]
 SLOT_PARTS = 5
 TERMS = 4 * GSLOTS
 F32 = jnp.float32
@@ -395,7 +396,7 @@
 
     def position(index):
         slot = index % SLOTS
-        return index // SLOTS * ROWS + jnp.where(slot < FAR_SLOT, near + NEAR_RATE * slot, far)
+        return (SEQ - 1 - index // SLOTS) * ROWS + jnp.where(slot < FAR_SLOT, near + NEAR_RATE * slot, far)
 
     return col, line, position(col), position(line)
 
@@ -464,8 +465,12 @@
     return query_side * jnp.where(low, 1.0, SCALE), key_side * jnp.where(low, SCALE, 1.0)
 
 
+def far_order(index):
+    return SEQ * OUTER - 1 - index
+
+
 def owner_kernel(got_ref, stat_ref, far_got_ref, send_ref):
-    place = lax.axis_index("outer") * SEQ
+    place = (OUTER - 1 - lax.axis_index("outer")) * SEQ
     got = got_ref[...].astype(F32)
     near, far, copy = read_offsets(got)
     rows = SEQ * SLOTS
@@ -477,7 +482,8 @@
     far_halves = pair_halves(far_qk, far_vg)
     scores = dot_nt(far_halves[0], far_halves[1]) * SCALE
     grads = dot_nt(far_halves[3], far_halves[2])
-    allowed = iota((rows, rows), 1) <= iota((rows, rows), 0)
+    ask, key = far_order(iota((rows, rows), 0)), far_order(iota((rows, rows), 1))
+    allowed = key <= ask
     top, total, grad_total = softmax_terms(scores, allowed, grads)
     lse, delta = merge_terms(*read_parts(far_stats, lane), top, total, grad_total)
     query_side, key_side = level_grads(far_halves, scores, allowed, grads, lse, delta)
@@ -526,7 +532,7 @@
 
 
 def finish_kernel(got_ref, *refs):
-    halves, outs, (results, out_sems) = (refs[:5],), refs[5:9], refs[9:]
+    halves, outs, (results, out_sems) = (refs[:5], refs[5:10]), refs[10:14], refs[14:]
     mask = head_mask()
     low = iota((GSLOTS, 128), 1) < FEAT
     slot = iota((GSLOTS, 128), 0) % SLOTS
@@ -551,7 +557,7 @@
             yield jnp.where(mask, jnp.concatenate([half, half], axis=1), 0.0)
 
     for b in range(GROUPS):
-        half, at = 0, b
+        half, at = (0, b) if b < EARLY else (1, b - EARLY)
         there = slice(at * GLANES, (at + 1) * GLANES)
         query_part, key_part, stat_ref, slot_ref, left_ref = halves[half]
         near = got_ref[b * GSLOTS : (b + 1) * GSLOTS].astype(F32)
@@ -588,7 +594,7 @@
     vmem = pl.BlockSpec(memory_space=pltpu.VMEM)
     return pl.pallas_call(
         finish_kernel,
-        in_specs=[vmem] * 6,
+        in_specs=[vmem] * 11,
         out_specs=[hbm] * 4,
         out_shape=[jax.ShapeDtypeStruct((ROWS, WIDTH), BF16)] * 4,
         scratch_shapes=[
@@ -600,21 +606,25 @@
     )(got, *parts)
 
 
-def exchange(x, axis):
-    return lax.all_to_all(x, axis, split_axis=0, concat_axis=0, tiled=True)
+def exchange(x, axis, groups=None):
+    return lax.all_to_all(
+        x, axis, split_axis=0, concat_axis=0, axis_index_groups=groups, tiled=True
+    )
 
 
 def on_device(queries, keys, values, out_grad, near_offsets, far_offsets):
     arrays = (queries, keys, values, out_grad)
     pay = select_call(near_offsets, far_offsets, *arrays)
-    got = exchange(pay.reshape(SEQ, 2 * SLOTS, 128), "seq")
-    parts = []
+    got = exchange(pay.reshape(SEQ, 2 * SLOTS, 128), "seq", BACKWARDS)
+    (near_1, far_1), _ = lax.optimization_barrier(((near_offsets, far_offsets), pay))
+    parts = local_call(0, EARLY, near_1, far_1, *arrays, BF16)
+    got, parts = lax.optimization_barrier((got, parts))
     far_pay, stats = near_call(got)
-    far_got = exchange(far_pay, "outer")
+    far_got = exchange(far_pay, "outer", [list(range(OUTER - 1, -1, -1))])
     back = owner_call(got, stats, far_got)
     (near_2, far_2), back = lax.optimization_barrier(((near_offsets, far_offsets), back))
-    back_got = exchange(back, "seq")
-    parts += local_call(EARLY, GROUPS - EARLY, near_2, far_2, *arrays, BF16)
+    back_got = exchange(back, "seq", BACKWARDS)
+    parts += local_call(EARLY, GROUPS - EARLY, near_2, far_2, *arrays, F32)
     return finish_call(back_got, parts)
 
 

time: 54.2 us -> 50.9 us (0.939)
  blocking collectives: 33.2 us -> 10.5 us
  starting transfers between devices: 3.86 us -> 20.3 us
  Pallas kernels: 15.4 us -> 17.1 us
  waiting for transfers between devices: 0.84 us -> 1.68 us
    all_to_all x2 -> x1, blocking collectives: 33.2 us -> 10.5 us  [exchange(): lax.all_to_all(x, axis, split_axis=0, concat_axis=0, axis_index_groups=gr...]
    all_to_all x1 -> x2, starting transfers between devices: 3.86 us -> 20.3 us  [exchange(): lax.all_to_all(x, axis, split_axis=0, concat_axis=0, axis_index_groups=gr...]
    pallas_call x1 -> x2, Pallas kernels: 8.03 us -> 9.09 us  [local_call(): pl.pallas_call(functools.partial(local_kernel, base, count), in_specs=[hb...]
    all_to_all x1 -> x2, waiting for transfers between devices: 0.84 us -> 1.68 us  [exchange(): lax.all_to_all(x, axis, split_axis=0, concat_axis=0, axis_index_groups=gr...]
    pallas_call x1, Pallas kernels: 2.36 us -> 3.01 us  [select_call(): pl.pallas_call(select_kernel, in_specs=[hbm] * 6, out_specs=vmem, out_sha...]
  transfers between devices with their start and end apart: 1 -> 2, of which waited for: 1 -> 2; matrix products, arithmetic and copies ran while one was open for 0% -> 0% of each run, Pallas kernels for 15% -> 18%
where the time goes in v6:
time: 50.9 us; the launch traced here: 50.4 us
  starting transfers between devices  20.3 us (40%)
  Pallas kernels  17.1 us (34%)
  blocking collectives  10.5 us (21%)
  waiting for transfers between devices  1.68 us (3%)
  between operations  0.68 us (1%)
    all_to_all x2, starting transfers between devices, exchange(): lax.all_to_all(x, axis, split_axis=0, concat_axis=0, axis_index_groups=gr...  20.3 us
    all_to_all x1, blocking collectives, exchange(): lax.all_to_all(x, axis, split_axis=0, concat_axis=0, axis_index_groups=gr...  10.5 us
    pallas_call x2, Pallas kernels, local_call(): pl.pallas_call(functools.partial(local_kernel, base, count), in_specs=[hb...  9.09 us
    pallas_call x1, Pallas kernels, select_call(): pl.pallas_call(select_kernel, in_specs=[hbm] * 6, out_specs=vmem, out_sha...  3.01 us
    pallas_call x1, Pallas kernels, owner_call(): pl.pallas_call(owner_kernel, in_specs=[vmem, vmem, vmem], out_specs=vmem,...  2.26 us
    pallas_call x1, Pallas kernels, finish_call(): pl.pallas_call(finish_kernel, in_specs=[vmem] * 11, out_specs=[hbm] * 4,...  2.07 us
    all_to_all x2, waiting for transfers between devices, exchange(): lax.all_to_all(x, axis, split_axis=0, concat_axis=0, axis_index_groups=gr...  1.68 us
  transfers between devices with their start and end apart: 2, of which 2 were waited for; matrix products, arithmetic and copies ran while one was open for 0% of the time, Pallas kernels for 18%

profile of v6, /device:TPU:1, one launch (start us, length us, event | category | flops | bytes accessed | tf_op | source)
XLA Modules:
  0.0 50.4 jit_solution(16156187077380617350)
XLA Ops:
  0.6 3.0 %select_rows.1 = bf16[2,16,16,128]{3,2,1,0:T(8,128)(2,1)} custom-call(s32[16]{0:T(128)} %near_in.3, s32[16]{0:T(128)} %far_in.3, bf16[256,1024]{1,0:T(8,128)(2,1)} %q_ref.5, bf16[256,1024]{1,0:T(8,128)(2,1)} %k_ref.5, bf16[256,1024]{1,0:T(8,128)(2,1)} %v_ref.5, bf16[256,1024]{1,0:T(8,128)(2,1)} %g_ref.5), custom_call_target="tpu_custom_call" | custom-call | tf_op jit(solution)/shard_map/select_rows/pallas_call | solution.py:243
  3.6 12.6 %all-to-all-start = ((bf16[32,16,128]{2,1,0:T(8,128)(2,1)}), bf16[32,16,128]{2,1,0:T(8,128)(2,1)S(1)}, u32[]{:S(2)}, u32[]{:S(2)}) async-start(bf16[32,16,128]{2,1,0:T(8,128)(2,1)} %bitcast), calls=%async_computation | async-start | bytes 262144 | tf_op jit(solution)/shard_map/all_to_all | solution.py:610
  16.2 4.5 %local_level.2 = (bf16[2,256,512]{2,1,0:T(8,128)(2,1)S(1)}, bf16[2,256,512]{2,1,0:T(8,128)(2,1)S(1)}, f32[32,512]{1,0:T(8,128)S(1)}, bf16[160,512]{1,0:T(8,128)(2,1)S(1)}, bf16[256,256]{1,0:T(8,128)(2,1)S(1)}) custom-call(s32[16]{0:T(128)} %near_in.3, s32[16]{0:T(128)} %far_in.3, bf16[256,1024]{1,0:T(8,128)(2,1)} %q_ref.5, bf16[256,1024]{1,0:T(8,128)(2,1)} %k_ref.5, ...), custom_call_target="tpu_custom_call" | custom-call | flops 469762048 | bytes 1835008 | tf_op jit(solution)/shard_map/local_level/pallas_call | solution.py:370
  20.8 1.0 %all-to-all-done.got_ref = bf16[32,16,128]{2,1,0:T(8,128)(2,1)S(1)} async-done(((bf16[32,16,128]{2,1,0:T(8,128)(2,1)}), bf16[32,16,128]{2,1,0:T(8,128)(2,1)S(1)}, u32[]{:S(2)}, u32[]{:S(2)}) %all-to-all-start) | async-done | bytes 131104 | tf_op jit(solution)/shard_map/all_to_all | solution.py:610
  21.8 0.7 %near_forward.1 = (bf16[8,96,128]{2,1,0:T(8,128)(2,1)S(1)}, f32[256,128]{1,0:T(8,128)S(1)}) custom-call(bf16[32,16,128]{2,1,0:T(8,128)(2,1)S(1)} %all-to-all-done.got_ref), custom_call_target="tpu_custom_call" | custom-call | tf_op jit(solution)/shard_map/near_forward/pallas_call | solution.py:444
  22.5 10.5 %all_to_all.21.far_got_ref = bf16[8,96,128]{2,1,0:T(8,128)(2,1)S(1)} all-to-all(bf16[8,96,128]{2,1,0:T(8,128)(2,1)S(1)} %get-tuple-element.36), channel_id=1, replica_groups={{7,6,5,4,3,2,1,0},{15,14,13,12,11,10,9,8},{23,22,21,20,19,18,17,16},{31..., dimensions={0} | all-to-all | bytes 393216 | tf_op jit(solution)/shard_map/all_to_all | solution.py:610
  33.0 2.3 %owner_level.1 = bf16[256,128]{1,0:T(8,128)(2,1)} custom-call(bf16[32,16,128]{2,1,0:T(8,128)(2,1)S(1)} %all-to-all-done.got_ref, f32[256,128]{1,0:T(8,128)S(1)} %get-tuple-element.35.stat_ref, bf16[8,96,128]{2,1,0:T(8,128)(2,1)S(1)} %all_to_all.21.far_got_ref), custom_call_target="tpu_custom_call" | custom-call | tf_op jit(solution)/shard_map/owner_level/pallas_call | solution.py:524
  35.3 7.7 %all-to-all-start.2 = ((bf16[32,8,128]{2,1,0:T(8,128)(2,1)}), bf16[32,8,128]{2,1,0:T(8,128)(2,1)S(1)}, u32[]{:S(2)}, u32[]{:S(2)}) async-start(bf16[32,8,128]{2,1,0:T(8,128)(2,1)} %bitcast.1), calls=%async_computation.2 | async-start | bytes 131072 | tf_op jit(solution)/shard_map/all_to_all | solution.py:610
  43.0 4.5 %local_level.3 = (bf16[2,256,512]{2,1,0:T(8,128)(2,1)S(1)}, f32[2,256,512]{2,1,0:T(8,128)S(1)}, f32[32,512]{1,0:T(8,128)S(1)}, bf16[160,512]{1,0:T(8,128)(2,1)S(1)}, bf16[256,256]{1,0:T(8,128)(2,1)S(1)}) custom-call(s32[16]{0:T(128)} %near_in.3, s32[16]{0:T(128)} %far_in.3, bf16[256,1024]{1,0:T(8,128)(2,1)} %q_ref.5, bf16[256,1024]{1,0:T(8,128)(2,1)} %k_ref.5, ...), custom_call_target="tpu_custom_call" | custom-call | flops 469762048 | bytes 1835008 | tf_op jit(solution)/shard_map/local_level/pallas_call | solution.py:370
  47.6 0.7 %all-to-all-done.2 = bf16[32,8,128]{2,1,0:T(8,128)(2,1)S(1)} async-done(((bf16[32,8,128]{2,1,0:T(8,128)(2,1)}), bf16[32,8,128]{2,1,0:T(8,128)(2,1)S(1)}, u32[]{:S(2)}, u32[]{:S(2)}) %all-to-all-start.2) | async-done | bytes 65568 | tf_op jit(solution)/shard_map/all_to_all | solution.py:610
  48.3 2.1 %finish_rows.1 = (bf16[256,1024]{1,0:T(8,128)(2,1)}, bf16[256,1024]{1,0:T(8,128)(2,1)}, bf16[256,1024]{1,0:T(8,128)(2,1)}, bf16[256,1024]{1,0:T(8,128)(2,1)}) custom-call(bf16[256,128]{1,0:T(8,128)(2,1)S(1)} %bitcast.3, bf16[2,256,512]{2,1,0:T(8,128)(2,1)S(1)} %get-tuple-element.38.refs_0_, bf16[2,256,512]{2,1,0:T(8,128)(2,1)S(1)} %get-tuple-element.39.refs_1_, ...), custom_call_target="tpu_custom_call" | custom-call | tf_op jit(solution)/shard_map/finish_rows/pallas_call | solution.py:595
Async XLA Ops:
  3.6 18.1 %all-to-all-start = ((bf16[32,16,128]{2,1,0:T(8,128)(2,1)}), bf16[32,16,128]{2,1,0:T(8,128)(2,1)S(1)}, u32[]{:S(2)}, u32[]{:S(2)}) async-start(bf16[32,16,128]{2,1,0:T(8,128)(2,1)} %bitcast), calls=%async_computation | async-start | bytes 262144 | tf_op jit(solution)/shard_map/all_to_all | solution.py:610
  35.3 13.0 %all-to-all-start.2 = ((bf16[32,8,128]{2,1,0:T(8,128)(2,1)}), bf16[32,8,128]{2,1,0:T(8,128)(2,1)S(1)}, u32[]{:S(2)}, u32[]{:S(2)}) async-start(bf16[32,8,128]{2,1,0:T(8,128)(2,1)} %bitcast.1), calls=%async_computation.2 | async-start | bytes 131072 | tf_op jit(solution)/shard_map/all_to_all | solution.py:610

commit v7 on v6

--- a/solution.py
+++ b/solution.py
@@ -434,8 +434,9 @@
     rows = SEQ * SLOTS
     pick = iota((SEQ, rows), 1) == iota((SEQ, rows), 0) * SLOTS + FAR_SLOT
     pick = jnp.where(pick, 1.0, 0.0).astype(BF16)
-    block = jnp.concatenate([dot_nn(pick, x.astype(BF16)) for x in (qk, vg, stats)], axis=0)
-    block = block.astype(BF16)
+    qk, vg, stats = (dot_nn(pick, x.astype(BF16)) for x in (qk, vg, stats))
+    stats = stats[: SEQ // 2] + swap_halves(stats[SEQ // 2 :])
+    block = jnp.concatenate([qk, vg, stats], axis=0).astype(BF16)
     for o in range(OUTER):
         send_ref[o] = block
 
@@ -446,7 +447,7 @@
         in_specs=[pl.BlockSpec(memory_space=pltpu.VMEM)],
         out_specs=[pl.BlockSpec(memory_space=pltpu.VMEM)] * 2,
         out_shape=[
-            pltpu.VMEM((OUTER, 3 * SEQ, 128), BF16),
+            pltpu.VMEM((OUTER, 5 * SEQ // 2, 128), BF16),
             pltpu.VMEM((SEQ * SLOTS, 128), F32),
         ],
         compiler_params=pltpu.CompilerParams(vmem_limit_bytes=VMEM_BYTES),
@@ -478,7 +479,9 @@
 
     far_qk = far_got_ref[:, :SEQ].reshape(rows, 128).astype(F32)
     far_vg = far_got_ref[:, SEQ : 2 * SEQ].reshape(rows, 128).astype(F32)
-    far_stats = far_got_ref[:, 2 * SEQ :].reshape(rows, 128).astype(F32)
+    far_stats = far_got_ref[:, 2 * SEQ :].astype(F32)
+    later = swap_halves(far_stats.reshape(rows // 2, 128)).reshape(far_stats.shape)
+    far_stats = jnp.concatenate([far_stats, later], axis=1).reshape(rows, 128)
     far_halves = pair_halves(far_qk, far_vg)
     scores = dot_nt(far_halves[0], far_halves[1]) * SCALE
     grads = dot_nt(far_halves[3], far_halves[2])

time: 50.9 us -> 50.6 us (level)
  no operation moved by 1% of the time
where the time goes in v7:
time: 50.6 us; the launch traced here: 50.1 us
  starting transfers between devices  20.3 us (40%)
  Pallas kernels  17.2 us (34%)
  blocking collectives  10.2 us (20%)
  waiting for transfers between devices  1.67 us (3%)
  between operations  0.67 us (1%)
    all_to_all x2, starting transfers between devices, exchange(): lax.all_to_all(x, axis, split_axis=0, concat_axis=0, axis_index_groups=gr...  20.3 us
    all_to_all x1, blocking collectives, exchange(): lax.all_to_all(x, axis, split_axis=0, concat_axis=0, axis_index_groups=gr...  10.2 us
    pallas_call x2, Pallas kernels, local_call(): pl.pallas_call(functools.partial(local_kernel, base, count), in_specs=[hb...  9.09 us
    pallas_call x1, Pallas kernels, select_call(): pl.pallas_call(select_kernel, in_specs=[hbm] * 6, out_specs=vmem, out_sha...  3.01 us
    pallas_call x1, Pallas kernels, owner_call(): pl.pallas_call(owner_kernel, in_specs=[vmem, vmem, vmem], out_specs=vmem,...  2.25 us
    pallas_call x1, Pallas kernels, finish_call(): pl.pallas_call(finish_kernel, in_specs=[vmem] * 11, out_specs=[hbm] * 4,...  2.06 us
    all_to_all x2, waiting for transfers between devices, exchange(): lax.all_to_all(x, axis, split_axis=0, concat_axis=0, axis_index_groups=gr...  1.67 us
  transfers between devices with their start and end apart: 2, of which 2 were waited for; matrix products, arithmetic and copies ran while one was open for 0% of the time, Pallas kernels for 18%

profile of v7, /device:TPU:1, one launch (start us, length us, event | category | flops | bytes accessed | tf_op | source)
XLA Modules:
  0.0 50.1 jit_solution(2706588812247766397)
XLA Ops:
  0.6 3.0 %select_rows.1 = bf16[2,16,16,128]{3,2,1,0:T(8,128)(2,1)} custom-call(s32[16]{0:T(128)} %near_in.3, s32[16]{0:T(128)} %far_in.3, bf16[256,1024]{1,0:T(8,128)(2,1)} %q_ref.5, bf16[256,1024]{1,0:T(8,128)(2,1)} %k_ref.5, bf16[256,1024]{1,0:T(8,128)(2,1)} %v_ref.5, bf16[256,1024]{1,0:T(8,128)(2,1)} %g_ref.5), custom_call_target="tpu_custom_call" | custom-call | tf_op jit(solution)/shard_map/select_rows/pallas_call | solution.py:243
  3.6 12.6 %all-to-all-start = ((bf16[32,16,128]{2,1,0:T(8,128)(2,1)}), bf16[32,16,128]{2,1,0:T(8,128)(2,1)S(1)}, u32[]{:S(2)}, u32[]{:S(2)}) async-start(bf16[32,16,128]{2,1,0:T(8,128)(2,1)} %bitcast), calls=%async_computation | async-start | bytes 262144 | tf_op jit(solution)/shard_map/all_to_all | solution.py:613
  16.2 4.5 %local_level.2 = (bf16[2,256,512]{2,1,0:T(8,128)(2,1)S(1)}, bf16[2,256,512]{2,1,0:T(8,128)(2,1)S(1)}, f32[32,512]{1,0:T(8,128)S(1)}, bf16[160,512]{1,0:T(8,128)(2,1)S(1)}, bf16[256,256]{1,0:T(8,128)(2,1)S(1)}) custom-call(s32[16]{0:T(128)} %near_in.3, s32[16]{0:T(128)} %far_in.3, bf16[256,1024]{1,0:T(8,128)(2,1)} %q_ref.5, bf16[256,1024]{1,0:T(8,128)(2,1)} %k_ref.5, ...), custom_call_target="tpu_custom_call" | custom-call | flops 469762048 | bytes 1835008 | tf_op jit(solution)/shard_map/local_level/pallas_call | solution.py:370
  20.8 1.0 %all-to-all-done.got_ref = bf16[32,16,128]{2,1,0:T(8,128)(2,1)S(1)} async-done(((bf16[32,16,128]{2,1,0:T(8,128)(2,1)}), bf16[32,16,128]{2,1,0:T(8,128)(2,1)S(1)}, u32[]{:S(2)}, u32[]{:S(2)}) %all-to-all-start) | async-done | bytes 131104 | tf_op jit(solution)/shard_map/all_to_all | solution.py:613
  21.8 0.8 %near_forward.1 = (bf16[8,80,128]{2,1,0:T(8,128)(2,1)S(1)}, f32[256,128]{1,0:T(8,128)S(1)}) custom-call(bf16[32,16,128]{2,1,0:T(8,128)(2,1)S(1)} %all-to-all-done.got_ref), custom_call_target="tpu_custom_call" | custom-call | tf_op jit(solution)/shard_map/near_forward/pallas_call | solution.py:445
  22.6 10.2 %all_to_all.21.far_got_ref = bf16[8,80,128]{2,1,0:T(8,128)(2,1)S(1)} all-to-all(bf16[8,80,128]{2,1,0:T(8,128)(2,1)S(1)} %get-tuple-element.36), channel_id=1, replica_groups={{7,6,5,4,3,2,1,0},{15,14,13,12,11,10,9,8},{23,22,21,20,19,18,17,16},{31..., dimensions={0} | all-to-all | bytes 327680 | tf_op jit(solution)/shard_map/all_to_all | solution.py:613
  32.8 2.2 %owner_level.1 = bf16[256,128]{1,0:T(8,128)(2,1)} custom-call(bf16[32,16,128]{2,1,0:T(8,128)(2,1)S(1)} %all-to-all-done.got_ref, f32[256,128]{1,0:T(8,128)S(1)} %get-tuple-element.35.stat_ref, bf16[8,80,128]{2,1,0:T(8,128)(2,1)S(1)} %all_to_all.21.far_got_ref), custom_call_target="tpu_custom_call" | custom-call | tf_op jit(solution)/shard_map/owner_level/pallas_call | solution.py:527
  35.0 7.8 %all-to-all-start.2 = ((bf16[32,8,128]{2,1,0:T(8,128)(2,1)}), bf16[32,8,128]{2,1,0:T(8,128)(2,1)S(1)}, u32[]{:S(2)}, u32[]{:S(2)}) async-start(bf16[32,8,128]{2,1,0:T(8,128)(2,1)} %bitcast.1), calls=%async_computation.2 | async-start | bytes 131072 | tf_op jit(solution)/shard_map/all_to_all | solution.py:613
  42.8 4.5 %local_level.3 = (bf16[2,256,512]{2,1,0:T(8,128)(2,1)S(1)}, f32[2,256,512]{2,1,0:T(8,128)S(1)}, f32[32,512]{1,0:T(8,128)S(1)}, bf16[160,512]{1,0:T(8,128)(2,1)S(1)}, bf16[256,256]{1,0:T(8,128)(2,1)S(1)}) custom-call(s32[16]{0:T(128)} %near_in.3, s32[16]{0:T(128)} %far_in.3, bf16[256,1024]{1,0:T(8,128)(2,1)} %q_ref.5, bf16[256,1024]{1,0:T(8,128)(2,1)} %k_ref.5, ...), custom_call_target="tpu_custom_call" | custom-call | flops 469762048 | bytes 1835008 | tf_op jit(solution)/shard_map/local_level/pallas_call | solution.py:370
  47.3 0.7 %all-to-all-done.2 = bf16[32,8,128]{2,1,0:T(8,128)(2,1)S(1)} async-done(((bf16[32,8,128]{2,1,0:T(8,128)(2,1)}), bf16[32,8,128]{2,1,0:T(8,128)(2,1)S(1)}, u32[]{:S(2)}, u32[]{:S(2)}) %all-to-all-start.2) | async-done | bytes 65568 | tf_op jit(solution)/shard_map/all_to_all | solution.py:613
  48.0 2.1 %finish_rows.1 = (bf16[256,1024]{1,0:T(8,128)(2,1)}, bf16[256,1024]{1,0:T(8,128)(2,1)}, bf16[256,1024]{1,0:T(8,128)(2,1)}, bf16[256,1024]{1,0:T(8,128)(2,1)}) custom-call(bf16[256,128]{1,0:T(8,128)(2,1)S(1)} %bitcast.3, bf16[2,256,512]{2,1,0:T(8,128)(2,1)S(1)} %get-tuple-element.38.refs_0_, bf16[2,256,512]{2,1,0:T(8,128)(2,1)S(1)} %get-tuple-element.39.refs_1_, ...), custom_call_target="tpu_custom_call" | custom-call | tf_op jit(solution)/shard_map/finish_rows/pallas_call | solution.py:598
Async XLA Ops:
  3.6 18.1 %all-to-all-start = ((bf16[32,16,128]{2,1,0:T(8,128)(2,1)}), bf16[32,16,128]{2,1,0:T(8,128)(2,1)S(1)}, u32[]{:S(2)}, u32[]{:S(2)}) async-start(bf16[32,16,128]{2,1,0:T(8,128)(2,1)} %bitcast), calls=%async_computation | async-start | bytes 262144 | tf_op jit(solution)/shard_map/all_to_all | solution.py:613
  35.0 13.0 %all-to-all-start.2 = ((bf16[32,8,128]{2,1,0:T(8,128)(2,1)}), bf16[32,8,128]{2,1,0:T(8,128)(2,1)S(1)}, u32[]{:S(2)}, u32[]{:S(2)}) async-start(bf16[32,8,128]{2,1,0:T(8,128)(2,1)} %bitcast.1), calls=%async_computation.2 | async-start | bytes 131072 | tf_op jit(solution)/shard_map/all_to_all | solution.py:613

commit v8 on v7

--- a/solution.py
+++ b/solution.py
@@ -76,6 +76,13 @@
     return lse, d
 
 
+def read_wide(lanes, at):
+    part = iota((128, 256), 0) % 8
+    ones = jnp.where(part // 3 == iota((128, 256), 1) // 128, 1.0, 0.0).astype(BF16)
+    both = dot_nn(jnp.where((at >= 0) & (at < 6), lanes, 0.0).astype(BF16), ones)
+    return both[:, :128], both[:, 128:]
+
+
 def pack_stats(lse, d):
     rows = lse.shape[0]
     row, lane = iota((rows, 128), 0), iota((rows, 128), 1)
@@ -85,11 +92,11 @@
     return jnp.broadcast_to(total, spread.shape).reshape(rows, 128)
 
 
-def unpack_stats(block, at=STAT_SLOT):
+def unpack_stats(block, at=STAT_SLOT, read=read_parts):
     lanes = jnp.broadcast_to(block[:, at : at + 1, :], (block.shape[0], SLOTS, 128))
     lanes = lanes.reshape(block.shape[0] * SLOTS, 128)
     row, lane = iota(lanes.shape, 0), iota(lanes.shape, 1)
-    return read_parts(lanes, jnp.where(lane // 8 == row % SLOTS, lane % 8, -1))
+    return read(lanes, jnp.where(lane // 8 == row % SLOTS, lane % 8, -1))
 
 
 def swap_halves(x):
@@ -421,7 +428,7 @@
     got = got_ref[...].astype(F32)
     near, far, _ = read_offsets(got)
     qk, vg = got[:, :SLOTS].reshape(SEQ * SLOTS, 128), got[:, SLOTS:].reshape(SEQ * SLOTS, 128)
-    lse, d = unpack_stats(got)
+    lse, d = unpack_stats(got, read=read_wide)
     q0, k0, v0, g0, _, _ = pair_halves(qk, vg)
     col, line, col_at, line_at = slot_positions(near, far)
     asks = (col % SLOTS < FAR_SLOT) | ((col % SLOTS == FAR_SLOT) & (far % NEAR_RATE == near))

time: 50.6 us -> 50.6 us (level)
  no operation moved by 1% of the time
where the time goes in v8:
time: 50.6 us; the launch traced here: 50 us
  starting transfers between devices  20.3 us (40%)
  Pallas kernels  17.2 us (34%)
  blocking collectives  10.2 us (20%)
  waiting for transfers between devices  1.67 us (3%)
  between operations  0.67 us (1%)
    all_to_all x2, starting transfers between devices, exchange(): lax.all_to_all(x, axis, split_axis=0, concat_axis=0, axis_index_groups=gr...  20.3 us
    all_to_all x1, blocking collectives, exchange(): lax.all_to_all(x, axis, split_axis=0, concat_axis=0, axis_index_groups=gr...  10.2 us
    pallas_call x2, Pallas kernels, local_call(): pl.pallas_call(functools.partial(local_kernel, base, count), in_specs=[hb...  9.09 us
    pallas_call x1, Pallas kernels, select_call(): pl.pallas_call(select_kernel, in_specs=[hbm] * 6, out_specs=vmem, out_sha...  3.01 us
    pallas_call x1, Pallas kernels, owner_call(): pl.pallas_call(owner_kernel, in_specs=[vmem, vmem, vmem], out_specs=vmem,...  2.25 us
    pallas_call x1, Pallas kernels, finish_call(): pl.pallas_call(finish_kernel, in_specs=[vmem] * 11, out_specs=[hbm] * 4,...  2.06 us
    all_to_all x2, waiting for transfers between devices, exchange(): lax.all_to_all(x, axis, split_axis=0, concat_axis=0, axis_index_groups=gr...  1.67 us
  transfers between devices with their start and end apart: 2, of which 2 were waited for; matrix products, arithmetic and copies ran while one was open for 0% of the time, Pallas kernels for 18%

profile of v8, /device:TPU:1, one launch (start us, length us, event | category | flops | bytes accessed | tf_op | source)
XLA Modules:
  0.0 50.0 jit_solution(9307082302151008411)
XLA Ops:
  0.6 3.0 %select_rows.1 = bf16[2,16,16,128]{3,2,1,0:T(8,128)(2,1)} custom-call(s32[16]{0:T(128)} %near_in.3, s32[16]{0:T(128)} %far_in.3, bf16[256,1024]{1,0:T(8,128)(2,1)} %q_ref.5, bf16[256,1024]{1,0:T(8,128)(2,1)} %k_ref.5, bf16[256,1024]{1,0:T(8,128)(2,1)} %v_ref.5, bf16[256,1024]{1,0:T(8,128)(2,1)} %g_ref.5), custom_call_target="tpu_custom_call" | custom-call | tf_op jit(solution)/shard_map/select_rows/pallas_call | solution.py:250
  3.6 12.6 %all-to-all-start = ((bf16[32,16,128]{2,1,0:T(8,128)(2,1)}), bf16[32,16,128]{2,1,0:T(8,128)(2,1)S(1)}, u32[]{:S(2)}, u32[]{:S(2)}) async-start(bf16[32,16,128]{2,1,0:T(8,128)(2,1)} %bitcast), calls=%async_computation | async-start | bytes 262144 | tf_op jit(solution)/shard_map/all_to_all | solution.py:620
  16.2 4.5 %local_level.2 = (bf16[2,256,512]{2,1,0:T(8,128)(2,1)S(1)}, bf16[2,256,512]{2,1,0:T(8,128)(2,1)S(1)}, f32[32,512]{1,0:T(8,128)S(1)}, bf16[160,512]{1,0:T(8,128)(2,1)S(1)}, bf16[256,256]{1,0:T(8,128)(2,1)S(1)}) custom-call(s32[16]{0:T(128)} %near_in.3, s32[16]{0:T(128)} %far_in.3, bf16[256,1024]{1,0:T(8,128)(2,1)} %q_ref.5, bf16[256,1024]{1,0:T(8,128)(2,1)} %k_ref.5, ...), custom_call_target="tpu_custom_call" | custom-call | flops 469762048 | bytes 1835008 | tf_op jit(solution)/shard_map/local_level/pallas_call | solution.py:377
  20.8 1.0 %all-to-all-done.got_ref = bf16[32,16,128]{2,1,0:T(8,128)(2,1)S(1)} async-done(((bf16[32,16,128]{2,1,0:T(8,128)(2,1)}), bf16[32,16,128]{2,1,0:T(8,128)(2,1)S(1)}, u32[]{:S(2)}, u32[]{:S(2)}) %all-to-all-start) | async-done | bytes 131104 | tf_op jit(solution)/shard_map/all_to_all | solution.py:620
  21.8 0.8 %near_forward.1 = (bf16[8,80,128]{2,1,0:T(8,128)(2,1)S(1)}, f32[256,128]{1,0:T(8,128)S(1)}) custom-call(bf16[32,16,128]{2,1,0:T(8,128)(2,1)S(1)} %all-to-all-done.got_ref), custom_call_target="tpu_custom_call" | custom-call | tf_op jit(solution)/shard_map/near_forward/pallas_call | solution.py:452
  22.5 10.2 %all_to_all.21.far_got_ref = bf16[8,80,128]{2,1,0:T(8,128)(2,1)S(1)} all-to-all(bf16[8,80,128]{2,1,0:T(8,128)(2,1)S(1)} %get-tuple-element.36), channel_id=1, replica_groups={{7,6,5,4,3,2,1,0},{15,14,13,12,11,10,9,8},{23,22,21,20,19,18,17,16},{31..., dimensions={0} | all-to-all | bytes 327680 | tf_op jit(solution)/shard_map/all_to_all | solution.py:620
  32.7 2.3 %owner_level.1 = bf16[256,128]{1,0:T(8,128)(2,1)} custom-call(bf16[32,16,128]{2,1,0:T(8,128)(2,1)S(1)} %all-to-all-done.got_ref, f32[256,128]{1,0:T(8,128)S(1)} %get-tuple-element.35.stat_ref, bf16[8,80,128]{2,1,0:T(8,128)(2,1)S(1)} %all_to_all.21.far_got_ref), custom_call_target="tpu_custom_call" | custom-call | tf_op jit(solution)/shard_map/owner_level/pallas_call | solution.py:534
  35.0 7.7 %all-to-all-start.2 = ((bf16[32,8,128]{2,1,0:T(8,128)(2,1)}), bf16[32,8,128]{2,1,0:T(8,128)(2,1)S(1)}, u32[]{:S(2)}, u32[]{:S(2)}) async-start(bf16[32,8,128]{2,1,0:T(8,128)(2,1)} %bitcast.1), calls=%async_computation.2 | async-start | bytes 131072 | tf_op jit(solution)/shard_map/all_to_all | solution.py:620
  42.7 4.5 %local_level.3 = (bf16[2,256,512]{2,1,0:T(8,128)(2,1)S(1)}, f32[2,256,512]{2,1,0:T(8,128)S(1)}, f32[32,512]{1,0:T(8,128)S(1)}, bf16[160,512]{1,0:T(8,128)(2,1)S(1)}, bf16[256,256]{1,0:T(8,128)(2,1)S(1)}) custom-call(s32[16]{0:T(128)} %near_in.3, s32[16]{0:T(128)} %far_in.3, bf16[256,1024]{1,0:T(8,128)(2,1)} %q_ref.5, bf16[256,1024]{1,0:T(8,128)(2,1)} %k_ref.5, ...), custom_call_target="tpu_custom_call" | custom-call | flops 469762048 | bytes 1835008 | tf_op jit(solution)/shard_map/local_level/pallas_call | solution.py:377
  47.3 0.7 %all-to-all-done.2 = bf16[32,8,128]{2,1,0:T(8,128)(2,1)S(1)} async-done(((bf16[32,8,128]{2,1,0:T(8,128)(2,1)}), bf16[32,8,128]{2,1,0:T(8,128)(2,1)S(1)}, u32[]{:S(2)}, u32[]{:S(2)}) %all-to-all-start.2) | async-done | bytes 65568 | tf_op jit(solution)/shard_map/all_to_all | solution.py:620
  48.0 2.1 %finish_rows.1 = (bf16[256,1024]{1,0:T(8,128)(2,1)}, bf16[256,1024]{1,0:T(8,128)(2,1)}, bf16[256,1024]{1,0:T(8,128)(2,1)}, bf16[256,1024]{1,0:T(8,128)(2,1)}) custom-call(bf16[256,128]{1,0:T(8,128)(2,1)S(1)} %bitcast.3, bf16[2,256,512]{2,1,0:T(8,128)(2,1)S(1)} %get-tuple-element.38.refs_0_, bf16[2,256,512]{2,1,0:T(8,128)(2,1)S(1)} %get-tuple-element.39.refs_1_, ...), custom_call_target="tpu_custom_call" | custom-call | tf_op jit(solution)/shard_map/finish_rows/pallas_call | solution.py:605
Async XLA Ops:
  3.6 18.1 %all-to-all-start = ((bf16[32,16,128]{2,1,0:T(8,128)(2,1)}), bf16[32,16,128]{2,1,0:T(8,128)(2,1)S(1)}, u32[]{:S(2)}, u32[]{:S(2)}) async-start(bf16[32,16,128]{2,1,0:T(8,128)(2,1)} %bitcast), calls=%async_computation | async-start | bytes 262144 | tf_op jit(solution)/shard_map/all_to_all | solution.py:620
  35.0 13.0 %all-to-all-start.2 = ((bf16[32,8,128]{2,1,0:T(8,128)(2,1)}), bf16[32,8,128]{2,1,0:T(8,128)(2,1)S(1)}, u32[]{:S(2)}, u32[]{:S(2)}) async-start(bf16[32,8,128]{2,1,0:T(8,128)(2,1)} %bitcast.1), calls=%async_computation.2 | async-start | bytes 131072 | tf_op jit(solution)/shard_map/all_to_all | solution.py:620
